TPU v7x, 512 devices: a whole 4x8x8 slice. The times are simulated.
512 devices in a mesh: dp: 16 (over z, core), sketch: 32 (over x, y).
Axes of the slice: x: 4, y: 8, z: 8, core: 2. Of those that a mesh axis runs over, the one named last changes fastest.
Arguments:
- samples: bfloat16 [16384, 512], P('dp'), may hold values from -6 to 6
- projections: bfloat16 [4, 512, 16384], P(None, 'dp', 'sketch'), may hold values from -0.25 to 0.25
- targets: bfloat16 [16384, 64], P('dp'), may hold values from -6 to 6
- feature_scale: float32 [16384], P('sketch'), may hold values from 0.1 to 1.5
- coarse_factor: bfloat16 [1024, 1024], replicated, may hold values from -1 to 3, as said below
Outputs:
- solution: float32 [16384, 64], P('sketch')
- residual: float32 [16384, 64], P('sketch')
Inputs may be any that keep to these rules, and one draw needn't show every extreme that they name: `coarse_factor`: lower triangular; its diagonal entries lie between 2 and 3.
All inputs are finite; a program needn't handle non-finite values.
Results may differ from a plain program's by a relative error of at most 0.0075.
The roundings to bfloat16 on the way count: a program that leaves them out, or rounds other values in their place, can miss the bound.
Values may be sent and summed in bfloat16 or wider, within the bound.
No kernel may reach another device: no remote copies, remote signals or barrier semaphores. Data moves between devices by JAX's collectives and lax.ppermute only.
A program may use at most 64 MiB of HBM per device.

v0:
```python
import math

import jax
import jax.numpy as jnp
from jax import lax
from jax.sharding import PartitionSpec as P

F = 16384
K = 1024
ITERS = 2


RIDGE = 0.5


def solve_coarse(lower, restricted):
    forward = lax.linalg.triangular_solve(lower, restricted, left_side=True, lower=True)
    return lax.linalg.triangular_solve(lower, forward, left_side=True, lower=True, transpose_a=True)


def body(samples, projections, targets, feature_scale, coarse_factor):
    count = projections.shape[2]
    width = targets.shape[1]
    contract = (((0,), (0,)), ((), ()))
    panels = jnp.einsum(
        "nd,jdf->jnf",
        samples,
        lax.all_gather(projections, "dp", axis=1, tiled=True),
        preferred_element_type=jnp.float32,
    )
    features = (panels[0] * panels[1] * panels[2] * panels[3] * (1.0 / math.sqrt(F))).astype(
        jnp.bfloat16
    )
    lower = coarse_factor.astype(jnp.float32)
    factor = 1.0 / math.sqrt(F // K)
    offset = lax.axis_index("sketch") * count % K

    def restrict(resid):
        return lax.dynamic_update_slice_in_dim(
            jnp.zeros((K, width), jnp.float32), resid * factor, offset, 0
        )

    def prolong(solved):
        return lax.dynamic_slice_in_dim(solved, offset, count, 0) * factor

    def back_project(values):
        return lax.psum(
            lax.dot_general(features, values, contract, preferred_element_type=jnp.float32), "dp"
        )

    def total(value):
        return lax.psum(value, "sketch")

    def precondition(resid):
        local = restrict(resid)
        restricted = lax.psum(local, "sketch")
        solved = solve_coarse(lower, restricted)
        fine = feature_scale[:, None] * resid + prolong(solved)
        product = total(jnp.sum(resid * fine, 0))
        return (fine, product)

    rhs = back_project(targets)
    solution = jnp.zeros_like(rhs)
    resid = rhs
    fine, product = precondition(resid)
    direction = fine
    for step in range(ITERS):
        whole = direction.astype(jnp.bfloat16)
        partial_sums = jnp.dot(features, whole, preferred_element_type=jnp.float32)
        sums = lax.psum(partial_sums, "sketch").astype(jnp.bfloat16)
        image = back_project(sums) + RIDGE * direction
        alpha = product / total(jnp.sum(direction * image, 0))
        solution = solution + alpha * direction
        resid = resid - alpha * image
        if step + 1 < ITERS:
            fine, fresh = precondition(resid)
            direction = fine + fresh / product * direction
            product = fresh
    return (solution, resid)


def solution(mesh):
    placed = (P("dp", None), P(None, "dp", "sketch"), P("dp", None), P("sketch"), P())
    return jax.shard_map(
        body,
        mesh=mesh,
        in_specs=placed,
        out_specs=(P("sketch", None), P("sketch", None)),
        check_vma=False,
    )
```

profile of v0, /device:TPU:1, one launch (start us, length us, event | category | flops | bytes accessed | tf_op | source)
XLA Modules:
  0.0 1260.4 jit_solution(6117825082097410547)
XLA Ops:
  8.0 4.0 convert_select_fusion
  12.0 47.3 %all-gather.2.cloned.1.call-done = bf16[4,512,512]{2,1,0:T(8,128)(2,1)} async-done(((bf16[4,32,512]{2,1,0:T(8,128)(2,1)}), bf16[4,512,512]{2,1,0:T(8,128)(2,1)}) %all-gather.2.cloned.1.call-update) | async-done | bytes 2097168 | tf_op jit(solution)/shard_map/all_gather | solution.py:28
  59.3 4.0 convolution_bitcast_fusion
  65.6 111.5 %all-reduce.9.cloned.1.call-done = f32[512,64]{0,1:T(8,128)} async-done(((f32[512,64]{0,1:T(8,128)}), f32[512,64]{0,1:T(8,128)}) %all-reduce.9.cloned.1.call-update) | async-done | bytes 131088 | tf_op jit(solution)/shard_map/psum | solution.py:47
  179.0 23.4 %while.8 = (s32[]{:T(128)}, f32[1024,1024]{1,0:T(8,128)}, s32[8,2]{0,1:T(2,128)S(1)}, f32[8,128,128]{2,1,0:T(8,128)S(1)}, s32[]{:T(128)}) while((s32[]{:T(128)}, f32[1024,1024]{1,0:T(8,128)}, s32[8,2]{0,1:T(2,128)S(1)}, f32[8,128,128]{2,1,0:T(8,128)S(1)}, s32[]{:T(128)}) %tuple.81), condition=%wide.while_cond.1, body=%wide.while_body.1.sunk | while | flops 2 | bytes 131181 | solution.py:18
  179.6 2.3 bitcast_dynamic-update-slice_fusion.2
  182.6 2.3 bitcast_dynamic-update-slice_fusion.2
  185.5 2.3 bitcast_dynamic-update-slice_fusion.2
  188.4 2.3 bitcast_dynamic-update-slice_fusion.2
  191.4 2.3 bitcast_dynamic-update-slice_fusion.2
  194.3 2.3 bitcast_dynamic-update-slice_fusion.2
  197.2 2.3 bitcast_dynamic-update-slice_fusion.2
  200.2 2.2 bitcast_dynamic-update-slice_fusion.2
  202.4 78.6 %custom-call.9 = f32[8,128,128]{1,2,0:T(8,128)S(1)} custom-call(f32[8,128,128]{2,1,0:T(8,128)S(1)} %get-tuple-element.33), custom_call_target="InvertDiagBlocksLowerTriangular" | custom-call | tf_op jit(solution)/shard_map/triangular_solve/custom-call.0 | solution.py:18
  281.0 51.3 %all-reduce.11.cloned.1.call-done = f32[1024,64]{0,1:T(8,128)} async-done(((f32[1024,64]{0,1:T(8,128)}), f32[1024,64]{0,1:T(8,128)}) %all-reduce.11.cloned.1.call-update) | async-done | bytes 262160 | tf_op jit(solution)/shard_map/psum | solution.py:56
  355.8 117.8 %all-reduce.18 = bf16[1024,64]{1,0:T(8,128)(2,1)} all-reduce(f32[1024,64]{1,0:T(8,128)S(1)} %fusion.94), channel_id=1, replica_groups=mesh['dp'=16,'sketch'=32] {'sketch'}, use_global_device_ids=true, to_apply=%region_4.0 | all-reduce | flops 65536 | bytes 393216 | tf_op jit(solution)/shard_map/psum | solution.py:70
  473.6 2.1 fusion.147
  475.7 140.8 %all-reduce.13.cloned.1.call-done = f32[512,64]{0,1:T(8,128)} async-done(((f32[512,64]{0,1:T(8,128)}), f32[512,64]{0,1:T(8,128)}) %all-reduce.13.cloned.1.call-update) | async-done | bytes 131088 | tf_op jit(solution)/shard_map/psum | solution.py:47
  617.5 60.7 %all-reduce = (f32[64]{0:T(128)S(1)}, f32[64]{0:T(128)S(1)}) all-reduce(f32[64]{0:T(128)S(1)} %get-tuple-element.37, f32[64]{0:T(128)S(1)} %get-tuple-element.36), channel_id=1, replica_groups=mesh['dp'=16,'sketch'=32] {'sketch'}, use_global_device_ids=true, to_apply=%region_3.0 | all-reduce | flops 128 | bytes 1024 | tf_op jit(solution)/shard_map/psum | solution.py:52
  680.3 156.8 %all-reduce.15.cloned.1.call-done = f32[1024,64]{0,1:T(8,128)} async-done(((f32[1024,64]{0,1:T(8,128)}), f32[1024,64]{0,1:T(8,128)}) %all-reduce.15.cloned.1.call-update) | async-done | bytes 262160 | tf_op jit(solution)/shard_map/psum | solution.py:56
  860.2 58.4 %psum.84 = f32[64]{0:T(128)S(1)} all-reduce(f32[64]{0:T(128)S(1)} %multiply_reduce_fusion.1), channel_id=1, replica_groups=mesh['dp'=16,'sketch'=32] {'sketch'}, use_global_device_ids=true, to_apply=%region_10.0 | all-reduce | flops 64 | bytes 512 | tf_op jit(solution)/shard_map/psum | solution.py:52
  919.1 114.5 %all-reduce.19 = bf16[1024,64]{1,0:T(8,128)(2,1)S(1)} all-reduce(f32[1024,64]{1,0:T(8,128)S(1)} %fusion.92), channel_id=1, replica_groups=mesh['dp'=16,'sketch'=32] {'sketch'}, use_global_device_ids=true, to_apply=%region_11.0 | all-reduce | flops 65536 | bytes 393216 | tf_op jit(solution)/shard_map/psum | solution.py:70
  1034.7 155.4 %all-reduce.17.cloned.1.call-done = f32[512,64]{0,1:T(8,128)} async-done(((f32[512,64]{0,1:T(8,128)}), f32[512,64]{0,1:T(8,128)}) %all-reduce.17.cloned.1.call-update) | async-done | bytes 131088 | tf_op jit(solution)/shard_map/psum | solution.py:47
  1191.1 60.7 %psum.87 = f32[64]{0:T(128)S(1)} all-reduce(f32[64]{0:T(128)S(1)} %multiply_reduce_fusion), channel_id=1, replica_groups=mesh['dp'=16,'sketch'=32] {'sketch'}, use_global_device_ids=true, to_apply=%region_14.0 | all-reduce | flops 64 | bytes 512 | tf_op jit(solution)/shard_map/psum | solution.py:52
  (165 shorter events, 63.3 us)
Async XLA Ops:
  7.2 52.1 %copy-start = (bf16[1024,512]{1,0:T(8,128)(2,1)S(1)}, bf16[1024,512]{1,0:T(8,128)(2,1)}, u32[]{:S(2)}) copy-start(bf16[1024,512]{1,0:T(8,128)(2,1)} %param.9) | copy-start | bytes 3145732
  7.2 52.1 %all-gather.2.cloned.1.call-start = ((), (), s32[]{:S(2)}) async-start(), calls=%async_computation | async-start | bytes 2228224 | tf_op jit(solution)/shard_map/all_gather | solution.py:28
  7.9 169.1 %all-reduce.9.cloned.1.call-start = ((), (), s32[]{:S(2)}) async-start(), calls=%async_computation.1 | async-start | bytes 262144 | tf_op jit(solution)/shard_map/psum | solution.py:47
  63.3 1.0 copy-start.4
  65.5 266.8 %all-reduce.11.cloned.1.call-start = ((), (), s32[]{:S(2)}) async-start(), calls=%async_computation.2 | async-start | bytes 524288 | tf_op jit(solution)/shard_map/psum | solution.py:56
  178.0 0.7 copy-start.3
  178.7 437.8 %all-reduce.13.cloned.1.call-start = ((), (), s32[]{:S(2)}) async-start(), calls=%async_computation.3 | async-start | bytes 262144 | tf_op jit(solution)/shard_map/psum | solution.py:47
  339.0 16.3 %copy-start.1 = (f32[512,64]{0,1:T(8,128)S(1)}, f32[512,64]{0,1:T(8,128)}, u32[]{:S(2)}) copy-start(f32[512,64]{0,1:T(8,128)} %all-reduce.9.cloned.1.call-done) | copy-start | bytes 393220
  339.0 16.3 %copy-start.5 = (f32[512]{0:T(512)S(1)}, f32[512]{0:T(512)}, u32[]{:S(2)}) copy-start(f32[512]{0:T(512)} %param.12) | copy-start | bytes 6148
  475.7 361.4 %all-reduce.15.cloned.1.call-start = ((), (), s32[]{:S(2)}) async-start(), calls=%async_computation.4 | async-start | bytes 524288 | tf_op jit(solution)/shard_map/psum | solution.py:56
  679.3 0.7 copy-start.2
  680.1 510.0 %all-reduce.17.cloned.1.call-start = ((), (), s32[]{:S(2)}) async-start(), calls=%async_computation.5 | async-start | bytes 262144 | tf_op jit(solution)/shard_map/psum | solution.py:47
Sparse Core Ops, SparseCore 0:
  10.2 49.1 all-gather.1
  65.6 111.3 all-reduce.8
  180.9 151.3 all-reduce.10
  475.8 140.6 all-reduce.12
  680.2 156.8 all-reduce.14
  1034.8 155.2 all-reduce.16
where the time goes:
time: 1270 us; the launch traced here: 1260 us
  waiting for transfers between devices  664 us (52%)
  blocking collectives  412 us (32%)
  other arithmetic  89.6 us (7%)
  matrix products  54.2 us (4%)
  local copies, waits for them, and re-layouts  25 us (2%)
  between operations  15 us (1%)
    psum x3, waiting for transfers between devices, back_project(): lax.psum(lax.dot_general(features, values, contract, preferred_element_ty...  408 us
    psum x2, blocking collectives, body(): sums = lax.psum(partial_sums, 'sketch').astype(jnp.bfloat16)  232 us
    psum x2, waiting for transfers between devices, precondition(): restricted = lax.psum(local, 'sketch')  208 us
    psum x3, blocking collectives, total(): return lax.psum(value, 'sketch')  180 us
    another operation x4, other arithmetic, solve_coarse(): lax.linalg.triangular_solve(lower, forward, left_side=True, lower=True, t...  82.6 us
    all_gather x1, waiting for transfers between devices, body(): lax.all_gather(projections, 'dp', axis=1, tiled=True)  47.3 us
  transfers between devices with their start and end apart: 6, of which 6 were waited for; matrix products, arithmetic and copies ran while one was open for 8% of the time, Pallas kernels for 0%

commit v1 on v0

v1 whole, which is shorter than its diff:
```python
import functools
import math

import jax
import jax.numpy as jnp
from jax import lax
from jax.experimental import pallas as pl
from jax.experimental.pallas import tpu as pltpu
from jax.sharding import PartitionSpec as P

F = 16384
K = 1024
ITERS = 2
RIDGE = 0.5

f32 = jnp.float32
bf16 = jnp.bfloat16


def split(value):
    high = value.astype(bf16)
    return high, (value - high.astype(f32)).astype(bf16)


def dot(a, b):
    return lax.dot_general(a, b, (((1,), (0,)), ((), ())), preferred_element_type=f32)


def dot3(a, b):
    ah, al = split(a)
    bh, bl = split(b)
    return dot(ah, bh) + (dot(ah, bl) + dot(al, bh))


def dot2_left(a, exact):
    ah, al = split(a)
    return dot(ah, exact) + dot(al, exact)


def dot2_right(exact, b):
    bh, bl = split(b)
    return dot(exact, bh) + dot(exact, bl)


BLOCK = 256


def inverse_kernel(lower_ref, high_ref, low_ref, inv):
    n = lower_ref.shape[0]
    blocks = n // BLOCK
    rows = lax.broadcasted_iota(jnp.int32, (BLOCK, BLOCK), 0)
    cols = lax.broadcasted_iota(jnp.int32, (BLOCK, BLOCK), 1)
    spans = [pl.ds(b * BLOCK, BLOCK) for b in range(blocks)]
    inv[...] = jnp.zeros_like(inv)
    for span in spans:
        block = lower_ref[span, span].astype(f32)
        diag = jnp.sum(jnp.where(rows == cols, block, 0.0), axis=1, keepdims=True)
        inv[span, span] = jnp.where(rows == cols, 1.0 / diag, 0.0)

    def level(k, carry):
        below = ((rows >> k) == (cols >> k) + 1) & ((rows >> (k + 1)) == (cols >> (k + 1)))
        for span in spans:
            x = inv[span, span]
            off = jnp.where(below, lower_ref[span, span].astype(f32), 0.0).astype(bf16)
            inv[span, span] = x - dot3(dot2_left(x, off), x)
        return carry

    lax.fori_loop(0, int(math.log2(BLOCK)), level, 0)
    size = BLOCK
    while size < n:
        for at in range(0, n, 2 * size):
            top, bottom = pl.ds(at, size), pl.ds(at + size, size)
            a, b = inv[top, top], inv[bottom, bottom]
            inv[bottom, top] = -dot3(b, dot2_right(lower_ref[bottom, top], a))
        size *= 2
    xh, xl = split(inv[...])
    xht, xlt = split(inv[...].T)
    for span in spans:
        m = dot(xht, xh[:, span.start : span.start + BLOCK]) + (
            dot(xht, xl[:, span.start : span.start + BLOCK])
            + dot(xlt, xh[:, span.start : span.start + BLOCK])
        )
        high_ref[:, span], low_ref[:, span] = split(m)


def coarse_inverse(lower):
    n = lower.shape[0]
    return pl.pallas_call(
        inverse_kernel,
        out_shape=[jax.ShapeDtypeStruct((n, n), bf16)] * 2,
        in_specs=[pl.BlockSpec(memory_space=pltpu.VMEM)],
        out_specs=[pl.BlockSpec(memory_space=pltpu.VMEM)] * 2,
        scratch_shapes=[pltpu.VMEM((n, n), f32)],
        compiler_params=pltpu.CompilerParams(vmem_limit_bytes=48 * 1024 * 1024),
        cost_estimate=pl.CostEstimate(flops=20 * 10**9, bytes_accessed=6 * 2**20, transcendentals=0),
    )(lower)


ROWS = 256


def feature_kernel(samples_ref, proj_ref, targets_ref, feat_ref, part_ref):
    n, parts = samples_ref.shape[0], part_ref.shape[0]
    total = None
    for at in range(0, n, ROWS):
        block = samples_ref[at : at + ROWS, :]
        acc = dot(block, proj_ref[0])
        for j in range(1, proj_ref.shape[0]):
            acc = acc * dot(block, proj_ref[j])
        feat = (acc * (1.0 / math.sqrt(F))).astype(bf16)
        feat_ref[at : at + ROWS, :] = feat
        term = dot(targets_ref[:, at : at + ROWS], feat)
        total = term if total is None else total + term
    step = total.shape[0] // parts
    for p in range(parts):
        part_ref[p] = total[p * step : (p + 1) * step, :]


def make_features(samples, proj, targets_t, parts):
    n, width = samples.shape[0], proj.shape[2]
    vmem = pl.BlockSpec(memory_space=pltpu.VMEM)
    return pl.pallas_call(
        feature_kernel,
        out_shape=[
            jax.ShapeDtypeStruct((n, width), bf16),
            jax.ShapeDtypeStruct((parts, targets_t.shape[0] // parts, width), f32),
        ],
        in_specs=[vmem] * 3,
        out_specs=[vmem] * 2,
        compiler_params=pltpu.CompilerParams(vmem_limit_bytes=48 * 1024 * 1024),
        cost_estimate=pl.CostEstimate(flops=2 * 10**9, bytes_accessed=5 * 2**20, transcendentals=0),
    )(samples, proj, targets_t)


def triple(value):
    high = value.astype(bf16)
    rest = value - high.astype(f32)
    mid = rest.astype(bf16)
    return jnp.stack([high, mid, (rest - mid.astype(f32)).astype(bf16)], -1)


def body(samples, projections, targets, feature_scale, coarse_factor):
    n_dp, n_sk = lax.axis_size("dp"), lax.axis_size("sketch")
    count = projections.shape[2]
    width = targets.shape[1]
    mine = width // n_dp
    cols = width // n_sk
    groups = F // K
    factor = 1.0 / math.sqrt(groups)
    halves = K // count
    parity = lax.axis_index("sketch") % halves
    n = samples.shape[0]
    scale = feature_scale[None, :]

    proj = lax.all_gather(projections, "dp", axis=1, tiled=True)
    inv_high, inv_low = coarse_inverse(coarse_factor)
    feat, part = make_features(samples, proj, targets.T, n_dp)

    def scatter_dp(value):
        got = lax.all_to_all(value, "dp", 0, 0)
        return jnp.sum(got, 0)

    def gather_dp(value):
        return lax.all_to_all(jnp.broadcast_to(value[None], (n_dp,) + value.shape), "dp", 0, 0)

    def gather_sk(value):
        return lax.all_to_all(jnp.broadcast_to(value[None], (n_sk,) + value.shape), "sketch", 0, 0)

    def everywhere(value, dots):
        k = dots.shape[1]
        extra = jnp.pad(triple(dots).reshape(mine, 3 * k), ((0, 0), (0, 128 - 3 * k)))
        got = gather_sk(jnp.concatenate([value.astype(bf16), extra], 1)).astype(f32)
        sums = jnp.sum(jnp.sum(got[:, :, count : count + 3 * k], 0).reshape(mine, k, 3), -1)
        rho = jnp.sum(got[:, :, :count].reshape(n_sk // halves, halves, mine, count), 0) * factor
        return jnp.concatenate([rho[h] for h in range(halves)], 1), sums

    def coarse(rho):
        high, low = split(rho)
        both = dot(jnp.concatenate([high, low], 0), inv_high)
        return both[:mine] + (both[mine:] + dot(high, inv_low))

    def own(solved):
        return lax.dynamic_slice_in_dim(solved, parity * count, count, 1) * factor

    def forward(direction):
        got = gather_dp(direction.astype(bf16)).reshape(width, count)
        sums = lax.dot_general(got, feat, (((1,), (1,)), ((), ())), preferred_element_type=f32)
        return sums.reshape(n_sk, cols, n)

    def backward(sums):
        u = jnp.sum(lax.all_to_all(sums, "sketch", 0, 0), 0).astype(bf16)
        whole = gather_sk(u).reshape(width, n)
        return dot(whole, feat).reshape(n_dp, mine, count)

    def row_sum(value):
        return jnp.sum(value, 1, keepdims=True)

    resid = scatter_dp(part)
    rho, dots = everywhere(resid, row_sum(scale * resid * resid))
    energy = dots
    solved = coarse(rho)
    product = energy + row_sum(rho * solved)
    direction = scale * resid + own(solved)
    answer = jnp.zeros_like(resid)
    for step in range(ITERS):
        image = scatter_dp(backward(forward(direction))) + RIDGE * direction
        if step + 1 < ITERS:
            weighted = scale * image
            rho_image, dots = everywhere(
                image,
                jnp.concatenate(
                    [row_sum(direction * image), row_sum(weighted * resid), row_sum(weighted * image)], 1
                ),
            )
            alpha = product / dots[:, 0:1]
        else:
            extra = jnp.pad(row_sum(direction * image), ((0, 0), (0, 127)))
            alpha = product / jnp.sum(gather_sk(extra), 0)[:, 0:1]
        answer = answer + alpha * direction
        resid = resid - alpha * image
        if step + 1 < ITERS:
            rho = rho - alpha * rho_image
            energy = energy - alpha * (2.0 * dots[:, 1:2] - alpha * dots[:, 2:3])
            solved = coarse(rho)
            fresh = energy + row_sum(rho * solved)
            direction = scale * resid + own(solved) + fresh / product * direction
            product = fresh
    got = gather_dp(jnp.stack([answer, resid]))
    out = jnp.swapaxes(got, 0, 1).reshape(2, width, count)
    return out[0].T, out[1].T


def solution(mesh):
    placed = (P("dp", None), P(None, "dp", "sketch"), P("dp", None), P("sketch"), P())
    return jax.shard_map(
        body,
        mesh=mesh,
        in_specs=placed,
        out_specs=(P("sketch", None), P("sketch", None)),
        check_vma=False,
    )
```

time: 1270 us -> 293 us (0.23)
  waiting for transfers between devices: 664 us -> 61.9 us
  blocking collectives: 412 us -> 155 us
  other arithmetic: 89.6 us -> 4.83 us
  matrix products: 54.2 us -> 6.37 us
  Pallas kernels: 0 us -> 24 us
  starting transfers between devices: 0.64 us -> 13.6 us
  local copies, waits for them, and re-layouts: 25 us -> 12.1 us
    psum x5 -> x0, waiting for transfers between devices: 616 us -> none  [the longest x3 408 us: back_project(): lax.psum(lax.dot_general(features, values, contract, preferred_element_ty...]
    psum x5 -> x0, blocking collectives: 412 us -> none  [the longest x2 232 us: body(): sums = lax.psum(partial_sums, 'sketch').astype(jnp.bfloat16)]
    all_to_all x0 -> x11, blocking collectives: none -> 155 us  [the longest x3 43.3 us: gather_sk(): lax.all_to_all(jnp.broadcast_to(value[None], (n_sk,) + value.shape), 'ske...]
    another operation x4, other arithmetic: 82.6 us -> 0.11 us  [the longest x2 0.09 us: body(): got = gather_dp(jnp.stack([answer, resid]))]
    another operation x60 -> x0, matrix products: 45 us -> none  [the longest x30 23.7 us: solve_coarse(): lax.linalg.triangular_solve(lower, restricted, left_side=True, lower=True)]
    pallas_call x0 -> x2, Pallas kernels: none -> 24 us  [the longest x1 21.1 us: coarse_inverse(): pl.pallas_call(inverse_kernel, out_shape=[jax.ShapeDtypeStruct((n, n), bf...]
    another operation x35 -> x1, local copies, waits for them, and re-layouts: 23.4 us -> 0.11 us  [triple(): return jnp.stack([high, mid, (rest - mid.astype(f32)).astype(bf16)], -1)]
    all_to_all x0 -> x2, starting transfers between devices: none -> 13.5 us  [gather_sk(): lax.all_to_all(jnp.broadcast_to(value[None], (n_sk,) + value.shape), 'ske...]
  transfers between devices with their start and end apart: 6 -> 3, of which waited for: 6 -> 2; matrix products, arithmetic and copies ran while one was open for 8% -> 0% of each run, Pallas kernels for 0% -> 7%
where the time goes in v1:
time: 293 us; the launch traced here: 292 us
  blocking collectives  155 us (53%)
  waiting for transfers between devices  61.9 us (21%)
  Pallas kernels  24 us (8%)
  between operations  14.3 us (5%)
  starting transfers between devices  13.6 us (5%)
  local copies, waits for them, and re-layouts  12.1 us (4%)
  matrix products  6.37 us (2%)
  other arithmetic  4.83 us (2%)
    all_gather x1, waiting for transfers between devices, body(): proj = lax.all_gather(projections, 'dp', axis=1, tiled=True)  51.4 us
    all_to_all x3, blocking collectives, gather_sk(): lax.all_to_all(jnp.broadcast_to(value[None], (n_sk,) + value.shape), 'ske...  43.3 us
    all_to_all x3, blocking collectives, scatter_dp(): got = lax.all_to_all(value, 'dp', 0, 0)  41.2 us
    all_to_all x3, blocking collectives, gather_dp(): lax.all_to_all(jnp.broadcast_to(value[None], (n_dp,) + value.shape), 'dp'...  37.5 us
    all_to_all x2, blocking collectives, backward(): u = jnp.sum(lax.all_to_all(sums, 'sketch', 0, 0), 0).astype(bf16)  33.3 us
    pallas_call x1, Pallas kernels, coarse_inverse(): pl.pallas_call(inverse_kernel, out_shape=[jax.ShapeDtypeStruct((n, n), bf...  21.1 us
    all_to_all x2, starting transfers between devices, gather_sk(): lax.all_to_all(jnp.broadcast_to(value[None], (n_sk,) + value.shape), 'ske...  13.5 us
    all_to_all x2, waiting for transfers between devices, gather_sk(): lax.all_to_all(jnp.broadcast_to(value[None], (n_sk,) + value.shape), 'ske...  9.85 us
  transfers between devices with their start and end apart: 3, of which 2 were waited for; matrix products, arithmetic and copies ran while one was open for 0% of the time, Pallas kernels for 7%

profile of v1, /device:TPU:1, one launch (start us, length us, event | category | flops | bytes accessed | tf_op | source)
XLA Modules:
  0.0 292.2 jit_solution(15932790650944086763)
XLA Ops:
  7.9 51.4 %all-gather.2.cloned.1.call-done.proj_ref = bf16[4,512,512]{2,1,0:T(8,128)(2,1)} async-done(((bf16[4,32,512]{2,1,0:T(8,128)(2,1)}), bf16[4,512,512]{2,1,0:T(8,128)(2,1)}) %all-gather.2.cloned.1.call-update) | async-done | bytes 2097168 | tf_op jit(solution)/shard_map/all_gather | solution.py:155
  59.3 1.6 copy-done.1
  60.9 1.2 copy-done.2
  63.0 2.9 shard_map.68
  65.9 13.4 %all_to_all.65 = f32[16,4,512]{2,1,0:T(4,128)S(1)} all-to-all(f32[16,4,512]{2,1,0:T(4,128)S(1)} %get-tuple-element.6), channel_id=1, replica_groups=mesh['dp'=16,'sketch'=32] {'dp'}, dimensions={0} | all-to-all | bytes 262144 | tf_op jit(solution)/shard_map/all_to_all | solution.py:160
  80.3 9.4 %all-to-all-start.1 = ((bf16[32,4,640]{2,1,0:T(4,128)(2,1)}), bf16[32,4,640]{2,1,0:T(4,128)(2,1)S(1)}, u32[]{:S(2)}, u32[]{:S(2)}) async-start(bf16[32,4,640]{2,1,0:T(4,128)(2,1)} %broadcast_in_dim.20), calls=%async_computation.1 | async-start | bytes 327680 | tf_op jit(solution)/shard_map/all_to_all | solution.py:167
  89.8 21.1 %shard_map.69 = (bf16[1024,1024]{1,0:T(8,128)(2,1)S(1)}, bf16[1024,1024]{1,0:T(8,128)(2,1)S(1)}) custom-call(bf16[1024,1024]{1,0:T(8,128)(2,1)} %lower_ref.1), custom_call_target="tpu_custom_call" | custom-call | flops 20000000000 | bytes 6291456 | tf_op jit(solution)/shard_map/pallas_call | solution.py:88
  110.9 1.3 copy-done
  112.9 1.0 reduce_sum.177
  114.0 2.0 fusion.14
  116.5 10.5 %all_to_all.66 = bf16[16,4,512]{2,1,0:T(4,128)(2,1)S(1)} all-to-all(bf16[16,4,512]{2,1,0:T(4,128)(2,1)S(1)} %broadcast_in_dim.21), channel_id=1, replica_groups=mesh['dp'=16,'sketch'=32] {'dp'}, dimensions={0} | all-to-all | bytes 131072 | tf_op jit(solution)/shard_map/all_to_all | solution.py:164
  127.7 19.3 %all_to_all.67 = f32[32,2,1024]{2,1,0:T(2,128)} all-to-all(f32[32,2,1024]{2,1,0:T(2,128)S(1)} %copy.91), channel_id=1, replica_groups=mesh['dp'=16,'sketch'=32] {'sketch'}, dimensions={0} | all-to-all | bytes 524288 | tf_op jit(solution)/shard_map/all_to_all | solution.py:191
  147.1 1.0 reduce_sum.180
  148.2 15.6 %all_to_all.68 = bf16[32,2,1024]{2,1,0:T(2,128)(2,1)} all-to-all(bf16[32,2,1024]{2,1,0:T(2,128)(2,1)S(1)} %broadcast_in_dim.22), channel_id=1, replica_groups=mesh['dp'=16,'sketch'=32] {'sketch'}, dimensions={0} | all-to-all | bytes 262144 | tf_op jit(solution)/shard_map/all_to_all | solution.py:167
  165.1 13.9 %all_to_all.69 = f32[16,4,512]{2,1,0:T(4,128)S(1)} all-to-all(f32[16,4,512]{2,1,0:T(4,128)S(1)} %copy.93), channel_id=1, replica_groups=mesh['dp'=16,'sketch'=32] {'dp'}, dimensions={0} | all-to-all | bytes 262144 | tf_op jit(solution)/shard_map/all_to_all | solution.py:160
  180.1 4.1 %all-to-all-start.6 = ((bf16[32,4,640]{2,1,0:T(4,128)(2,1)}), bf16[32,4,640]{2,1,0:T(4,128)(2,1)S(1)}, u32[]{:S(2)}, u32[]{:S(2)}) async-start(bf16[32,4,640]{2,1,0:T(4,128)(2,1)} %broadcast_in_dim.23), calls=%async_computation.6 | async-start | bytes 327680 | tf_op jit(solution)/shard_map/all_to_all | solution.py:167
  184.6 9.8 %all-to-all-done.6 = bf16[32,4,640]{2,1,0:T(4,128)(2,1)S(1)} async-done(((bf16[32,4,640]{2,1,0:T(4,128)(2,1)}), bf16[32,4,640]{2,1,0:T(4,128)(2,1)S(1)}, u32[]{:S(2)}, u32[]{:S(2)}) %all-to-all-start.6) | async-done | bytes 163872 | tf_op jit(solution)/shard_map/all_to_all | solution.py:167
  196.7 2.0 fusion.19
  199.5 11.4 %all_to_all.70 = bf16[16,4,512]{2,1,0:T(4,128)(2,1)S(1)} all-to-all(bf16[16,4,512]{2,1,0:T(4,128)(2,1)S(1)} %broadcast_in_dim.25), channel_id=1, replica_groups=mesh['dp'=16,'sketch'=32] {'dp'}, dimensions={0} | all-to-all | bytes 131072 | tf_op jit(solution)/shard_map/all_to_all | solution.py:164
  211.6 14.0 %all_to_all.71 = f32[32,2,1024]{2,1,0:T(2,128)S(1)} all-to-all(f32[32,2,1024]{2,1,0:T(2,128)S(1)} %copy.101), channel_id=1, replica_groups=mesh['dp'=16,'sketch'=32] {'sketch'}, dimensions={0} | all-to-all | bytes 524288 | tf_op jit(solution)/shard_map/all_to_all | solution.py:191
  225.8 15.5 %all_to_all.72 = bf16[32,2,1024]{2,1,0:T(2,128)(2,1)S(1)} all-to-all(bf16[32,2,1024]{2,1,0:T(2,128)(2,1)S(1)} %broadcast_in_dim.26), channel_id=1, replica_groups=mesh['dp'=16,'sketch'=32] {'sketch'}, dimensions={0} | all-to-all | bytes 262144 | tf_op jit(solution)/shard_map/all_to_all | solution.py:167
  241.7 13.9 %all_to_all.73 = f32[16,4,512]{2,1,0:T(4,128)S(1)} all-to-all(f32[16,4,512]{2,1,0:T(4,128)S(1)} %copy.103), channel_id=1, replica_groups=mesh['dp'=16,'sketch'=32] {'dp'}, dimensions={0} | all-to-all | bytes 262144 | tf_op jit(solution)/shard_map/all_to_all | solution.py:160
  255.9 12.2 %all_to_all.74 = f32[32,4,128]{2,1,0:T(4,128)S(1)} all-to-all(f32[32,4,128]{2,1,0:T(4,128)S(1)} %broadcast_in_dim.28), channel_id=1, replica_groups=mesh['dp'=16,'sketch'=32] {'sketch'}, dimensions={0} | all-to-all | bytes 131072 | tf_op jit(solution)/shard_map/all_to_all | solution.py:167
  268.3 15.6 %all_to_all.75 = f32[16,2,4,512]{3,2,1,0:T(4,128)S(1)} all-to-all(f32[16,2,4,512]{3,2,1,0:T(4,128)S(1)} %broadcast_in_dim.29), channel_id=1, replica_groups=mesh['dp'=16,'sketch'=32] {'dp'}, dimensions={0} | all-to-all | bytes 524288 | tf_op jit(solution)/shard_map/all_to_all | solution.py:164
  (83 shorter events, 13.8 us)
Async XLA Ops:
  7.2 52.1 %all-gather.2.cloned.1.call-start = ((), (), s32[]{:S(2)}) async-start(), calls=%async_computation.13 | async-start | bytes 2228224 | tf_op jit(solution)/shard_map/all_gather | solution.py:155
  59.3 1.6 copy-start.1
  60.9 1.2 copy-start.2
  62.1 0.9 copy-start.3
  63.0 16.3 %copy-start.4 = (f32[512]{0:T(512)S(1)}, f32[512]{0:T(512)}, u32[]{:S(2)}) copy-start(f32[512]{0:T(512)} %param.8) | copy-start | bytes 6148
  80.3 31.9 %all-to-all-start.1 = ((bf16[32,4,640]{2,1,0:T(4,128)(2,1)}), bf16[32,4,640]{2,1,0:T(4,128)(2,1)S(1)}, u32[]{:S(2)}, u32[]{:S(2)}) async-start(bf16[32,4,640]{2,1,0:T(4,128)(2,1)} %broadcast_in_dim.20), calls=%async_computation.1 | async-start | bytes 327680 | tf_op jit(solution)/shard_map/all_to_all | solution.py:167
  110.8 1.4 copy-start
  180.1 14.3 %all-to-all-start.6 = ((bf16[32,4,640]{2,1,0:T(4,128)(2,1)}), bf16[32,4,640]{2,1,0:T(4,128)(2,1)S(1)}, u32[]{:S(2)}, u32[]{:S(2)}) async-start(bf16[32,4,640]{2,1,0:T(4,128)(2,1)} %broadcast_in_dim.23), calls=%async_computation.6 | async-start | bytes 327680 | tf_op jit(solution)/shard_map/all_to_all | solution.py:167
Sparse Core Ops, SparseCore 0:
  10.1 49.1 all-gather.1

commit v2 on v1

v2 whole, which is shorter than its diff:
```python
import functools
import math

import jax
import jax.numpy as jnp
from jax import lax
from jax.experimental import pallas as pl
from jax.experimental.pallas import tpu as pltpu
from jax.sharding import PartitionSpec as P

F = 16384
K = 1024
ITERS = 2
RIDGE = 0.5

f32 = jnp.float32
bf16 = jnp.bfloat16


def split(value):
    high = value.astype(bf16)
    return high, (value - high.astype(f32)).astype(bf16)


def dot(a, b):
    return lax.dot_general(a, b, (((1,), (0,)), ((), ())), preferred_element_type=f32)


def dot3(a, b):
    ah, al = split(a)
    bh, bl = split(b)
    return dot(ah, bh) + (dot(ah, bl) + dot(al, bh))


def dot2_left(a, exact):
    ah, al = split(a)
    return dot(ah, exact) + dot(al, exact)


def dot2_right(exact, b):
    bh, bl = split(b)
    return dot(exact, bh) + dot(exact, bl)


BLOCK = 256


def inverse_kernel(lower_ref, high_ref, low_ref, made_ref, inv):
    made_ref[...] = jnp.zeros_like(made_ref)
    n = lower_ref.shape[0]
    blocks = n // BLOCK
    rows = lax.broadcasted_iota(jnp.int32, (BLOCK, BLOCK), 0)
    cols = lax.broadcasted_iota(jnp.int32, (BLOCK, BLOCK), 1)
    spans = [pl.ds(b * BLOCK, BLOCK) for b in range(blocks)]
    inv[...] = jnp.zeros_like(inv)
    for span in spans:
        block = lower_ref[span, span].astype(f32)
        diag = jnp.sum(jnp.where(rows == cols, block, 0.0), axis=1, keepdims=True)
        inv[span, span] = jnp.where(rows == cols, 1.0 / diag, 0.0)

    def level(k, carry):
        below = ((rows >> k) == (cols >> k) + 1) & ((rows >> (k + 1)) == (cols >> (k + 1)))
        for span in spans:
            x = inv[span, span]
            off = jnp.where(below, lower_ref[span, span].astype(f32), 0.0).astype(bf16)
            inv[span, span] = x - dot3(dot2_left(x, off), x)
        return carry

    lax.fori_loop(0, int(math.log2(BLOCK)), level, 0)
    size = BLOCK
    while size < n:
        for at in range(0, n, 2 * size):
            top, bottom = pl.ds(at, size), pl.ds(at + size, size)
            a, b = inv[top, top], inv[bottom, bottom]
            inv[bottom, top] = -dot3(b, dot2_right(lower_ref[bottom, top], a))
        size *= 2
    xh, xl = split(inv[...])
    xht, xlt = split(inv[...].T)
    for span in spans:
        at, cols = slice(span.start, n), slice(span.start, span.start + BLOCK)
        m = dot(xht[:, at], xh[at, cols]) + (dot(xht[:, at], xl[at, cols]) + dot(xlt[:, at], xh[at, cols]))
        high_ref[:, span], low_ref[:, span] = split(m)


def coarse_inverse(lower):
    n = lower.shape[0]
    return pl.pallas_call(
        inverse_kernel,
        out_shape=[jax.ShapeDtypeStruct((n, n), bf16)] * 2 + [jax.ShapeDtypeStruct((8, 128), f32)],
        in_specs=[pl.BlockSpec(memory_space=pltpu.VMEM)],
        out_specs=[pl.BlockSpec(memory_space=pltpu.VMEM)] * 3,
        scratch_shapes=[pltpu.VMEM((n, n), f32)],
        compiler_params=pltpu.CompilerParams(vmem_limit_bytes=30 * 1024 * 1024),
        cost_estimate=pl.CostEstimate(flops=20 * 10**9, bytes_accessed=6 * 2**20, transcendentals=0),
    )(lower)


ROWS = 256


def feature_kernel(
    core_ref, samples_hbm, mine_hbm, other_hbm, targets_hbm, after_hbm, feat_ref, part_ref, samples, proj, targets, acc, sems
):
    del after_hbm
    n, parts, panels = samples.shape[0], part_ref.shape[0], proj.shape[0]
    core = core_ref[0]
    get_samples = pltpu.make_async_copy(samples_hbm, samples, sems.at[0])
    get_targets = pltpu.make_async_copy(targets_hbm, targets, sems.at[1])
    get_proj = [
        [
            pltpu.make_async_copy(half.at[:, j], proj.at[j, :, at], sems.at[2 + 2 * j + k])
            for k, (half, at) in enumerate(((mine_hbm, core), (other_hbm, 1 - core)))
        ]
        for j in range(panels)
    ]
    for copy in [get_samples] + sum(get_proj, []) + [get_targets]:
        copy.start()
    get_samples.wait()
    total = None
    for j in range(panels):
        for copy in get_proj[j]:
            copy.wait()
        panel = proj[j].reshape(samples.shape[1], proj.shape[-1])
        if j == panels - 1:
            get_targets.wait()
        for at in range(0, n, ROWS):
            value = dot(samples[at : at + ROWS, :], panel)
            if j:
                value = acc[at : at + ROWS, :] * value
            if j < panels - 1:
                acc[at : at + ROWS, :] = value
            else:
                feat = (value * (1.0 / math.sqrt(F))).astype(bf16)
                feat_ref[at : at + ROWS, :] = feat
                term = dot(targets[:, at : at + ROWS], feat)
                total = term if total is None else total + term
    step = total.shape[0] // parts
    for p in range(parts):
        part_ref[p] = total[p * step : (p + 1) * step, :]


def make_features(core, samples, mine, other, targets_t, parts, after):
    n = samples.shape[0]
    chips, panels, rows, width = mine.shape
    return pl.pallas_call(
        feature_kernel,
        out_shape=[
            jax.ShapeDtypeStruct((n, width), bf16),
            jax.ShapeDtypeStruct((parts, targets_t.shape[0] // parts, width), f32),
        ],
        in_specs=[pl.BlockSpec(memory_space=pltpu.SMEM)] + [pl.BlockSpec(memory_space=pl.ANY)] * 5,
        out_specs=[pl.BlockSpec(memory_space=pltpu.VMEM)] * 2,
        scratch_shapes=[
            pltpu.VMEM(samples.shape, bf16),
            pltpu.VMEM((panels, chips, 2, rows, width), bf16),
            pltpu.VMEM(targets_t.shape, bf16),
            pltpu.VMEM((n, width), f32),
            pltpu.SemaphoreType.DMA((2 + 2 * panels,)),
        ],
        compiler_params=pltpu.CompilerParams(vmem_limit_bytes=58 * 1024 * 1024),
        cost_estimate=pl.CostEstimate(flops=2 * 10**9, bytes_accessed=5 * 2**20, transcendentals=0),
    )(core, samples, mine, other, targets_t, after)


SLOTS = 128


def row_sum(value):
    return jnp.sum(value, axis=1, keepdims=True)


def lane(value, k):
    at = lax.broadcasted_iota(jnp.int32, value.shape, 1)
    return row_sum(jnp.where(at == k, value, 0.0))


def gathered(got_ref, halves, count):
    parts = []
    for h in range(halves):
        acc = got_ref[h, :, :count].astype(f32)
        for p in range(h + halves, got_ref.shape[0], halves):
            acc = acc + got_ref[p, :, :count].astype(f32)
        parts.append(acc)
    dots = got_ref[0, :, count:].astype(f32)
    for p in range(1, got_ref.shape[0]):
        dots = dots + got_ref[p, :, count:].astype(f32)
    at = lax.broadcasted_iota(jnp.int32, dots.shape, 1)
    sums = [row_sum(jnp.where((at >= 3 * k) & (at < 3 * k + 3), dots, 0.0)) for k in range(3)]
    return parts, sums


def coarse(parts, high_ref, low_ref):
    rows, total = parts[0].shape[0], None
    for h, part in enumerate(parts):
        span = slice(h * part.shape[1], (h + 1) * part.shape[1])
        high = part.astype(bf16).astype(f32)
        both = jnp.concatenate([high, part - high], 0).astype(bf16)
        one = dot(both, high_ref[span, :])
        term = one[:rows] + one[rows:] + dot(both, low_ref[span, :])[:rows]
        total = term if total is None else total + term
    return total


def next_direction(parity_ref, parts, high_ref, low_ref, resid, scale, energy, factor):
    count = resid.shape[1]
    solved = coarse(parts, high_ref, low_ref)
    product = energy
    mine = solved[:, :count]
    for h, part in enumerate(parts):
        here = solved[:, h * count : (h + 1) * count]
        product = product + row_sum(part * here)
        if h:
            mine = jnp.where(parity_ref[0] == h, here, mine)
    return product, scale * resid + factor * mine


def first_kernel(factor, parity_ref, got_ref, high_ref, low_ref, resid_ref, scale_ref, dir_ref, send_ref, rho_ref, dots_ref):
    count = resid_ref.shape[1]
    parts, sums = gathered(got_ref, rho_ref.shape[1] // count, count)
    parts = [part * factor for part in parts]
    product, direction = next_direction(
        parity_ref, parts, high_ref, low_ref, resid_ref[...], scale_ref[...], sums[0], factor
    )
    dir_ref[...] = direction
    for p in range(send_ref.shape[0]):
        send_ref[p] = direction.astype(bf16)
    for h, part in enumerate(parts):
        rho_ref[:, h * count : (h + 1) * count] = part
    at = lax.broadcasted_iota(jnp.int32, dots_ref.shape, 1)
    dots_ref[...] = jnp.where(at == 0, sums[0], jnp.where(at == 1, product, 0.0))


def step_kernel(
    factor, parity_ref, got_ref, high_ref, low_ref, resid_ref, scale_ref, image_ref, old_ref, rho_ref, dots_ref, answer_ref,
    dir_ref, send_ref, new_rho_ref, new_dots_ref, new_resid_ref, new_answer_ref,
):
    count = resid_ref.shape[1]
    parts, sums = gathered(got_ref, rho_ref.shape[1] // count, count)
    energy, product = lane(dots_ref[...], 0), lane(dots_ref[...], 1)
    alpha = product / sums[0]
    old = old_ref[...]
    new_answer_ref[...] = answer_ref[...] + alpha * old
    resid = resid_ref[...] - alpha * image_ref[...]
    new_resid_ref[...] = resid
    energy = energy - alpha * (2.0 * sums[1] - alpha * sums[2])
    parts = [
        rho_ref[:, h * count : (h + 1) * count] - alpha * (part * factor) for h, part in enumerate(parts)
    ]
    fresh, fine = next_direction(parity_ref, parts, high_ref, low_ref, resid, scale_ref[...], energy, factor)
    direction = fine + fresh / product * old
    dir_ref[...] = direction
    for p in range(send_ref.shape[0]):
        send_ref[p] = direction.astype(bf16)
    for h, part in enumerate(parts):
        new_rho_ref[:, h * count : (h + 1) * count] = part
    at = lax.broadcasted_iota(jnp.int32, dots_ref.shape, 1)
    new_dots_ref[...] = jnp.where(at == 0, energy, jnp.where(at == 1, fresh, 0.0))


def run_coarse(kernel, factor, n_dp, parity, *operands, more=0):
    rows, count = operands[3].shape
    n = operands[1].shape[0]
    vmem = pl.BlockSpec(memory_space=pltpu.VMEM)
    wide = jax.ShapeDtypeStruct((rows, count), f32)
    outs = [
        wide,
        jax.ShapeDtypeStruct((n_dp, rows, count), bf16),
        jax.ShapeDtypeStruct((rows, n), f32),
        jax.ShapeDtypeStruct((rows, SLOTS), f32),
    ] + [wide] * more
    return pl.pallas_call(
        functools.partial(kernel, factor),
        out_shape=outs,
        in_specs=[pl.BlockSpec(memory_space=pltpu.SMEM)] + [vmem] * len(operands),
        out_specs=[vmem] * len(outs),
        compiler_params=pltpu.CompilerParams(vmem_limit_bytes=12 * 1024 * 1024),
        cost_estimate=pl.CostEstimate(flops=10**8, bytes_accessed=5 * 2**20, transcendentals=0),
    )(parity, *operands)


def triple(value):
    high = lax.reduce_precision(value, 8, 7)
    mid = lax.reduce_precision(value - high, 8, 7)
    return jnp.stack([high, mid, value - high - mid], -1).astype(bf16)


def rounded(value):
    return lax.reduce_precision(value, 8, 7).astype(bf16)


def slots(values):
    parts = triple(values)
    flat = parts.reshape(parts.shape[:-2] + (-1,))
    return jnp.pad(flat, ((0, 0),) * (flat.ndim - 1) + ((0, SLOTS - flat.shape[-1]),))


def body(samples, projections, targets, feature_scale, coarse_factor):
    n_dp, n_sk = lax.axis_size("dp"), lax.axis_size("sketch")
    count = projections.shape[2]
    width = targets.shape[1]
    mine = width // n_dp
    cols = width // n_sk
    factor = 1.0 / math.sqrt(F // K)
    halves = K // count
    parity = (lax.axis_index("sketch") % halves).astype(jnp.int32).reshape(1)
    n = samples.shape[0]
    scale = feature_scale[None, :]

    chips = n_dp // 2
    core = (lax.axis_index("dp") % 2).astype(jnp.int32).reshape(1)
    mine_proj = lax.all_to_all(
        jnp.broadcast_to(projections[None], (chips,) + projections.shape),
        "dp",
        0,
        0,
        axis_index_groups=[[2 * z + c for z in range(chips)] for c in range(2)],
    )
    inv_high, inv_low, made = coarse_inverse(coarse_factor)
    mine_proj, made = lax.optimization_barrier((mine_proj, made))
    other_proj = lax.ppermute(mine_proj, "dp", [(i, i ^ 1) for i in range(n_dp)])
    feat, part = make_features(core, samples, mine_proj, other_proj, targets.T, n_dp, made)

    def scatter_dp(value):
        return jnp.sum(lax.all_to_all(value, "dp", 0, 0), 0)

    def gather_sk(value):
        return lax.all_to_all(jnp.broadcast_to(value[None], (n_sk,) + value.shape), "sketch", 0, 0)

    def everywhere(value, dots):
        return gather_sk(jnp.concatenate([value.astype(bf16), slots(dots)], 1))

    def forward(send):
        whole = lax.all_to_all(send, "dp", 0, 0).reshape(width, count)
        sums = lax.dot_general(whole, feat, (((1,), (1,)), ((), ())), preferred_element_type=f32)
        return whole, sums.astype(bf16).reshape(n_sk, cols, n)

    resid = scatter_dp(part)
    got = everywhere(resid, row_sum(scale * resid * resid))
    direction, send, rho, dots = run_coarse(
        first_kernel, factor, n_dp, parity, got, inv_high, inv_low, resid, scale
    )
    answer = jnp.zeros_like(resid)
    for step in range(ITERS - 1):
        _, sums = forward(send)
        u = rounded(jnp.sum(lax.all_to_all(sums, "sketch", 0, 0).astype(f32), 0))
        whole = gather_sk(u).reshape(width, n)
        image = scatter_dp(dot(whole, feat).reshape(n_dp, mine, count)) + RIDGE * direction
        weighted = scale * image
        got = everywhere(
            image,
            jnp.concatenate(
                [row_sum(direction * image), row_sum(weighted * resid), row_sum(weighted * image)], 1
            ),
        )
        direction, send, rho, dots, resid, answer = run_coarse(
            step_kernel, factor, n_dp, parity, got, inv_high, inv_low, resid, scale, image, direction, rho, dots, answer,
            more=2,
        )
    whole, sums = forward(send)
    squares = jnp.sum(jnp.square(whole.astype(f32)), 1).reshape(n_sk, cols, 1)
    got = lax.all_to_all(jnp.concatenate([sums, slots(squares)], 2), "sketch", 0, 0).astype(f32)
    total = jnp.sum(got, 0)
    u = rounded(total[:, :n])
    curve = row_sum(total[:, :n] * u.astype(f32)) + (RIDGE / n_dp) * row_sum(total[:, n:])
    got = gather_sk(jnp.concatenate([u, slots(curve)], 1)).reshape(width, n + SLOTS)
    image = dot(got[:, :n], feat)
    curve = row_sum(got[:, n : n + 3].astype(f32))
    sent = jnp.concatenate([image, jnp.broadcast_to(curve, (width, SLOTS))], 1)
    total = scatter_dp(sent.reshape(n_dp, mine, count + SLOTS))
    image = total[:, :count] + RIDGE * direction
    alpha = dots[:, 1:2] / total[:, count : count + 1]
    out = jnp.stack([answer + alpha * direction, resid - alpha * image])
    got = lax.all_to_all(jnp.broadcast_to(out[None], (n_dp,) + out.shape), "dp", 0, 0)
    return got[:, 0].reshape(width, count).T, got[:, 1].reshape(width, count).T


def solution(mesh):
    placed = (P("dp", None), P(None, "dp", "sketch"), P("dp", None), P("sketch"), P())
    return jax.shard_map(
        body,
        mesh=mesh,
        in_specs=placed,
        out_specs=(P("sketch", None), P("sketch", None)),
        check_vma=False,
    )
```

time: 293 us -> 232 us (0.79)
  waiting for transfers between devices: 61.9 us -> 20.6 us
  between operations: 14.3 us -> 0.88 us
  starting transfers between devices: 13.6 us -> 22.9 us
  blocking collectives: 155 us -> 146 us
  matrix products: 6.37 us -> 1.44 us
  other arithmetic: 4.83 us -> 1.67 us
    all_gather x1 -> x0, waiting for transfers between devices: 51.4 us -> none  [body(): proj = lax.all_gather(projections, 'dp', axis=1, tiled=True)]
    all_to_all x0 -> x1, starting transfers between devices: none -> 10.9 us  [body(): lax.all_to_all(jnp.broadcast_to(projections[None], (chips,) + projections...]
    all_to_all x0 -> x1, waiting for transfers between devices: none -> 8.62 us  [body(): lax.all_to_all(jnp.broadcast_to(projections[None], (chips,) + projections...]
    all_to_all x8, blocking collectives: 112 us -> 106 us  [the longest x3 42.1 us: scatter_dp(): return jnp.sum(lax.all_to_all(value, 'dp', 0, 0), 0)]
    dot_general x6 -> x2, matrix products: 5.51 us -> 0.56 us  [dot(): lax.dot_general(a, b, (((1,), (0,)), ((), ())), preferred_element_type=f32)]
    pallas_call x1, Pallas kernels: 21.1 us -> 17 us  [coarse_inverse(): pl.pallas_call(inverse_kernel, out_shape=[jax.ShapeDtypeStruct((n, n), bf...]
    all_to_all x2 -> x1, starting transfers between devices: 13.5 us -> 9.67 us  [gather_sk(): lax.all_to_all(jnp.broadcast_to(value[None], (n_sk,) + value.shape), 'ske...]
    all_to_all x3, blocking collectives: 43.3 us -> 39.9 us  [gather_sk(): lax.all_to_all(jnp.broadcast_to(value[None], (n_sk,) + value.shape), 'ske...]
  transfers between devices with their start and end apart: 3 -> 3, of which waited for: 2 -> 3; matrix products, arithmetic and copies ran while one was open for 0% -> 0% of each run, Pallas kernels for 7% -> 7%
where the time goes in v2:
time: 232 us; the launch traced here: 231 us
  blocking collectives  146 us (63%)
  Pallas kernels  24.9 us (11%)
  starting transfers between devices  22.9 us (10%)
  waiting for transfers between devices  20.6 us (9%)
  local copies, waits for them, and re-layouts  12.3 us (5%)
    all_to_all x3, blocking collectives, scatter_dp(): return jnp.sum(lax.all_to_all(value, 'dp', 0, 0), 0)  42.1 us
    all_to_all x3, blocking collectives, gather_sk(): lax.all_to_all(jnp.broadcast_to(value[None], (n_sk,) + value.shape), 'ske...  39.9 us
    all_to_all x2, blocking collectives, forward(): whole = lax.all_to_all(send, 'dp', 0, 0).reshape(width, count)  23.9 us
    pallas_call x1, Pallas kernels, coarse_inverse(): pl.pallas_call(inverse_kernel, out_shape=[jax.ShapeDtypeStruct((n, n), bf...  17 us
    all_to_all x1, blocking collectives, body(): lax.all_to_all(jnp.broadcast_to(out[None], (n_dp,) + out.shape), 'dp', 0, 0)  14.2 us
    all_to_all x1, blocking collectives, body(): lax.all_to_all(jnp.concatenate([sums, slots(squares)], 2), 'sketch', 0, 0)  13.1 us
    all_to_all x1, blocking collectives, body(): u = rounded(jnp.sum(lax.all_to_all(sums, 'sketch', 0, 0).astype(f32), 0))  13 us
    all_to_all x1, starting transfers between devices, body(): lax.all_to_all(jnp.broadcast_to(projections[None], (chips,) + projections...  10.9 us
  transfers between devices with their start and end apart: 3, of which 3 were waited for; matrix products, arithmetic and copies ran while one was open for 0% of the time, Pallas kernels for 7%

profile of v2, /device:TPU:1, one launch (start us, length us, event | category | flops | bytes accessed | tf_op | source)
XLA Modules:
  0.0 230.9 jit_solution(9969295103317197016)
XLA Ops:
  0.6 2.0 broadcast_in_dim.18
  2.6 10.9 %all-to-all-start = ((bf16[8,4,32,512]{3,2,1,0:T(8,128)(2,1)}), bf16[8,4,32,512]{3,2,1,0:T(8,128)(2,1)S(1)}, u32[]{:S(2)}, u32[]{:S(2)}) async-start(bf16[8,4,32,512]{3,2,1,0:T(8,128)(2,1)} %broadcast_in_dim.18), calls=%async_computation | async-start | bytes 2097152 | tf_op jit(solution)/shard_map/all_to_all | solution.py:311
  13.5 1.6 copy-done.4
  15.1 17.0 %shard_map.68 = (bf16[1024,1024]{1,0:T(8,128)(2,1)S(1)}, bf16[1024,1024]{1,0:T(8,128)(2,1)S(1)}, f32[8,128]{1,0:T(8,128)S(1)}) custom-call(bf16[1024,1024]{1,0:T(8,128)(2,1)S(1)} %copy-done.4), custom_call_target="tpu_custom_call" | custom-call | flops 20000000000 | bytes 6291456 | tf_op jit(solution)/shard_map/pallas_call | solution.py:87
  34.1 8.6 %all-to-all-done.mine_hbm = bf16[8,4,32,512]{3,2,1,0:T(8,128)(2,1)S(1)} async-done(((bf16[8,4,32,512]{3,2,1,0:T(8,128)(2,1)}), bf16[8,4,32,512]{3,2,1,0:T(8,128)(2,1)S(1)}, u32[]{:S(2)}, u32[]{:S(2)}) %all-to-all-start) | async-done | bytes 1048608 | tf_op jit(solution)/shard_map/all_to_all | solution.py:311
  42.7 2.4 %collective-permute-start = (bf16[8,4,32,512]{3,2,1,0:T(8,128)(2,1)S(1)}, bf16[8,4,32,512]{3,2,1,0:T(8,128)(2,1)}, u32[]{:S(2)}, u32[]{:S(2)}) collective-permute-start(bf16[8,4,32,512]{3,2,1,0:T(8,128)(2,1)S(1)} %all-to-all-done.mine_hbm), channel_id=1, source_target_pairs={{0,32},{32,0},{64,96},{96,64},{128,160},{160,128},{192,224},{224,1... | collective-permute-start | bytes 3145736 | tf_op jit(solution)/shard_map/ppermute | solution.py:320
  45.1 2.4 %collective-permute-done.other_hbm = bf16[8,4,32,512]{3,2,1,0:T(8,128)(2,1)} collective-permute-done((bf16[8,4,32,512]{3,2,1,0:T(8,128)(2,1)S(1)}, bf16[8,4,32,512]{3,2,1,0:T(8,128)(2,1)}, u32[]{:S(2)}, u32[]{:S(2)}) %collective-permute-start) | collective-permute-done | bytes 1048608 | tf_op jit(solution)/shard_map/ppermute | solution.py:320
  47.5 5.7 %shard_map.69 = (bf16[1024,512]{1,0:T(8,128)(2,1)}, f32[16,4,512]{2,1,0:T(4,128)}) custom-call(s32[1]{0:T(128)} %bitcast.1.core_ref, bf16[1024,512]{1,0:T(8,128)(2,1)} %samples_hbm.1, bf16[8,4,32,512]{3,2,1,0:T(8,128)(2,1)} %copy-done.7, bf16[8,4,32,512]{3,2,1,0:T(8,128)(2,1)} %collective-permute-done.other_hbm, bf16[64,1024]{1,0:T(8,128)(2,1)} %bitcast.39, ...), custom_call_target="tpu_custom_call" | custom-call | flops 2000000000 | bytes 5242880 | tf_op jit(solution)/shard_map/pallas_call | solution.py:145
  53.2 12.9 %all_to_all.65 = f32[16,4,512]{2,1,0:T(4,128)S(1)} all-to-all(f32[16,4,512]{2,1,0:T(4,128)} %get-tuple-element.21), channel_id=1, replica_groups=mesh['dp'=16,'sketch'=32] {'dp'}, dimensions={0} | all-to-all | bytes 262144 | tf_op jit(solution)/shard_map/all_to_all | solution.py:324
  67.2 9.7 %all-to-all-start.2 = ((bf16[32,4,640]{2,1,0:T(4,128)(2,1)}), bf16[32,4,640]{2,1,0:T(4,128)(2,1)S(1)}, u32[]{:S(2)}, u32[]{:S(2)}) async-start(bf16[32,4,640]{2,1,0:T(4,128)(2,1)} %broadcast_in_dim.19), calls=%async_computation.2 | async-start | bytes 327680 | tf_op jit(solution)/shard_map/all_to_all | solution.py:327
  76.9 9.6 %all-to-all-done.2.got_ref = bf16[32,4,640]{2,1,0:T(4,128)(2,1)S(1)} async-done(((bf16[32,4,640]{2,1,0:T(4,128)(2,1)}), bf16[32,4,640]{2,1,0:T(4,128)(2,1)S(1)}, u32[]{:S(2)}, u32[]{:S(2)}) %all-to-all-start.2) | async-done | bytes 163872 | tf_op jit(solution)/shard_map/all_to_all | solution.py:327
  86.5 1.6 copy-done.1
  88.8 12.0 %all_to_all.66 = bf16[16,4,512]{2,1,0:T(4,128)(2,1)S(1)} all-to-all(bf16[16,4,512]{2,1,0:T(4,128)(2,1)S(1)} %get-tuple-element.24), channel_id=1, replica_groups=mesh['dp'=16,'sketch'=32] {'dp'}, dimensions={0} | all-to-all | bytes 131072 | tf_op jit(solution)/shard_map/all_to_all | solution.py:333
  101.3 13.0 %all_to_all.67 = bf16[32,2,1024]{2,1,0:T(2,128)(2,1)S(1)} all-to-all(bf16[32,2,1024]{2,1,0:T(2,128)(2,1)S(1)} %reshape.407), channel_id=1, replica_groups=mesh['dp'=16,'sketch'=32] {'sketch'}, dimensions={0} | all-to-all | bytes 262144 | tf_op jit(solution)/shard_map/all_to_all | solution.py:345
  114.6 13.4 %all_to_all.68 = bf16[32,2,1024]{2,1,0:T(2,128)(2,1)S(1)} all-to-all(bf16[32,2,1024]{2,1,0:T(2,128)(2,1)S(1)} %broadcast_in_dim.21), channel_id=1, replica_groups=mesh['dp'=16,'sketch'=32] {'sketch'}, dimensions={0} | all-to-all | bytes 262144 | tf_op jit(solution)/shard_map/all_to_all | solution.py:327
  128.4 14.3 %all_to_all.69 = f32[16,4,512]{2,1,0:T(4,128)S(1)} all-to-all(f32[16,4,512]{2,1,0:T(4,128)S(1)} %copy.53), channel_id=1, replica_groups=mesh['dp'=16,'sketch'=32] {'dp'}, dimensions={0} | all-to-all | bytes 262144 | tf_op jit(solution)/shard_map/all_to_all | solution.py:324
  143.1 12.8 %all_to_all.70.got_ref = bf16[32,4,640]{2,1,0:T(4,128)(2,1)S(1)} all-to-all(bf16[32,4,640]{2,1,0:T(4,128)(2,1)S(1)} %broadcast_in_dim.22), channel_id=1, replica_groups=mesh['dp'=16,'sketch'=32] {'sketch'}, dimensions={0} | all-to-all | bytes 327680 | tf_op jit(solution)/shard_map/all_to_all | solution.py:327
  155.9 1.6 copy-done.2
  157.5 1.4 shard_map.71
  158.8 12.0 %all_to_all.71 = bf16[16,4,512]{2,1,0:T(4,128)(2,1)S(1)} all-to-all(bf16[16,4,512]{2,1,0:T(4,128)(2,1)S(1)} %get-tuple-element.31), channel_id=1, replica_groups=mesh['dp'=16,'sketch'=32] {'dp'}, dimensions={0} | all-to-all | bytes 131072 | tf_op jit(solution)/shard_map/all_to_all | solution.py:333
  171.9 13.1 %all_to_all.72 = bf16[32,2,1152]{2,1,0:T(2,128)(2,1)S(1)} all-to-all(bf16[32,2,1152]{2,1,0:T(2,128)(2,1)S(1)} %fusion.2), channel_id=1, replica_groups=mesh['dp'=16,'sketch'=32] {'sketch'}, dimensions={0} | all-to-all | bytes 294912 | tf_op jit(solution)/shard_map/all_to_all | solution.py:361
  185.6 13.8 %all_to_all.73 = bf16[32,2,1152]{2,1,0:T(2,128)(2,1)S(1)} all-to-all(bf16[32,2,1152]{2,1,0:T(2,128)(2,1)S(1)} %broadcast_in_dim.24), channel_id=1, replica_groups=mesh['dp'=16,'sketch'=32] {'sketch'}, dimensions={0} | all-to-all | bytes 294912 | tf_op jit(solution)/shard_map/all_to_all | solution.py:327
  200.0 15.0 %all_to_all.74 = f32[16,4,640]{2,1,0:T(4,128)S(1)} all-to-all(f32[16,4,640]{2,1,0:T(4,128)S(1)} %reshape.412), channel_id=1, replica_groups=mesh['dp'=16,'sketch'=32] {'dp'}, dimensions={0} | all-to-all | bytes 327680 | tf_op jit(solution)/shard_map/all_to_all | solution.py:324
  215.3 14.2 %all_to_all.75 = f32[16,2,4,512]{3,2,1,0:T(4,128)S(1)} all-to-all(f32[16,2,4,512]{3,2,1,0:T(4,128)S(1)} %broadcast_in_dim.26), channel_id=1, replica_groups=mesh['dp'=16,'sketch'=32] {'dp'}, dimensions={0} | all-to-all | bytes 524288 | tf_op jit(solution)/shard_map/all_to_all | solution.py:373
  (75 shorter events, 9.3 us)
Async XLA Ops:
  2.6 40.1 %all-to-all-start = ((bf16[8,4,32,512]{3,2,1,0:T(8,128)(2,1)}), bf16[8,4,32,512]{3,2,1,0:T(8,128)(2,1)S(1)}, u32[]{:S(2)}, u32[]{:S(2)}) async-start(bf16[8,4,32,512]{3,2,1,0:T(8,128)(2,1)} %broadcast_in_dim.18), calls=%async_computation | async-start | bytes 2097152 | tf_op jit(solution)/shard_map/all_to_all | solution.py:311
  13.5 1.6 copy-start.4
  32.1 1.4 copy-start
  33.5 0.6 copy-start.5
  42.7 4.8 %copy-start.7 = (bf16[8,4,32,512]{3,2,1,0:T(8,128)(2,1)}, bf16[8,4,32,512]{3,2,1,0:T(8,128)(2,1)S(1)}, u32[]{:S(2)}) copy-start(bf16[8,4,32,512]{3,2,1,0:T(8,128)(2,1)S(1)} %all-to-all-done.mine_hbm) | copy-start | bytes 3145732
  42.7 4.8 %collective-permute-start = (bf16[8,4,32,512]{3,2,1,0:T(8,128)(2,1)S(1)}, bf16[8,4,32,512]{3,2,1,0:T(8,128)(2,1)}, u32[]{:S(2)}, u32[]{:S(2)}) collective-permute-start(bf16[8,4,32,512]{3,2,1,0:T(8,128)(2,1)S(1)} %all-to-all-done.mine_hbm), channel_id=1, source_target_pairs={{0,32},{32,0},{64,96},{96,64},{128,160},{160,128},{192,224},{224,1... | collective-permute-start | bytes 3145736 | tf_op jit(solution)/shard_map/ppermute | solution.py:320
  47.5 18.7 %copy-start.3 = (f32[512]{0:T(512)S(1)}, f32[512]{0:T(512)}, u32[]{:S(2)}) copy-start(f32[512]{0:T(512)} %param.8) | copy-start | bytes 6148
  67.2 19.3 %all-to-all-start.2 = ((bf16[32,4,640]{2,1,0:T(4,128)(2,1)}), bf16[32,4,640]{2,1,0:T(4,128)(2,1)S(1)}, u32[]{:S(2)}, u32[]{:S(2)}) async-start(bf16[32,4,640]{2,1,0:T(4,128)(2,1)} %broadcast_in_dim.19), calls=%async_computation.2 | async-start | bytes 327680 | tf_op jit(solution)/shard_map/all_to_all | solution.py:327
  86.5 1.6 copy-start.1
  88.1 12.7 %copy-start.6 = (bf16[1024,512]{1,0:T(8,128)(2,1)S(1)}, bf16[1024,512]{1,0:T(8,128)(2,1)}, u32[]{:S(2)}) copy-start(bf16[1024,512]{1,0:T(8,128)(2,1)} %get-tuple-element.25) | copy-start | bytes 3145732
  155.9 1.6 copy-start.2

commit v3 on v2

--- a/solution.py
+++ b/solution.py
@@ -45,63 +45,137 @@
 BLOCK = 256
 
 
-def inverse_kernel(lower_ref, high_ref, low_ref, made_ref, inv):
-    made_ref[...] = jnp.zeros_like(made_ref)
-    n = lower_ref.shape[0]
+def inverse_kernel(core_ref, lower_hbm, high_ref, low_ref, made_ref, lower, inv, sems):
+    n = lower.shape[0]
     blocks = n // BLOCK
+    spans = [pl.ds(b * BLOCK, BLOCK) for b in range(blocks)]
+    parts = [(span, span) for span in spans]
+    size = BLOCK
+    while size < n:
+        parts += [(pl.ds(at + size, size), pl.ds(at, size)) for at in range(0, n, 2 * size)]
+        size *= 2
+    copies = [
+        pltpu.make_async_copy(lower_hbm.at[part], lower.at[part], sems.at[k]) for k, part in enumerate(parts)
+    ]
+    for copy in copies:
+        copy.start()
+    made_ref[0] = core_ref[0]
+    inv[...] = jnp.zeros_like(inv)
     rows = lax.broadcasted_iota(jnp.int32, (BLOCK, BLOCK), 0)
     cols = lax.broadcasted_iota(jnp.int32, (BLOCK, BLOCK), 1)
-    spans = [pl.ds(b * BLOCK, BLOCK) for b in range(blocks)]
-    inv[...] = jnp.zeros_like(inv)
-    for span in spans:
-        block = lower_ref[span, span].astype(f32)
-        diag = jnp.sum(jnp.where(rows == cols, block, 0.0), axis=1, keepdims=True)
-        inv[span, span] = jnp.where(rows == cols, 1.0 / diag, 0.0)
+
+    def below(k):
+        return ((rows >> k) == (cols >> k) + 1) & ((rows >> (k + 1)) == (cols >> (k + 1)))
+
+    for copy, span in zip(copies, spans):
+        copy.wait()
+        block = lower[span, span].astype(f32)
+        diag = jnp.where(rows == cols, block, 0.0)
+        down = 1.0 / jnp.sum(diag, axis=1, keepdims=True)
+        across = 1.0 / jnp.sum(diag, axis=0, keepdims=True)
+        inv[span, span] = jnp.where(rows == cols, down, jnp.where(below(0), -(block * down) * across, 0.0))
 
     def level(k, carry):
-        below = ((rows >> k) == (cols >> k) + 1) & ((rows >> (k + 1)) == (cols >> (k + 1)))
+        mask = below(k)
         for span in spans:
             x = inv[span, span]
-            off = jnp.where(below, lower_ref[span, span].astype(f32), 0.0).astype(bf16)
+            off = jnp.where(mask, lower[span, span].astype(f32), 0.0).astype(bf16)
             inv[span, span] = x - dot3(dot2_left(x, off), x)
         return carry
 
-    lax.fori_loop(0, int(math.log2(BLOCK)), level, 0)
-    size = BLOCK
-    while size < n:
-        for at in range(0, n, 2 * size):
-            top, bottom = pl.ds(at, size), pl.ds(at + size, size)
-            a, b = inv[top, top], inv[bottom, bottom]
-            inv[bottom, top] = -dot3(b, dot2_right(lower_ref[bottom, top], a))
-        size *= 2
-    xh, xl = split(inv[...])
-    xht, xlt = split(inv[...].T)
+    lax.fori_loop(1, int(math.log2(BLOCK)), level, 0)
+    for copy, (bottom, top) in list(zip(copies, parts))[blocks:]:
+        copy.wait()
+        a, b = inv[top, top], inv[bottom, bottom]
+        inv[bottom, top] = -dot3(b, dot2_right(lower[bottom, top], a))
     for span in spans:
-        at, cols = slice(span.start, n), slice(span.start, span.start + BLOCK)
-        m = dot(xht[:, at], xh[at, cols]) + (dot(xht[:, at], xl[at, cols]) + dot(xlt[:, at], xh[at, cols]))
-        high_ref[:, span], low_ref[:, span] = split(m)
-
-
-def coarse_inverse(lower):
+        high_ref[span, :], low_ref[span, :] = split(inv[span, :])
+
+
+def coarse_factor_inverse(core, lower):
     n = lower.shape[0]
+    vmem = pl.BlockSpec(memory_space=pltpu.VMEM)
     return pl.pallas_call(
         inverse_kernel,
-        out_shape=[jax.ShapeDtypeStruct((n, n), bf16)] * 2 + [jax.ShapeDtypeStruct((8, 128), f32)],
-        in_specs=[pl.BlockSpec(memory_space=pltpu.VMEM)],
-        out_specs=[pl.BlockSpec(memory_space=pltpu.VMEM)] * 3,
-        scratch_shapes=[pltpu.VMEM((n, n), f32)],
-        compiler_params=pltpu.CompilerParams(vmem_limit_bytes=30 * 1024 * 1024),
-        cost_estimate=pl.CostEstimate(flops=20 * 10**9, bytes_accessed=6 * 2**20, transcendentals=0),
-    )(lower)
+        out_shape=[jax.ShapeDtypeStruct((n, n), bf16)] * 2 + [jax.ShapeDtypeStruct((1,), jnp.int32)],
+        in_specs=[pl.BlockSpec(memory_space=pltpu.SMEM), pl.BlockSpec(memory_space=pl.ANY)],
+        out_specs=[vmem] * 2 + [pl.BlockSpec(memory_space=pltpu.SMEM)],
+        scratch_shapes=[
+            pltpu.VMEM((n, n), bf16),
+            pltpu.VMEM((n, n), f32),
+            pltpu.SemaphoreType.DMA((2 * (n // BLOCK) - 1,)),
+        ],
+        compiler_params=pltpu.CompilerParams(vmem_limit_bytes=56 * 1024 * 1024),
+        cost_estimate=pl.CostEstimate(flops=10**10, bytes_accessed=6 * 2**20, transcendentals=0),
+    )(core, lower)
+
+
+def product_kernel(xh_ref, xl_ref, high_ref, low_ref):
+    n = xh_ref.shape[0]
+    xht = xh_ref[...].astype(f32).T.astype(bf16)
+    xlt = xl_ref[...].astype(f32).T.astype(bf16)
+    for start in range(0, n, BLOCK):
+        at, cols = slice(start, n), slice(start, start + BLOCK)
+        xh, xl = xh_ref[at, cols], xl_ref[at, cols]
+        m = dot(xht[:, at], xh) + (dot(xht[:, at], xl) + dot(xlt[:, at], xh))
+        high_ref[:, cols], low_ref[:, cols] = split(m)
+
+
+def coarse_inverse(xh, xl):
+    n = xh.shape[0]
+    vmem = pl.BlockSpec(memory_space=pltpu.VMEM)
+    return pl.pallas_call(
+        product_kernel,
+        out_shape=[jax.ShapeDtypeStruct((n, n), bf16)] * 2,
+        in_specs=[vmem] * 2,
+        out_specs=[vmem] * 2,
+        compiler_params=pltpu.CompilerParams(vmem_limit_bytes=56 * 1024 * 1024),
+        cost_estimate=pl.CostEstimate(flops=4 * 10**9, bytes_accessed=8 * 2**20, transcendentals=0),
+    )(xh, xl)
+
+
+def copies_kernel(value_hbm, out_hbm, sems):
+    copies = [pltpu.make_async_copy(value_hbm, out_hbm.at[p], sems.at[p]) for p in range(out_hbm.shape[0])]
+    for copy in copies:
+        copy.start()
+    for copy in copies:
+        copy.wait()
+
+
+def repeat(value, count):
+    return pl.pallas_call(
+        copies_kernel,
+        out_shape=jax.ShapeDtypeStruct((count,) + value.shape, value.dtype),
+        in_specs=[pl.BlockSpec(memory_space=pl.ANY)],
+        out_specs=pl.BlockSpec(memory_space=pl.ANY),
+        scratch_shapes=[pltpu.SemaphoreType.DMA((count,))],
+    )(value)
+
+
+def output_kernel(got_ref, answer_ref, resid_ref):
+    rows = got_ref.shape[2]
+    for p in range(got_ref.shape[0]):
+        answer_ref[p * rows : (p + 1) * rows, :] = got_ref[p, 0].astype(f32)
+        resid_ref[p * rows : (p + 1) * rows, :] = got_ref[p, 1].astype(f32)
+
+
+def outputs(got):
+    parts, _, rows, count = got.shape
+    vmem = pl.BlockSpec(memory_space=pltpu.VMEM)
+    return pl.pallas_call(
+        output_kernel,
+        out_shape=[jax.ShapeDtypeStruct((parts * rows, count), f32)] * 2,
+        in_specs=[vmem],
+        out_specs=[vmem] * 2,
+    )(got)
 
 
 ROWS = 256
 
 
 def feature_kernel(
-    core_ref, samples_hbm, mine_hbm, other_hbm, targets_hbm, after_hbm, feat_ref, part_ref, samples, proj, targets, acc, sems
+    core_ref, samples_hbm, mine_hbm, other_hbm, targets_hbm, feat_ref, part_ref, samples, proj, targets, acc, sems
 ):
-    del after_hbm
     n, parts, panels = samples.shape[0], part_ref.shape[0], proj.shape[0]
     core = core_ref[0]
     get_samples = pltpu.make_async_copy(samples_hbm, samples, sems.at[0])
@@ -139,7 +213,7 @@
         part_ref[p] = total[p * step : (p + 1) * step, :]
 
 
-def make_features(core, samples, mine, other, targets_t, parts, after):
+def make_features(core, samples, mine, other, targets_t, parts):
     n = samples.shape[0]
     chips, panels, rows, width = mine.shape
     return pl.pallas_call(
@@ -148,7 +222,7 @@
             jax.ShapeDtypeStruct((n, width), bf16),
             jax.ShapeDtypeStruct((parts, targets_t.shape[0] // parts, width), f32),
         ],
-        in_specs=[pl.BlockSpec(memory_space=pltpu.SMEM)] + [pl.BlockSpec(memory_space=pl.ANY)] * 5,
+        in_specs=[pl.BlockSpec(memory_space=pltpu.SMEM)] + [pl.BlockSpec(memory_space=pl.ANY)] * 4,
         out_specs=[pl.BlockSpec(memory_space=pltpu.VMEM)] * 2,
         scratch_shapes=[
             pltpu.VMEM(samples.shape, bf16),
@@ -157,9 +231,9 @@
             pltpu.VMEM((n, width), f32),
             pltpu.SemaphoreType.DMA((2 + 2 * panels,)),
         ],
-        compiler_params=pltpu.CompilerParams(vmem_limit_bytes=58 * 1024 * 1024),
+        compiler_params=pltpu.CompilerParams(vmem_limit_bytes=48 * 1024 * 1024),
         cost_estimate=pl.CostEstimate(flops=2 * 10**9, bytes_accessed=5 * 2**20, transcendentals=0),
-    )(core, samples, mine, other, targets_t, after)
+    )(core, samples, mine, other, targets_t)
 
 
 SLOTS = 128
@@ -189,21 +263,38 @@
     return parts, sums
 
 
-def coarse(parts, high_ref, low_ref):
+def fetch(high_hbm, low_hbm, high, low, sems, halves):
+    span = high.shape[0] // halves
+    copies = [
+        [
+            pltpu.make_async_copy(src.at[pl.ds(h * span, span)], dst.at[pl.ds(h * span, span)], sems.at[2 * h + k])
+            for k, (src, dst) in enumerate(((high_hbm, high), (low_hbm, low)))
+        ]
+        for h in range(halves)
+    ]
+    for copy in sum(copies, []):
+        copy.start()
+    return high, low, copies
+
+
+def coarse(parts, inverse):
+    high_ref, low_ref, copies = inverse
     rows, total = parts[0].shape[0], None
     for h, part in enumerate(parts):
         span = slice(h * part.shape[1], (h + 1) * part.shape[1])
         high = part.astype(bf16).astype(f32)
         both = jnp.concatenate([high, part - high], 0).astype(bf16)
+        copies[h][0].wait()
         one = dot(both, high_ref[span, :])
+        copies[h][1].wait()
         term = one[:rows] + one[rows:] + dot(both, low_ref[span, :])[:rows]
         total = term if total is None else total + term
     return total
 
 
-def next_direction(parity_ref, parts, high_ref, low_ref, resid, scale, energy, factor):
+def next_direction(parity_ref, parts, inverse, resid, scale, energy, factor):
     count = resid.shape[1]
-    solved = coarse(parts, high_ref, low_ref)
+    solved = coarse(parts, inverse)
     product = energy
     mine = solved[:, :count]
     for h, part in enumerate(parts):
@@ -214,12 +305,15 @@
     return product, scale * resid + factor * mine
 
 
-def first_kernel(factor, parity_ref, got_ref, high_ref, low_ref, resid_ref, scale_ref, dir_ref, send_ref, rho_ref, dots_ref):
+def first_kernel(
+    factor, parity_ref, got_ref, high_hbm, low_hbm, resid_ref, scale_ref, dir_ref, send_ref, rho_ref, dots_ref, high, low, sems
+):
     count = resid_ref.shape[1]
+    inverse = fetch(high_hbm, low_hbm, high, low, sems, rho_ref.shape[1] // count)
     parts, sums = gathered(got_ref, rho_ref.shape[1] // count, count)
     parts = [part * factor for part in parts]
     product, direction = next_direction(
-        parity_ref, parts, high_ref, low_ref, resid_ref[...], scale_ref[...], sums[0], factor
+        parity_ref, parts, inverse, resid_ref[...], scale_ref[...], sums[0], factor
     )
     dir_ref[...] = direction
     for p in range(send_ref.shape[0]):
@@ -231,10 +325,11 @@
 
 
 def step_kernel(
-    factor, parity_ref, got_ref, high_ref, low_ref, resid_ref, scale_ref, image_ref, old_ref, rho_ref, dots_ref, answer_ref,
-    dir_ref, send_ref, new_rho_ref, new_dots_ref, new_resid_ref, new_answer_ref,
+    factor, parity_ref, got_ref, high_hbm, low_hbm, resid_ref, scale_ref, image_ref, old_ref, rho_ref, dots_ref, answer_ref,
+    dir_ref, send_ref, new_rho_ref, new_dots_ref, new_resid_ref, new_answer_ref, high, low, sems,
 ):
     count = resid_ref.shape[1]
+    inverse = fetch(high_hbm, low_hbm, high, low, sems, rho_ref.shape[1] // count)
     parts, sums = gathered(got_ref, rho_ref.shape[1] // count, count)
     energy, product = lane(dots_ref[...], 0), lane(dots_ref[...], 1)
     alpha = product / sums[0]
@@ -246,7 +341,7 @@
     parts = [
         rho_ref[:, h * count : (h + 1) * count] - alpha * (part * factor) for h, part in enumerate(parts)
     ]
-    fresh, fine = next_direction(parity_ref, parts, high_ref, low_ref, resid, scale_ref[...], energy, factor)
+    fresh, fine = next_direction(parity_ref, parts, inverse, resid, scale_ref[...], energy, factor)
     direction = fine + fresh / product * old
     dir_ref[...] = direction
     for p in range(send_ref.shape[0]):
@@ -271,9 +366,12 @@
     return pl.pallas_call(
         functools.partial(kernel, factor),
         out_shape=outs,
-        in_specs=[pl.BlockSpec(memory_space=pltpu.SMEM)] + [vmem] * len(operands),
+        in_specs=[pl.BlockSpec(memory_space=pltpu.SMEM), vmem]
+        + [pl.BlockSpec(memory_space=pl.ANY)] * 2
+        + [vmem] * (len(operands) - 3),
         out_specs=[vmem] * len(outs),
-        compiler_params=pltpu.CompilerParams(vmem_limit_bytes=12 * 1024 * 1024),
+        scratch_shapes=[pltpu.VMEM((n, n), bf16)] * 2 + [pltpu.SemaphoreType.DMA((2 * (n // count),))],
+        compiler_params=pltpu.CompilerParams(vmem_limit_bytes=52 * 1024 * 1024),
         cost_estimate=pl.CostEstimate(flops=10**8, bytes_accessed=5 * 2**20, transcendentals=0),
     )(parity, *operands)
 
@@ -309,16 +407,17 @@
     chips = n_dp // 2
     core = (lax.axis_index("dp") % 2).astype(jnp.int32).reshape(1)
     mine_proj = lax.all_to_all(
-        jnp.broadcast_to(projections[None], (chips,) + projections.shape),
+        repeat(projections, chips),
         "dp",
         0,
         0,
         axis_index_groups=[[2 * z + c for z in range(chips)] for c in range(2)],
     )
-    inv_high, inv_low, made = coarse_inverse(coarse_factor)
-    mine_proj, made = lax.optimization_barrier((mine_proj, made))
+    factor_high, factor_low, core = coarse_factor_inverse(core, coarse_factor)
+    mine_proj, core = lax.optimization_barrier((mine_proj, core))
     other_proj = lax.ppermute(mine_proj, "dp", [(i, i ^ 1) for i in range(n_dp)])
-    feat, part = make_features(core, samples, mine_proj, other_proj, targets.T, n_dp, made)
+    feat, part = make_features(core, samples, mine_proj, other_proj, targets.T, n_dp)
+    inv_high, inv_low = coarse_inverse(factor_high, factor_low)
 
     def scatter_dp(value):
         return jnp.sum(lax.all_to_all(value, "dp", 0, 0), 0)
@@ -364,14 +463,15 @@
     curve = row_sum(total[:, :n] * u.astype(f32)) + (RIDGE / n_dp) * row_sum(total[:, n:])
     got = gather_sk(jnp.concatenate([u, slots(curve)], 1)).reshape(width, n + SLOTS)
     image = dot(got[:, :n], feat)
-    curve = row_sum(got[:, n : n + 3].astype(f32))
-    sent = jnp.concatenate([image, jnp.broadcast_to(curve, (width, SLOTS))], 1)
-    total = scatter_dp(sent.reshape(n_dp, mine, count + SLOTS))
+    sent = jnp.concatenate([image.astype(bf16), got[:, n:]], 1)
+    got = lax.all_to_all(sent.reshape(n_dp, mine, count + SLOTS), "dp", 0, 0).astype(f32)
+    total = jnp.sum(got, 0)
     image = total[:, :count] + RIDGE * direction
-    alpha = dots[:, 1:2] / total[:, count : count + 1]
-    out = jnp.stack([answer + alpha * direction, resid - alpha * image])
+    alpha = dots[:, 1:2] / row_sum(total[:, count:])
+    out = jnp.stack([answer + alpha * direction, resid - alpha * image]).astype(bf16)
     got = lax.all_to_all(jnp.broadcast_to(out[None], (n_dp,) + out.shape), "dp", 0, 0)
-    return got[:, 0].reshape(width, count).T, got[:, 1].reshape(width, count).T
+    answer, resid = outputs(got)
+    return answer.T, resid.T
 
 
 def solution(mesh):

time: 232 us -> 262 us (1.13)
  Pallas kernels: 24.9 us -> 69.2 us
  blocking collectives: 146 us -> 133 us
  local copies, waits for them, and re-layouts: 12.3 us -> 2.05 us
  waiting for transfers between devices: 20.6 us -> 26.2 us
  starting transfers between devices: 22.9 us -> 26.6 us
    pallas_call x1 -> x4, Pallas kernels: 17 us -> 58.6 us  [the longest x1 32.9 us: repeat(): pl.pallas_call(copies_kernel, out_shape=jax.ShapeDtypeStruct((count,) + v...]
    all_to_all x3 -> x1, blocking collectives: 42.1 us -> 14.2 us  [scatter_dp(): return jnp.sum(lax.all_to_all(value, 'dp', 0, 0), 0)]
    all_to_all x1 -> x2, waiting for transfers between devices: 8.62 us -> 22.8 us  [the longest x1 13.6 us: body(): lax.all_to_all(repeat(projections, chips), 'dp', 0, 0, axis_index_groups=...]
    all_to_all x0 -> x1, blocking collectives: none -> 13.3 us  [body(): lax.all_to_all(sent.reshape(n_dp, mine, count + SLOTS), 'dp', 0, 0)]
    all_to_all x1, waiting for transfers between devices: 9.59 us -> 1.11 us  [gather_sk(): lax.all_to_all(jnp.broadcast_to(value[None], (n_sk,) + value.shape), 'ske...]
    unnamed x19 -> x8, local copies, waits for them, and re-layouts: 7.02 us -> 0.23 us
    all_to_all x1 -> x2, starting transfers between devices: 10.9 us -> 14.6 us  [the longest x1 10.9 us: body(): lax.all_to_all(repeat(projections, chips), 'dp', 0, 0, axis_index_groups=...]
    pallas_call x2, Pallas kernels: 2.1 us -> 5.37 us  [run_coarse(): pl.pallas_call(functools.partial(kernel, factor), out_shape=outs, in_spec...]
  transfers between devices with their start and end apart: 3 -> 4, of which waited for: 3 -> 4; matrix products, arithmetic and copies ran while one was open for 0% -> 0% of each run, Pallas kernels for 7% -> 9%
where the time goes in v3:
time: 262 us; the launch traced here: 261 us
  blocking collectives  133 us (51%)
  Pallas kernels  69.2 us (26%)
  starting transfers between devices  26.6 us (10%)
  waiting for transfers between devices  26.2 us (10%)
    all_to_all x3, blocking collectives, gather_sk(): lax.all_to_all(jnp.broadcast_to(value[None], (n_sk,) + value.shape), 'ske...  39.9 us
    pallas_call x1, Pallas kernels, repeat(): pl.pallas_call(copies_kernel, out_shape=jax.ShapeDtypeStruct((count,) + v...  32.9 us
    all_to_all x2, blocking collectives, forward(): whole = lax.all_to_all(send, 'dp', 0, 0).reshape(width, count)  24.1 us
    all_to_all x1, blocking collectives, body(): u = rounded(jnp.sum(lax.all_to_all(sums, 'sketch', 0, 0).astype(f32), 0))  15.9 us
    pallas_call x1, Pallas kernels, coarse_factor_inverse(): pl.pallas_call(inverse_kernel, out_shape=[jax.ShapeDtypeStruct((n, n), bf...  15.6 us
    all_to_all x1, blocking collectives, scatter_dp(): return jnp.sum(lax.all_to_all(value, 'dp', 0, 0), 0)  14.2 us
    all_to_all x1, waiting for transfers between devices, body(): lax.all_to_all(repeat(projections, chips), 'dp', 0, 0, axis_index_groups=...  13.6 us
    all_to_all x1, blocking collectives, body(): lax.all_to_all(sent.reshape(n_dp, mine, count + SLOTS), 'dp', 0, 0)  13.3 us
  transfers between devices with their start and end apart: 4, of which 4 were waited for; matrix products, arithmetic and copies ran while one was open for 0% of the time, Pallas kernels for 9%

profile of v3, /device:TPU:1, one launch (start us, length us, event | category | flops | bytes accessed | tf_op | source)
XLA Modules:
  0.0 261.0 jit_solution(3396758487954083885)
XLA Ops:
  0.6 32.9 %shard_map.68 = bf16[8,4,32,512]{3,2,1,0:T(8,128)(2,1)} custom-call(bf16[4,32,512]{2,1,0:T(8,128)(2,1)} %value_hbm.1), custom_call_target="tpu_custom_call" | custom-call | tf_op jit(solution)/shard_map/pallas_call | solution.py:146
  33.6 10.9 %all-to-all-start = ((bf16[8,4,32,512]{3,2,1,0:T(8,128)(2,1)}), bf16[8,4,32,512]{3,2,1,0:T(8,128)(2,1)S(1)}, u32[]{:S(2)}, u32[]{:S(2)}) async-start(bf16[8,4,32,512]{3,2,1,0:T(8,128)(2,1)} %shard_map.68), calls=%async_computation | async-start | bytes 2097152 | tf_op jit(solution)/shard_map/all_to_all | solution.py:409
  44.5 15.6 %shard_map.69 = (bf16[1024,1024]{1,0:T(8,128)(2,1)}, bf16[1024,1024]{1,0:T(8,128)(2,1)}, s32[1]{0:T(128)}) custom-call(s32[1]{0:T(128)} %bitcast.1.core_ref, bf16[1024,1024]{1,0:T(8,128)(2,1)} %lower_hbm.1), custom_call_target="tpu_custom_call" | custom-call | flops 10000000000 | bytes 6291456 | tf_op jit(solution)/shard_map/pallas_call | solution.py:98
  60.0 13.6 %all-to-all-done.mine_hbm = bf16[8,4,32,512]{3,2,1,0:T(8,128)(2,1)S(1)} async-done(((bf16[8,4,32,512]{3,2,1,0:T(8,128)(2,1)}), bf16[8,4,32,512]{3,2,1,0:T(8,128)(2,1)S(1)}, u32[]{:S(2)}, u32[]{:S(2)}) %all-to-all-start) | async-done | bytes 1048608 | tf_op jit(solution)/shard_map/all_to_all | solution.py:409
  73.6 2.4 collective-permute-start
  76.0 2.3 collective-permute-done.other_hbm
  78.3 5.2 %shard_map.70 = (bf16[1024,512]{1,0:T(8,128)(2,1)S(1)}, f32[16,4,512]{2,1,0:T(4,128)}) custom-call(s32[1]{0:T(128)} %get-tuple-element.23.core_ref, bf16[1024,512]{1,0:T(8,128)(2,1)S(1)} %copy-done.1, bf16[8,4,32,512]{3,2,1,0:T(8,128)(2,1)S(1)} %all-to-all-done.mine_hbm, bf16[8,4,32,512]{3,2,1,0:T(8,128)(2,1)S(1)} %collective-permute-done.other_hbm, ...), custom_call_target="tpu_custom_call" | custom-call | flops 2000000000 | bytes 5242880 | tf_op jit(solution)/shard_map/pallas_call | solution.py:219
  83.5 3.7 %all-to-all-start.1 = ((f32[16,4,512]{2,1,0:T(4,128)}), f32[16,4,512]{2,1,0:T(4,128)S(1)}, u32[]{:S(2)}, u32[]{:S(2)}) async-start(f32[16,4,512]{2,1,0:T(4,128)} %get-tuple-element.25), calls=%async_computation.1 | async-start | bytes 262144 | tf_op jit(solution)/shard_map/all_to_all | solution.py:423
  87.2 9.2 %all-to-all-done.1 = f32[16,4,512]{2,1,0:T(4,128)S(1)} async-done(((f32[16,4,512]{2,1,0:T(4,128)}), f32[16,4,512]{2,1,0:T(4,128)S(1)}, u32[]{:S(2)}, u32[]{:S(2)}) %all-to-all-start.1) | async-done | bytes 131104 | tf_op jit(solution)/shard_map/all_to_all | solution.py:423
  97.5 9.7 %all-to-all-start.2 = ((bf16[32,4,640]{2,1,0:T(4,128)(2,1)}), bf16[32,4,640]{2,1,0:T(4,128)(2,1)S(1)}, u32[]{:S(2)}, u32[]{:S(2)}) async-start(bf16[32,4,640]{2,1,0:T(4,128)(2,1)} %broadcast_in_dim.16), calls=%async_computation.2 | async-start | bytes 327680 | tf_op jit(solution)/shard_map/all_to_all | solution.py:426
  107.2 8.5 %shard_map.71 = (bf16[1024,1024]{1,0:T(8,128)(2,1)}, bf16[1024,1024]{1,0:T(8,128)(2,1)}) custom-call(bf16[1024,1024]{1,0:T(8,128)(2,1)} %get-tuple-element.26.xh_ref, bf16[1024,1024]{1,0:T(8,128)(2,1)} %get-tuple-element.27.xl_ref), custom_call_target="tpu_custom_call" | custom-call | flops 4000000000 | bytes 8388608 | tf_op jit(solution)/shard_map/pallas_call | solution.py:127
  116.8 2.5 shard_map.72
  119.4 12.2 %all_to_all.65 = bf16[16,4,512]{2,1,0:T(4,128)(2,1)S(1)} all-to-all(bf16[16,4,512]{2,1,0:T(4,128)(2,1)S(1)} %get-tuple-element.30), channel_id=1, replica_groups=mesh['dp'=16,'sketch'=32] {'dp'}, dimensions={0} | all-to-all | bytes 131072 | tf_op jit(solution)/shard_map/all_to_all | solution.py:432
  132.0 15.9 %all_to_all.66 = bf16[32,2,1024]{2,1,0:T(2,128)(2,1)S(1)} all-to-all(bf16[32,2,1024]{2,1,0:T(2,128)(2,1)S(1)} %reshape.423), channel_id=1, replica_groups=mesh['dp'=16,'sketch'=32] {'sketch'}, dimensions={0} | all-to-all | bytes 262144 | tf_op jit(solution)/shard_map/all_to_all | solution.py:444
  148.1 13.4 %all_to_all.67 = bf16[32,2,1024]{2,1,0:T(2,128)(2,1)S(1)} all-to-all(bf16[32,2,1024]{2,1,0:T(2,128)(2,1)S(1)} %broadcast_in_dim.18), channel_id=1, replica_groups=mesh['dp'=16,'sketch'=32] {'sketch'}, dimensions={0} | all-to-all | bytes 262144 | tf_op jit(solution)/shard_map/all_to_all | solution.py:426
  161.9 14.2 %all_to_all.68 = f32[16,4,512]{2,1,0:T(4,128)S(1)} all-to-all(f32[16,4,512]{2,1,0:T(4,128)S(1)} %copy.34), channel_id=1, replica_groups=mesh['dp'=16,'sketch'=32] {'dp'}, dimensions={0} | all-to-all | bytes 262144 | tf_op jit(solution)/shard_map/all_to_all | solution.py:423
  176.6 12.8 %all_to_all.69.got_ref = bf16[32,4,640]{2,1,0:T(4,128)(2,1)S(1)} all-to-all(bf16[32,4,640]{2,1,0:T(4,128)(2,1)S(1)} %broadcast_in_dim.19), channel_id=1, replica_groups=mesh['dp'=16,'sketch'=32] {'sketch'}, dimensions={0} | all-to-all | bytes 327680 | tf_op jit(solution)/shard_map/all_to_all | solution.py:426
  189.4 2.8 %shard_map.73 = (f32[4,512]{1,0:T(4,128)S(1)}, bf16[16,4,512]{2,1,0:T(4,128)(2,1)S(1)}, f32[4,1024]{1,0:T(4,128)}, f32[4,128]{1,0:T(4,128)S(1)}, f32[4,512]{1,0:T(4,128)S(1)}, /*index=5*/f32[4,512]{1,0:T(4,128)S(1)}) custom-call(s32[1]{0:T(128)} %bitcast.parity_ref, bf16[32,4,640]{2,1,0:T(4,128)(2,1)S(1)} %all_to_all.69.got_ref, ...), custom_call_target="tpu_custom_call" | custom-call | flops 100000000 | bytes 5242880 | tf_op jit(solution)/shard_map/pallas_call | solution.py:366
  192.3 12.0 %all_to_all.70 = bf16[16,4,512]{2,1,0:T(4,128)(2,1)S(1)} all-to-all(bf16[16,4,512]{2,1,0:T(4,128)(2,1)S(1)} %get-tuple-element.37), channel_id=1, replica_groups=mesh['dp'=16,'sketch'=32] {'dp'}, dimensions={0} | all-to-all | bytes 131072 | tf_op jit(solution)/shard_map/all_to_all | solution.py:432
  205.3 13.1 %all_to_all.71 = bf16[32,2,1152]{2,1,0:T(2,128)(2,1)S(1)} all-to-all(bf16[32,2,1152]{2,1,0:T(2,128)(2,1)S(1)} %fusion.2), channel_id=1, replica_groups=mesh['dp'=16,'sketch'=32] {'sketch'}, dimensions={0} | all-to-all | bytes 294912 | tf_op jit(solution)/shard_map/all_to_all | solution.py:460
  219.0 13.8 %all_to_all.72 = bf16[32,2,1152]{2,1,0:T(2,128)(2,1)S(1)} all-to-all(bf16[32,2,1152]{2,1,0:T(2,128)(2,1)S(1)} %broadcast_in_dim.21), channel_id=1, replica_groups=mesh['dp'=16,'sketch'=32] {'sketch'}, dimensions={0} | all-to-all | bytes 294912 | tf_op jit(solution)/shard_map/all_to_all | solution.py:426
  233.2 13.3 %all_to_all.73 = bf16[16,4,640]{2,1,0:T(4,128)(2,1)S(1)} all-to-all(bf16[16,4,640]{2,1,0:T(4,128)(2,1)S(1)} %reshape.428), channel_id=1, replica_groups=mesh['dp'=16,'sketch'=32] {'dp'}, dimensions={0} | all-to-all | bytes 163840 | tf_op jit(solution)/shard_map/all_to_all | solution.py:467
  247.0 12.3 %all_to_all.74.got_ref = bf16[16,2,4,512]{3,2,1,0:T(4,128)(2,1)} all-to-all(bf16[16,2,4,512]{3,2,1,0:T(4,128)(2,1)S(1)} %broadcast_in_dim.23), channel_id=1, replica_groups=mesh['dp'=16,'sketch'=32] {'dp'}, dimensions={0} | all-to-all | bytes 262144 | tf_op jit(solution)/shard_map/all_to_all | solution.py:472
  259.4 1.6 shard_map.74
  (64 shorter events, 6.4 us)
Async XLA Ops:
  33.6 40.1 %all-to-all-start = ((bf16[8,4,32,512]{3,2,1,0:T(8,128)(2,1)}), bf16[8,4,32,512]{3,2,1,0:T(8,128)(2,1)S(1)}, u32[]{:S(2)}, u32[]{:S(2)}) async-start(bf16[8,4,32,512]{3,2,1,0:T(8,128)(2,1)} %shard_map.68), calls=%async_computation | async-start | bytes 2097152 | tf_op jit(solution)/shard_map/all_to_all | solution.py:409
  44.5 33.9 %copy-start.1 = (bf16[1024,512]{1,0:T(8,128)(2,1)S(1)}, bf16[1024,512]{1,0:T(8,128)(2,1)}, u32[]{:S(2)}) copy-start(bf16[1024,512]{1,0:T(8,128)(2,1)} %samples_hbm.1) | copy-start | bytes 3145732
  44.5 33.9 %copy-start.2 = (bf16[1024,64]{0,1:T(8,128)(2,1)S(1)}, bf16[1024,64]{0,1:T(8,128)(2,1)}, u32[]{:S(2)}) copy-start(bf16[1024,64]{0,1:T(8,128)(2,1)} %param.7) | copy-start | bytes 393220
  73.6 4.7 %collective-permute-start = (bf16[8,4,32,512]{3,2,1,0:T(8,128)(2,1)S(1)}, bf16[8,4,32,512]{3,2,1,0:T(8,128)(2,1)S(1)}, u32[]{:S(2)}, u32[]{:S(2)}) collective-permute-start(bf16[8,4,32,512]{3,2,1,0:T(8,128)(2,1)S(1)} %all-to-all-done.mine_hbm), channel_id=1, source_target_pairs={{0,32},{32,0},{64,96},{96,64},{128,160},{160,128},{192,224},{224,1... | collective-permute-start | bytes 3145736 | tf_op jit(solution)/shard_map/ppermute | solution.py:418
  78.3 18.2 %copy-start = (f32[512]{0:T(512)S(1)}, f32[512]{0:T(512)}, u32[]{:S(2)}) copy-start(f32[512]{0:T(512)} %param.8) | copy-start | bytes 6148
  83.5 12.9 %all-to-all-start.1 = ((f32[16,4,512]{2,1,0:T(4,128)}), f32[16,4,512]{2,1,0:T(4,128)S(1)}, u32[]{:S(2)}, u32[]{:S(2)}) async-start(f32[16,4,512]{2,1,0:T(4,128)} %get-tuple-element.25), calls=%async_computation.1 | async-start | bytes 262144 | tf_op jit(solution)/shard_map/all_to_all | solution.py:423
  97.5 19.3 %all-to-all-start.2 = ((bf16[32,4,640]{2,1,0:T(4,128)(2,1)}), bf16[32,4,640]{2,1,0:T(4,128)(2,1)S(1)}, u32[]{:S(2)}, u32[]{:S(2)}) async-start(bf16[32,4,640]{2,1,0:T(4,128)(2,1)} %broadcast_in_dim.16), calls=%async_computation.2 | async-start | bytes 327680 | tf_op jit(solution)/shard_map/all_to_all | solution.py:426

commit v4 on v3

--- a/solution.py
+++ b/solution.py
@@ -45,22 +45,15 @@
 BLOCK = 256
 
 
-def inverse_kernel(core_ref, lower_hbm, high_ref, low_ref, made_ref, lower, inv, sems):
-    n = lower.shape[0]
-    blocks = n // BLOCK
-    spans = [pl.ds(b * BLOCK, BLOCK) for b in range(blocks)]
-    parts = [(span, span) for span in spans]
-    size = BLOCK
-    while size < n:
-        parts += [(pl.ds(at + size, size), pl.ds(at, size)) for at in range(0, n, 2 * size)]
-        size *= 2
+def blocks_kernel(order_ref, lower_hbm, inv_ref, lower, sems):
+    del order_ref
+    n = lower_hbm.shape[0]
+    spans = [pl.ds(b * BLOCK, BLOCK) for b in range(n // BLOCK)]
     copies = [
-        pltpu.make_async_copy(lower_hbm.at[part], lower.at[part], sems.at[k]) for k, part in enumerate(parts)
+        pltpu.make_async_copy(lower_hbm.at[span, span], lower.at[span], sems.at[b]) for b, span in enumerate(spans)
     ]
     for copy in copies:
         copy.start()
-    made_ref[0] = core_ref[0]
-    inv[...] = jnp.zeros_like(inv)
     rows = lax.broadcasted_iota(jnp.int32, (BLOCK, BLOCK), 0)
     cols = lax.broadcasted_iota(jnp.int32, (BLOCK, BLOCK), 1)
 
@@ -69,86 +62,99 @@
 
     for copy, span in zip(copies, spans):
         copy.wait()
-        block = lower[span, span].astype(f32)
+        block = lower[span, :].astype(f32)
         diag = jnp.where(rows == cols, block, 0.0)
         down = 1.0 / jnp.sum(diag, axis=1, keepdims=True)
         across = 1.0 / jnp.sum(diag, axis=0, keepdims=True)
-        inv[span, span] = jnp.where(rows == cols, down, jnp.where(below(0), -(block * down) * across, 0.0))
+        inv_ref[span, :] = jnp.where(rows == cols, down, jnp.where(below(0), -(block * down) * across, 0.0))
 
     def level(k, carry):
         mask = below(k)
         for span in spans:
-            x = inv[span, span]
-            off = jnp.where(mask, lower[span, span].astype(f32), 0.0).astype(bf16)
-            inv[span, span] = x - dot3(dot2_left(x, off), x)
+            x = inv_ref[span, :]
+            off = jnp.where(mask, lower[span, :].astype(f32), 0.0).astype(bf16)
+            inv_ref[span, :] = x - dot3(dot2_left(x, off), x)
         return carry
 
     lax.fori_loop(1, int(math.log2(BLOCK)), level, 0)
-    for copy, (bottom, top) in list(zip(copies, parts))[blocks:]:
+
+
+def block_inverses(order, lower):
+    n = lower.shape[0]
+    return pl.pallas_call(
+        blocks_kernel,
+        out_shape=jax.ShapeDtypeStruct((n, BLOCK), f32),
+        in_specs=[pl.BlockSpec(memory_space=pltpu.SMEM), pl.BlockSpec(memory_space=pl.ANY)],
+        out_specs=pl.BlockSpec(memory_space=pltpu.VMEM),
+        scratch_shapes=[pltpu.VMEM((n, BLOCK), bf16), pltpu.SemaphoreType.DMA((n // BLOCK,))],
+        compiler_params=pltpu.CompilerParams(vmem_limit_bytes=52 * 1024 * 1024),
+        cost_estimate=pl.CostEstimate(flops=10**10, bytes_accessed=2 * 2**20, transcendentals=0),
+    )(order, lower)
+
+
+def product_kernel(blocks_ref, lower_hbm, order_hbm, high_ref, low_ref, lower, inv, sems):
+    del order_hbm
+    n = lower.shape[0]
+    size, joins = BLOCK, []
+    while size < n:
+        joins += [(pl.ds(at + size, size), pl.ds(at, size)) for at in range(0, n, 2 * size)]
+        size *= 2
+    copies = [
+        pltpu.make_async_copy(lower_hbm.at[part], lower.at[part], sems.at[k]) for k, part in enumerate(joins)
+    ]
+    for copy in copies:
+        copy.start()
+    spans = [slice(b, b + BLOCK) for b in range(0, n, BLOCK)]
+    inv[...] = jnp.zeros_like(inv)
+    for span in spans:
+        inv[span, span] = blocks_ref[span, :]
+    for copy, (bottom, top) in zip(copies, joins):
         copy.wait()
         a, b = inv[top, top], inv[bottom, bottom]
         inv[bottom, top] = -dot3(b, dot2_right(lower[bottom, top], a))
-    for span in spans:
-        high_ref[span, :], low_ref[span, :] = split(inv[span, :])
-
-
-def coarse_factor_inverse(core, lower):
+    parts = [[split(inv[row, col]) for col in spans[: r + 1]] for r, row in enumerate(spans)]
+    turned = [[tuple(half.astype(f32).T.astype(bf16) for half in part) for part in row] for row in parts]
+    for a, row in enumerate(spans):
+        for b, col in enumerate(spans):
+            total = None
+            for k in range(max(a, b), len(spans)):
+                (ah, al), (bh, bl) = turned[k][a], parts[k][b]
+                term = dot(ah, bh) + (dot(ah, bl) + dot(al, bh))
+                total = term if total is None else total + term
+            high_ref[row, col], low_ref[row, col] = split(total)
+
+
+def coarse_inverse(blocks, lower, order):
     n = lower.shape[0]
-    vmem = pl.BlockSpec(memory_space=pltpu.VMEM)
-    return pl.pallas_call(
-        inverse_kernel,
-        out_shape=[jax.ShapeDtypeStruct((n, n), bf16)] * 2 + [jax.ShapeDtypeStruct((1,), jnp.int32)],
-        in_specs=[pl.BlockSpec(memory_space=pltpu.SMEM), pl.BlockSpec(memory_space=pl.ANY)],
-        out_specs=[vmem] * 2 + [pl.BlockSpec(memory_space=pltpu.SMEM)],
+    vmem, anywhere = pl.BlockSpec(memory_space=pltpu.VMEM), pl.BlockSpec(memory_space=pl.ANY)
+    return pl.pallas_call(
+        product_kernel,
+        out_shape=[jax.ShapeDtypeStruct((n, n), bf16)] * 2,
+        in_specs=[vmem, anywhere, anywhere],
+        out_specs=[vmem] * 2,
         scratch_shapes=[
             pltpu.VMEM((n, n), bf16),
             pltpu.VMEM((n, n), f32),
-            pltpu.SemaphoreType.DMA((2 * (n // BLOCK) - 1,)),
+            pltpu.SemaphoreType.DMA((n // BLOCK - 1,)),
         ],
-        compiler_params=pltpu.CompilerParams(vmem_limit_bytes=56 * 1024 * 1024),
-        cost_estimate=pl.CostEstimate(flops=10**10, bytes_accessed=6 * 2**20, transcendentals=0),
-    )(core, lower)
-
-
-def product_kernel(xh_ref, xl_ref, high_ref, low_ref):
-    n = xh_ref.shape[0]
-    xht = xh_ref[...].astype(f32).T.astype(bf16)
-    xlt = xl_ref[...].astype(f32).T.astype(bf16)
-    for start in range(0, n, BLOCK):
-        at, cols = slice(start, n), slice(start, start + BLOCK)
-        xh, xl = xh_ref[at, cols], xl_ref[at, cols]
-        m = dot(xht[:, at], xh) + (dot(xht[:, at], xl) + dot(xlt[:, at], xh))
-        high_ref[:, cols], low_ref[:, cols] = split(m)
-
-
-def coarse_inverse(xh, xl):
-    n = xh.shape[0]
+        compiler_params=pltpu.CompilerParams(vmem_limit_bytes=50 * 1024 * 1024),
+        cost_estimate=pl.CostEstimate(flops=10**10, bytes_accessed=8 * 2**20, transcendentals=0),
+    )(blocks, lower, order)
+
+
+def repeat_kernel(value_ref, out_ref):
+    for p in range(out_ref.shape[0]):
+        out_ref[p] = value_ref[...]
+
+
+def repeat(value, count):
     vmem = pl.BlockSpec(memory_space=pltpu.VMEM)
     return pl.pallas_call(
-        product_kernel,
-        out_shape=[jax.ShapeDtypeStruct((n, n), bf16)] * 2,
-        in_specs=[vmem] * 2,
-        out_specs=[vmem] * 2,
-        compiler_params=pltpu.CompilerParams(vmem_limit_bytes=56 * 1024 * 1024),
-        cost_estimate=pl.CostEstimate(flops=4 * 10**9, bytes_accessed=8 * 2**20, transcendentals=0),
-    )(xh, xl)
-
-
-def copies_kernel(value_hbm, out_hbm, sems):
-    copies = [pltpu.make_async_copy(value_hbm, out_hbm.at[p], sems.at[p]) for p in range(out_hbm.shape[0])]
-    for copy in copies:
-        copy.start()
-    for copy in copies:
-        copy.wait()
-
-
-def repeat(value, count):
-    return pl.pallas_call(
-        copies_kernel,
+        repeat_kernel,
         out_shape=jax.ShapeDtypeStruct((count,) + value.shape, value.dtype),
-        in_specs=[pl.BlockSpec(memory_space=pl.ANY)],
-        out_specs=pl.BlockSpec(memory_space=pl.ANY),
-        scratch_shapes=[pltpu.SemaphoreType.DMA((count,))],
+        in_specs=[vmem],
+        out_specs=vmem,
+        compiler_params=pltpu.CompilerParams(vmem_limit_bytes=8 * 1024 * 1024),
     )(value)
 
 
@@ -174,10 +180,11 @@
 
 
 def feature_kernel(
-    core_ref, samples_hbm, mine_hbm, other_hbm, targets_hbm, feat_ref, part_ref, samples, proj, targets, acc, sems
+    core_ref, samples_hbm, mine_hbm, other_hbm, targets_hbm, feat_ref, part_ref, order_ref, samples, proj, targets, acc, sems
 ):
     n, parts, panels = samples.shape[0], part_ref.shape[0], proj.shape[0]
     core = core_ref[0]
+    order_ref[0] = core
     get_samples = pltpu.make_async_copy(samples_hbm, samples, sems.at[0])
     get_targets = pltpu.make_async_copy(targets_hbm, targets, sems.at[1])
     get_proj = [
@@ -221,9 +228,10 @@
         out_shape=[
             jax.ShapeDtypeStruct((n, width), bf16),
             jax.ShapeDtypeStruct((parts, targets_t.shape[0] // parts, width), f32),
+            jax.ShapeDtypeStruct((1,), jnp.int32),
         ],
         in_specs=[pl.BlockSpec(memory_space=pltpu.SMEM)] + [pl.BlockSpec(memory_space=pl.ANY)] * 4,
-        out_specs=[pl.BlockSpec(memory_space=pltpu.VMEM)] * 2,
+        out_specs=[pl.BlockSpec(memory_space=pltpu.VMEM)] * 2 + [pl.BlockSpec(memory_space=pltpu.SMEM)],
         scratch_shapes=[
             pltpu.VMEM(samples.shape, bf16),
             pltpu.VMEM((panels, chips, 2, rows, width), bf16),
@@ -231,7 +239,7 @@
             pltpu.VMEM((n, width), f32),
             pltpu.SemaphoreType.DMA((2 + 2 * panels,)),
         ],
-        compiler_params=pltpu.CompilerParams(vmem_limit_bytes=48 * 1024 * 1024),
+        compiler_params=pltpu.CompilerParams(vmem_limit_bytes=50 * 1024 * 1024),
         cost_estimate=pl.CostEstimate(flops=2 * 10**9, bytes_accessed=5 * 2**20, transcendentals=0),
     )(core, samples, mine, other, targets_t)
 
@@ -263,32 +271,20 @@
     return parts, sums
 
 
-def fetch(high_hbm, low_hbm, high, low, sems, halves):
-    span = high.shape[0] // halves
-    copies = [
-        [
-            pltpu.make_async_copy(src.at[pl.ds(h * span, span)], dst.at[pl.ds(h * span, span)], sems.at[2 * h + k])
-            for k, (src, dst) in enumerate(((high_hbm, high), (low_hbm, low)))
-        ]
-        for h in range(halves)
-    ]
-    for copy in sum(copies, []):
-        copy.start()
-    return high, low, copies
-
-
 def coarse(parts, inverse):
-    high_ref, low_ref, copies = inverse
-    rows, total = parts[0].shape[0], None
+    high_ref, low_ref, copy = inverse
+    rows, total, left = parts[0].shape[0], None, []
     for h, part in enumerate(parts):
         span = slice(h * part.shape[1], (h + 1) * part.shape[1])
         high = part.astype(bf16).astype(f32)
         both = jnp.concatenate([high, part - high], 0).astype(bf16)
-        copies[h][0].wait()
         one = dot(both, high_ref[span, :])
-        copies[h][1].wait()
-        term = one[:rows] + one[rows:] + dot(both, low_ref[span, :])[:rows]
+        term = one[:rows] + one[rows:]
         total = term if total is None else total + term
+        left.append((span, both))
+    copy.wait()
+    for span, both in left:
+        total = total + dot(both, low_ref[span, :])[:rows]
     return total
 
 
@@ -306,10 +302,12 @@
 
 
 def first_kernel(
-    factor, parity_ref, got_ref, high_hbm, low_hbm, resid_ref, scale_ref, dir_ref, send_ref, rho_ref, dots_ref, high, low, sems
+    factor, parity_ref, got_ref, high_ref, low_hbm, resid_ref, scale_ref, dir_ref, send_ref, rho_ref, dots_ref, low, sem
 ):
     count = resid_ref.shape[1]
-    inverse = fetch(high_hbm, low_hbm, high, low, sems, rho_ref.shape[1] // count)
+    fetch = pltpu.make_async_copy(low_hbm, low, sem)
+    fetch.start()
+    inverse = high_ref, low, fetch
     parts, sums = gathered(got_ref, rho_ref.shape[1] // count, count)
     parts = [part * factor for part in parts]
     product, direction = next_direction(
@@ -325,11 +323,13 @@
 
 
 def step_kernel(
-    factor, parity_ref, got_ref, high_hbm, low_hbm, resid_ref, scale_ref, image_ref, old_ref, rho_ref, dots_ref, answer_ref,
-    dir_ref, send_ref, new_rho_ref, new_dots_ref, new_resid_ref, new_answer_ref, high, low, sems,
+    factor, parity_ref, got_ref, high_ref, low_hbm, resid_ref, scale_ref, image_ref, old_ref, rho_ref, dots_ref, answer_ref,
+    dir_ref, send_ref, new_rho_ref, new_dots_ref, new_resid_ref, new_answer_ref, low, sem,
 ):
     count = resid_ref.shape[1]
-    inverse = fetch(high_hbm, low_hbm, high, low, sems, rho_ref.shape[1] // count)
+    fetch = pltpu.make_async_copy(low_hbm, low, sem)
+    fetch.start()
+    inverse = high_ref, low, fetch
     parts, sums = gathered(got_ref, rho_ref.shape[1] // count, count)
     energy, product = lane(dots_ref[...], 0), lane(dots_ref[...], 1)
     alpha = product / sums[0]
@@ -366,12 +366,11 @@
     return pl.pallas_call(
         functools.partial(kernel, factor),
         out_shape=outs,
-        in_specs=[pl.BlockSpec(memory_space=pltpu.SMEM), vmem]
-        + [pl.BlockSpec(memory_space=pl.ANY)] * 2
+        in_specs=[pl.BlockSpec(memory_space=pltpu.SMEM), vmem, vmem, pl.BlockSpec(memory_space=pl.ANY)]
         + [vmem] * (len(operands) - 3),
         out_specs=[vmem] * len(outs),
-        scratch_shapes=[pltpu.VMEM((n, n), bf16)] * 2 + [pltpu.SemaphoreType.DMA((2 * (n // count),))],
-        compiler_params=pltpu.CompilerParams(vmem_limit_bytes=52 * 1024 * 1024),
+        scratch_shapes=[pltpu.VMEM((n, n), bf16), pltpu.SemaphoreType.DMA],
+        compiler_params=pltpu.CompilerParams(vmem_limit_bytes=50 * 1024 * 1024),
         cost_estimate=pl.CostEstimate(flops=10**8, bytes_accessed=5 * 2**20, transcendentals=0),
     )(parity, *operands)
 
@@ -413,11 +412,8 @@
         0,
         axis_index_groups=[[2 * z + c for z in range(chips)] for c in range(2)],
     )
-    factor_high, factor_low, core = coarse_factor_inverse(core, coarse_factor)
-    mine_proj, core = lax.optimization_barrier((mine_proj, core))
     other_proj = lax.ppermute(mine_proj, "dp", [(i, i ^ 1) for i in range(n_dp)])
-    feat, part = make_features(core, samples, mine_proj, other_proj, targets.T, n_dp)
-    inv_high, inv_low = coarse_inverse(factor_high, factor_low)
+    feat, part, order = make_features(core, samples, mine_proj, other_proj, targets.T, n_dp)
 
     def scatter_dp(value):
         return jnp.sum(lax.all_to_all(value, "dp", 0, 0), 0)
@@ -433,7 +429,9 @@
         sums = lax.dot_general(whole, feat, (((1,), (1,)), ((), ())), preferred_element_type=f32)
         return whole, sums.astype(bf16).reshape(n_sk, cols, n)
 
+    blocks = block_inverses(order, coarse_factor)
     resid = scatter_dp(part)
+    inv_high, inv_low = coarse_inverse(blocks, coarse_factor, resid)
     got = everywhere(resid, row_sum(scale * resid * resid))
     direction, send, rho, dots = run_coarse(
         first_kernel, factor, n_dp, parity, got, inv_high, inv_low, resid, scale

time: 262 us -> 238 us (0.908)
  blocking collectives: 133 us -> 176 us
  Pallas kernels: 69.2 us -> 30.9 us
  waiting for transfers between devices: 26.2 us -> 2.25 us
  starting transfers between devices: 26.6 us -> 17.7 us
  local copies, waits for them, and re-layouts: 2.05 us -> 6.13 us
    all_to_all x0 -> x1, blocking collectives: none -> 38 us  [body(): lax.all_to_all(repeat(projections, chips), 'dp', 0, 0, axis_index_groups=...]
    pallas_call x2, Pallas kernels: 48.5 us -> 10.9 us  [the longest x1 10.9 us: block_inverses(): pl.pallas_call(blocks_kernel, out_shape=jax.ShapeDtypeStruct((n, BLOCK),...]
    all_to_all x1 -> x0, waiting for transfers between devices: 13.6 us -> none  [body(): lax.all_to_all(repeat(projections, chips), 'dp', 0, 0, axis_index_groups=...]
    all_to_all x1 -> x0, starting transfers between devices: 10.9 us -> none  [body(): lax.all_to_all(repeat(projections, chips), 'dp', 0, 0, axis_index_groups=...]
    all_to_all x1, waiting for transfers between devices: 9.21 us -> 0.01 us  [scatter_dp(): return jnp.sum(lax.all_to_all(value, 'dp', 0, 0), 0)]
    all_to_all x2, blocking collectives: 24.1 us -> 28.8 us  [forward(): whole = lax.all_to_all(send, 'dp', 0, 0).reshape(width, count)]
    unnamed x8 -> x16, local copies, waits for them, and re-layouts: 0.23 us -> 4.32 us
  transfers between devices with their start and end apart: 4 -> 3, of which waited for: 4 -> 1; matrix products, arithmetic and copies ran while one was open for 0% -> 0% of each run, Pallas kernels for 9% -> 8%
where the time goes in v4:
time: 238 us
  blocking collectives  176 us (74%)
  Pallas kernels  30.9 us (13%)
  starting transfers between devices  17.7 us (7%)
  local copies, waits for them, and re-layouts  6.13 us (3%)
    all_to_all x3, blocking collectives, gather_sk(): lax.all_to_all(jnp.broadcast_to(value[None], (n_sk,) + value.shape), 'ske...  39.9 us
    all_to_all x1, blocking collectives, body(): lax.all_to_all(repeat(projections, chips), 'dp', 0, 0, axis_index_groups=...  38 us
    all_to_all x2, blocking collectives, forward(): whole = lax.all_to_all(send, 'dp', 0, 0).reshape(width, count)  28.8 us
    all_to_all x1, blocking collectives, body(): u = rounded(jnp.sum(lax.all_to_all(sums, 'sketch', 0, 0).astype(f32), 0))  16.8 us
    all_to_all x1, blocking collectives, scatter_dp(): return jnp.sum(lax.all_to_all(value, 'dp', 0, 0), 0)  14.2 us
    all_to_all x1, blocking collectives, body(): lax.all_to_all(sent.reshape(n_dp, mine, count + SLOTS), 'dp', 0, 0)  13.3 us
    all_to_all x1, blocking collectives, body(): lax.all_to_all(jnp.concatenate([sums, slots(squares)], 2), 'sketch', 0, 0)  13.1 us
    all_to_all x1, blocking collectives, body(): lax.all_to_all(jnp.broadcast_to(out[None], (n_dp,) + out.shape), 'dp', 0, 0)  12.3 us
  transfers between devices with their start and end apart: 3, of which 1 were waited for; matrix products, arithmetic and copies ran while one was open for 0% of the time, Pallas kernels for 8%

profile of v4, /device:TPU:1, one launch (start us, length us, event | category | flops | bytes accessed | tf_op | source)
XLA Modules:
  0.0 237.6 jit_solution(12790614545318318862)
XLA Ops:
  1.6 38.0 %all_to_all.65.mine_hbm = bf16[8,4,32,512]{3,2,1,0:T(8,128)(2,1)S(1)} all-to-all(bf16[8,4,32,512]{3,2,1,0:T(8,128)(2,1)S(1)} %shard_map.68), channel_id=1, replica_groups={{0,64,128,192,256,320,384,448},{32,96,160,224,288,352,416,480},{1,65,12..., dimensions={0} | all-to-all | bytes 2097152 | tf_op jit(solution)/shard_map/all_to_all | solution.py:408
  39.6 4.4 %collective-permute-start = (bf16[8,4,32,512]{3,2,1,0:T(8,128)(2,1)S(1)}, bf16[8,4,32,512]{3,2,1,0:T(8,128)(2,1)S(1)}, u32[]{:S(2)}, u32[]{:S(2)}) collective-permute-start(bf16[8,4,32,512]{3,2,1,0:T(8,128)(2,1)S(1)} %all_to_all.65.mine_hbm), channel_id=1, source_target_pairs={{0,32},{32,0},{64,96},{96,64},{128,160},{160,128},{192,224},{224,1... | collective-permute-start | bytes 3145736 | tf_op jit(solution)/shard_map/ppermute | solution.py:415
  44.0 2.2 collective-permute-done.other_hbm
  46.3 1.0 copy-done.6
  47.3 5.2 %shard_map.69 = (bf16[1024,512]{1,0:T(8,128)(2,1)S(1)}, f32[16,4,512]{2,1,0:T(4,128)}, s32[1]{0:T(128)}) custom-call(s32[1]{0:T(128)} %bitcast.1.core_ref, bf16[1024,512]{1,0:T(8,128)(2,1)S(1)} %copy-done.2, bf16[8,4,32,512]{3,2,1,0:T(8,128)(2,1)S(1)} %all_to_all.65.mine_hbm, bf16[8,4,32,512]{3,2,1,0:T(8,128)(2,1)} %copy-done.6, bf16[64,1024]{1,0:T(8,128)(2,1)S(1)} %bitcast.34), custom_call_target="tpu_custom_call" | custom-call | flops 2000000000 | bytes 5242880 | tf_op jit(solution)/shard_map/pallas_call | solution.py:226
  52.5 3.7 %all-to-all-start.1 = ((f32[16,4,512]{2,1,0:T(4,128)}), f32[16,4,512]{2,1,0:T(4,128)S(1)}, u32[]{:S(2)}, u32[]{:S(2)}) async-start(f32[16,4,512]{2,1,0:T(4,128)} %get-tuple-element.18), calls=%async_computation.1 | async-start | bytes 262144 | tf_op jit(solution)/shard_map/all_to_all | solution.py:419
  56.2 10.9 %shard_map.70.blocks_ref = f32[1024,256]{1,0:T(8,128)S(1)} custom-call(s32[1]{0:T(128)} %get-tuple-element.19.order_ref, bf16[1024,1024]{1,0:T(8,128)(2,1)} %lower_hbm.3), custom_call_target="tpu_custom_call" | custom-call | flops 10000000000 | bytes 2097152 | tf_op jit(solution)/shard_map/pallas_call | solution.py:84
  67.1 1.0 copy-done.4
  69.1 9.7 %all-to-all-start.2 = ((bf16[32,4,640]{2,1,0:T(4,128)(2,1)}), bf16[32,4,640]{2,1,0:T(4,128)(2,1)S(1)}, u32[]{:S(2)}, u32[]{:S(2)}) async-start(bf16[32,4,640]{2,1,0:T(4,128)(2,1)} %broadcast_in_dim.16), calls=%async_computation.2 | async-start | bytes 327680 | tf_op jit(solution)/shard_map/all_to_all | solution.py:422
  78.8 1.2 copy-done.5
  80.0 8.2 %shard_map.71 = (bf16[1024,1024]{1,0:T(8,128)(2,1)S(1)}, bf16[1024,1024]{1,0:T(8,128)(2,1)}) custom-call(f32[1024,256]{1,0:T(8,128)S(1)} %copy-done.5, bf16[1024,1024]{1,0:T(8,128)(2,1)} %lower_hbm.3, f32[4,512]{1,0:T(4,128)S(1)} %reduce_sum.119.order_hbm.resid_ref), custom_call_target="tpu_custom_call" | custom-call | flops 10000000000 | bytes 8388608 | tf_op jit(solution)/shard_map/pallas_call | solution.py:130
  88.3 2.3 shard_map.72
  90.6 16.8 %all_to_all.66 = bf16[16,4,512]{2,1,0:T(4,128)(2,1)S(1)} all-to-all(bf16[16,4,512]{2,1,0:T(4,128)(2,1)S(1)} %get-tuple-element.22), channel_id=1, replica_groups=mesh['dp'=16,'sketch'=32] {'dp'}, dimensions={0} | all-to-all | bytes 131072 | tf_op jit(solution)/shard_map/all_to_all | solution.py:428
  107.9 16.8 %all_to_all.67 = bf16[32,2,1024]{2,1,0:T(2,128)(2,1)S(1)} all-to-all(bf16[32,2,1024]{2,1,0:T(2,128)(2,1)S(1)} %reshape.423), channel_id=1, replica_groups=mesh['dp'=16,'sketch'=32] {'sketch'}, dimensions={0} | all-to-all | bytes 262144 | tf_op jit(solution)/shard_map/all_to_all | solution.py:442
  124.9 13.4 %all_to_all.68 = bf16[32,2,1024]{2,1,0:T(2,128)(2,1)S(1)} all-to-all(bf16[32,2,1024]{2,1,0:T(2,128)(2,1)S(1)} %broadcast_in_dim.18), channel_id=1, replica_groups=mesh['dp'=16,'sketch'=32] {'sketch'}, dimensions={0} | all-to-all | bytes 262144 | tf_op jit(solution)/shard_map/all_to_all | solution.py:422
  138.8 14.2 %all_to_all.69 = f32[16,4,512]{2,1,0:T(4,128)S(1)} all-to-all(f32[16,4,512]{2,1,0:T(4,128)S(1)} %copy.34), channel_id=1, replica_groups=mesh['dp'=16,'sketch'=32] {'dp'}, dimensions={0} | all-to-all | bytes 262144 | tf_op jit(solution)/shard_map/all_to_all | solution.py:419
  153.4 12.8 %all_to_all.70.got_ref = bf16[32,4,640]{2,1,0:T(4,128)(2,1)S(1)} all-to-all(bf16[32,4,640]{2,1,0:T(4,128)(2,1)S(1)} %broadcast_in_dim.19), channel_id=1, replica_groups=mesh['dp'=16,'sketch'=32] {'sketch'}, dimensions={0} | all-to-all | bytes 327680 | tf_op jit(solution)/shard_map/all_to_all | solution.py:422
  166.3 2.6 %shard_map.73 = (f32[4,512]{1,0:T(4,128)S(1)}, bf16[16,4,512]{2,1,0:T(4,128)(2,1)S(1)}, f32[4,1024]{1,0:T(4,128)}, f32[4,128]{1,0:T(4,128)S(1)}, f32[4,512]{1,0:T(4,128)S(1)}, /*index=5*/f32[4,512]{1,0:T(4,128)S(1)}) custom-call(s32[1]{0:T(128)} %bitcast.parity_ref, bf16[32,4,640]{2,1,0:T(4,128)(2,1)S(1)} %all_to_all.70.got_ref, ...), custom_call_target="tpu_custom_call" | custom-call | flops 100000000 | bytes 5242880 | tf_op jit(solution)/shard_map/pallas_call | solution.py:366
  168.8 12.0 %all_to_all.71 = bf16[16,4,512]{2,1,0:T(4,128)(2,1)S(1)} all-to-all(bf16[16,4,512]{2,1,0:T(4,128)(2,1)S(1)} %get-tuple-element.29), channel_id=1, replica_groups=mesh['dp'=16,'sketch'=32] {'dp'}, dimensions={0} | all-to-all | bytes 131072 | tf_op jit(solution)/shard_map/all_to_all | solution.py:428
  181.9 13.1 %all_to_all.72 = bf16[32,2,1152]{2,1,0:T(2,128)(2,1)S(1)} all-to-all(bf16[32,2,1152]{2,1,0:T(2,128)(2,1)S(1)} %fusion.2), channel_id=1, replica_groups=mesh['dp'=16,'sketch'=32] {'sketch'}, dimensions={0} | all-to-all | bytes 294912 | tf_op jit(solution)/shard_map/all_to_all | solution.py:458
  195.6 13.8 %all_to_all.73 = bf16[32,2,1152]{2,1,0:T(2,128)(2,1)S(1)} all-to-all(bf16[32,2,1152]{2,1,0:T(2,128)(2,1)S(1)} %broadcast_in_dim.21), channel_id=1, replica_groups=mesh['dp'=16,'sketch'=32] {'sketch'}, dimensions={0} | all-to-all | bytes 294912 | tf_op jit(solution)/shard_map/all_to_all | solution.py:422
  209.7 13.3 %all_to_all.74 = bf16[16,4,640]{2,1,0:T(4,128)(2,1)S(1)} all-to-all(bf16[16,4,640]{2,1,0:T(4,128)(2,1)S(1)} %reshape.428), channel_id=1, replica_groups=mesh['dp'=16,'sketch'=32] {'dp'}, dimensions={0} | all-to-all | bytes 163840 | tf_op jit(solution)/shard_map/all_to_all | solution.py:465
  223.6 12.3 %all_to_all.75.got_ref = bf16[16,2,4,512]{3,2,1,0:T(4,128)(2,1)} all-to-all(bf16[16,2,4,512]{3,2,1,0:T(4,128)(2,1)S(1)} %broadcast_in_dim.23), channel_id=1, replica_groups=mesh['dp'=16,'sketch'=32] {'dp'}, dimensions={0} | all-to-all | bytes 262144 | tf_op jit(solution)/shard_map/all_to_all | solution.py:470
  235.9 1.6 shard_map.74
  (71 shorter events, 6.2 us)
Async XLA Ops:
  0.6 0.9 copy-start
  1.5 45.7 %copy-start.2 = (bf16[1024,512]{1,0:T(8,128)(2,1)S(1)}, bf16[1024,512]{1,0:T(8,128)(2,1)}, u32[]{:S(2)}) copy-start(bf16[1024,512]{1,0:T(8,128)(2,1)} %samples_hbm.1) | copy-start | bytes 3145732
  1.5 45.7 %copy-start.3 = (bf16[1024,64]{0,1:T(8,128)(2,1)S(1)}, bf16[1024,64]{0,1:T(8,128)(2,1)}, u32[]{:S(2)}) copy-start(bf16[1024,64]{0,1:T(8,128)(2,1)} %param.7) | copy-start | bytes 393220
  39.6 6.6 %collective-permute-start = (bf16[8,4,32,512]{3,2,1,0:T(8,128)(2,1)S(1)}, bf16[8,4,32,512]{3,2,1,0:T(8,128)(2,1)S(1)}, u32[]{:S(2)}, u32[]{:S(2)}) collective-permute-start(bf16[8,4,32,512]{3,2,1,0:T(8,128)(2,1)S(1)} %all_to_all.65.mine_hbm), channel_id=1, source_target_pairs={{0,32},{32,0},{64,96},{96,64},{128,160},{160,128},{192,224},{224,1... | collective-permute-start | bytes 3145736 | tf_op jit(solution)/shard_map/ppermute | solution.py:415
  46.3 1.0 copy-start.6
  52.5 15.6 %all-to-all-start.1 = ((f32[16,4,512]{2,1,0:T(4,128)}), f32[16,4,512]{2,1,0:T(4,128)S(1)}, u32[]{:S(2)}, u32[]{:S(2)}) async-start(f32[16,4,512]{2,1,0:T(4,128)} %get-tuple-element.18), calls=%async_computation.1 | async-start | bytes 262144 | tf_op jit(solution)/shard_map/all_to_all | solution.py:419
  56.2 11.9 %copy-start.1 = (f32[512]{0:T(512)S(1)}, f32[512]{0:T(512)}, u32[]{:S(2)}) copy-start(f32[512]{0:T(512)} %param.8) | copy-start | bytes 6148
  67.1 1.0 copy-start.4
  69.1 19.1 %all-to-all-start.2 = ((bf16[32,4,640]{2,1,0:T(4,128)(2,1)}), bf16[32,4,640]{2,1,0:T(4,128)(2,1)S(1)}, u32[]{:S(2)}, u32[]{:S(2)}) async-start(bf16[32,4,640]{2,1,0:T(4,128)(2,1)} %broadcast_in_dim.16), calls=%async_computation.2 | async-start | bytes 327680 | tf_op jit(solution)/shard_map/all_to_all | solution.py:422
  78.8 1.2 copy-start.5

commit v5 on v3

--- a/solution.py
+++ b/solution.py
@@ -43,6 +43,7 @@
 
 
 BLOCK = 256
+DP = ("z", "core")
 
 
 def inverse_kernel(core_ref, lower_hbm, high_ref, low_ref, made_ref, lower, inv, sems):
@@ -110,45 +111,47 @@
     )(core, lower)
 
 
-def product_kernel(xh_ref, xl_ref, high_ref, low_ref):
-    n = xh_ref.shape[0]
-    xht = xh_ref[...].astype(f32).T.astype(bf16)
-    xlt = xl_ref[...].astype(f32).T.astype(bf16)
-    for start in range(0, n, BLOCK):
-        at, cols = slice(start, n), slice(start, start + BLOCK)
-        xh, xl = xh_ref[at, cols], xl_ref[at, cols]
-        m = dot(xht[:, at], xh) + (dot(xht[:, at], xl) + dot(xlt[:, at], xh))
-        high_ref[:, cols], low_ref[:, cols] = split(m)
-
-
-def coarse_inverse(xh, xl):
+def product_kernel(xh_ref, xl_ref, order_hbm, high_ref, low_ref):
+    del order_hbm
+    spans = [slice(b, b + BLOCK) for b in range(0, xh_ref.shape[0], BLOCK)]
+    parts = [[(xh_ref[row, col], xl_ref[row, col]) for col in spans[: r + 1]] for r, row in enumerate(spans)]
+    turned = [[tuple(half.astype(f32).T.astype(bf16) for half in part) for part in row] for row in parts]
+    for a, row in enumerate(spans):
+        for b, col in enumerate(spans):
+            total = None
+            for k in range(max(a, b), len(spans)):
+                (ah, al), (bh, bl) = turned[k][a], parts[k][b]
+                term = dot(ah, bh) + (dot(ah, bl) + dot(al, bh))
+                total = term if total is None else total + term
+            high_ref[row, col], low_ref[row, col] = split(total)
+
+
+def coarse_inverse(xh, xl, order):
     n = xh.shape[0]
     vmem = pl.BlockSpec(memory_space=pltpu.VMEM)
     return pl.pallas_call(
         product_kernel,
         out_shape=[jax.ShapeDtypeStruct((n, n), bf16)] * 2,
-        in_specs=[vmem] * 2,
+        in_specs=[vmem, vmem, pl.BlockSpec(memory_space=pl.ANY)],
         out_specs=[vmem] * 2,
-        compiler_params=pltpu.CompilerParams(vmem_limit_bytes=56 * 1024 * 1024),
+        compiler_params=pltpu.CompilerParams(vmem_limit_bytes=50 * 1024 * 1024),
         cost_estimate=pl.CostEstimate(flops=4 * 10**9, bytes_accessed=8 * 2**20, transcendentals=0),
-    )(xh, xl)
-
-
-def copies_kernel(value_hbm, out_hbm, sems):
-    copies = [pltpu.make_async_copy(value_hbm, out_hbm.at[p], sems.at[p]) for p in range(out_hbm.shape[0])]
-    for copy in copies:
-        copy.start()
-    for copy in copies:
-        copy.wait()
+    )(xh, xl, order)
+
+
+def repeat_kernel(value_ref, out_ref):
+    for p in range(out_ref.shape[0]):
+        out_ref[p] = value_ref[...]
 
 
 def repeat(value, count):
-    return pl.pallas_call(
-        copies_kernel,
+    vmem = pl.BlockSpec(memory_space=pltpu.VMEM)
+    return pl.pallas_call(
+        repeat_kernel,
         out_shape=jax.ShapeDtypeStruct((count,) + value.shape, value.dtype),
-        in_specs=[pl.BlockSpec(memory_space=pl.ANY)],
-        out_specs=pl.BlockSpec(memory_space=pl.ANY),
-        scratch_shapes=[pltpu.SemaphoreType.DMA((count,))],
+        in_specs=[vmem],
+        out_specs=vmem,
+        compiler_params=pltpu.CompilerParams(vmem_limit_bytes=8 * 1024 * 1024),
     )(value)
 
 
@@ -170,14 +173,14 @@
     )(got)
 
 
-ROWS = 256
+ROWS = 1024
 
 
 def feature_kernel(
     core_ref, samples_hbm, mine_hbm, other_hbm, targets_hbm, feat_ref, part_ref, samples, proj, targets, acc, sems
 ):
     n, parts, panels = samples.shape[0], part_ref.shape[0], proj.shape[0]
-    core = core_ref[0]
+    core, rows = core_ref[0], min(ROWS, n)
     get_samples = pltpu.make_async_copy(samples_hbm, samples, sems.at[0])
     get_targets = pltpu.make_async_copy(targets_hbm, targets, sems.at[1])
     get_proj = [
@@ -197,16 +200,16 @@
         panel = proj[j].reshape(samples.shape[1], proj.shape[-1])
         if j == panels - 1:
             get_targets.wait()
-        for at in range(0, n, ROWS):
-            value = dot(samples[at : at + ROWS, :], panel)
+        for at in range(0, n, rows):
+            value = dot(samples[at : at + rows, :], panel)
             if j:
-                value = acc[at : at + ROWS, :] * value
+                value = acc[at : at + rows, :] * value
             if j < panels - 1:
-                acc[at : at + ROWS, :] = value
+                acc[at : at + rows, :] = value
             else:
                 feat = (value * (1.0 / math.sqrt(F))).astype(bf16)
-                feat_ref[at : at + ROWS, :] = feat
-                term = dot(targets[:, at : at + ROWS], feat)
+                feat_ref[at : at + rows, :] = feat
+                term = dot(targets[:, at : at + rows], feat)
                 total = term if total is None else total + term
     step = total.shape[0] // parts
     for p in range(parts):
@@ -231,7 +234,7 @@
             pltpu.VMEM((n, width), f32),
             pltpu.SemaphoreType.DMA((2 + 2 * panels,)),
         ],
-        compiler_params=pltpu.CompilerParams(vmem_limit_bytes=48 * 1024 * 1024),
+        compiler_params=pltpu.CompilerParams(vmem_limit_bytes=50 * 1024 * 1024),
         cost_estimate=pl.CostEstimate(flops=2 * 10**9, bytes_accessed=5 * 2**20, transcendentals=0),
     )(core, samples, mine, other, targets_t)
 
@@ -263,32 +266,20 @@
     return parts, sums
 
 
-def fetch(high_hbm, low_hbm, high, low, sems, halves):
-    span = high.shape[0] // halves
-    copies = [
-        [
-            pltpu.make_async_copy(src.at[pl.ds(h * span, span)], dst.at[pl.ds(h * span, span)], sems.at[2 * h + k])
-            for k, (src, dst) in enumerate(((high_hbm, high), (low_hbm, low)))
-        ]
-        for h in range(halves)
-    ]
-    for copy in sum(copies, []):
-        copy.start()
-    return high, low, copies
-
-
 def coarse(parts, inverse):
-    high_ref, low_ref, copies = inverse
-    rows, total = parts[0].shape[0], None
+    high_ref, low_ref, copy = inverse
+    rows, total, left = parts[0].shape[0], None, []
     for h, part in enumerate(parts):
         span = slice(h * part.shape[1], (h + 1) * part.shape[1])
         high = part.astype(bf16).astype(f32)
         both = jnp.concatenate([high, part - high], 0).astype(bf16)
-        copies[h][0].wait()
         one = dot(both, high_ref[span, :])
-        copies[h][1].wait()
-        term = one[:rows] + one[rows:] + dot(both, low_ref[span, :])[:rows]
+        term = one[:rows] + one[rows:]
         total = term if total is None else total + term
+        left.append((span, both))
+    copy.wait()
+    for span, both in left:
+        total = total + dot(both, low_ref[span, :])[:rows]
     return total
 
 
@@ -306,10 +297,12 @@
 
 
 def first_kernel(
-    factor, parity_ref, got_ref, high_hbm, low_hbm, resid_ref, scale_ref, dir_ref, send_ref, rho_ref, dots_ref, high, low, sems
+    factor, parity_ref, got_ref, high_ref, low_hbm, resid_ref, scale_ref, dir_ref, send_ref, rho_ref, dots_ref, low, sem
 ):
     count = resid_ref.shape[1]
-    inverse = fetch(high_hbm, low_hbm, high, low, sems, rho_ref.shape[1] // count)
+    fetch = pltpu.make_async_copy(low_hbm, low, sem)
+    fetch.start()
+    inverse = high_ref, low, fetch
     parts, sums = gathered(got_ref, rho_ref.shape[1] // count, count)
     parts = [part * factor for part in parts]
     product, direction = next_direction(
@@ -325,11 +318,13 @@
 
 
 def step_kernel(
-    factor, parity_ref, got_ref, high_hbm, low_hbm, resid_ref, scale_ref, image_ref, old_ref, rho_ref, dots_ref, answer_ref,
-    dir_ref, send_ref, new_rho_ref, new_dots_ref, new_resid_ref, new_answer_ref, high, low, sems,
+    factor, parity_ref, got_ref, high_ref, low_hbm, resid_ref, scale_ref, image_ref, old_ref, rho_ref, dots_ref, answer_ref,
+    dir_ref, send_ref, new_rho_ref, new_dots_ref, new_resid_ref, new_answer_ref, low, sem,
 ):
     count = resid_ref.shape[1]
-    inverse = fetch(high_hbm, low_hbm, high, low, sems, rho_ref.shape[1] // count)
+    fetch = pltpu.make_async_copy(low_hbm, low, sem)
+    fetch.start()
+    inverse = high_ref, low, fetch
     parts, sums = gathered(got_ref, rho_ref.shape[1] // count, count)
     energy, product = lane(dots_ref[...], 0), lane(dots_ref[...], 1)
     alpha = product / sums[0]
@@ -366,12 +361,11 @@
     return pl.pallas_call(
         functools.partial(kernel, factor),
         out_shape=outs,
-        in_specs=[pl.BlockSpec(memory_space=pltpu.SMEM), vmem]
-        + [pl.BlockSpec(memory_space=pl.ANY)] * 2
+        in_specs=[pl.BlockSpec(memory_space=pltpu.SMEM), vmem, vmem, pl.BlockSpec(memory_space=pl.ANY)]
         + [vmem] * (len(operands) - 3),
         out_specs=[vmem] * len(outs),
-        scratch_shapes=[pltpu.VMEM((n, n), bf16)] * 2 + [pltpu.SemaphoreType.DMA((2 * (n // count),))],
-        compiler_params=pltpu.CompilerParams(vmem_limit_bytes=52 * 1024 * 1024),
+        scratch_shapes=[pltpu.VMEM((n, n), bf16), pltpu.SemaphoreType.DMA],
+        compiler_params=pltpu.CompilerParams(vmem_limit_bytes=50 * 1024 * 1024),
         cost_estimate=pl.CostEstimate(flops=10**8, bytes_accessed=5 * 2**20, transcendentals=0),
     )(parity, *operands)
 
@@ -393,7 +387,7 @@
 
 
 def body(samples, projections, targets, feature_scale, coarse_factor):
-    n_dp, n_sk = lax.axis_size("dp"), lax.axis_size("sketch")
+    n_dp, n_sk = lax.axis_size(DP), lax.axis_size("sketch")
     count = projections.shape[2]
     width = targets.shape[1]
     mine = width // n_dp
@@ -404,23 +398,15 @@
     n = samples.shape[0]
     scale = feature_scale[None, :]
 
-    chips = n_dp // 2
-    core = (lax.axis_index("dp") % 2).astype(jnp.int32).reshape(1)
-    mine_proj = lax.all_to_all(
-        repeat(projections, chips),
-        "dp",
-        0,
-        0,
-        axis_index_groups=[[2 * z + c for z in range(chips)] for c in range(2)],
-    )
+    core = lax.axis_index("core").astype(jnp.int32).reshape(1)
+    mine_proj = lax.all_to_all(repeat(projections, lax.axis_size("z")), "z", 0, 0)
     factor_high, factor_low, core = coarse_factor_inverse(core, coarse_factor)
     mine_proj, core = lax.optimization_barrier((mine_proj, core))
-    other_proj = lax.ppermute(mine_proj, "dp", [(i, i ^ 1) for i in range(n_dp)])
+    other_proj = lax.ppermute(mine_proj, "core", [(0, 1), (1, 0)])
     feat, part = make_features(core, samples, mine_proj, other_proj, targets.T, n_dp)
-    inv_high, inv_low = coarse_inverse(factor_high, factor_low)
 
     def scatter_dp(value):
-        return jnp.sum(lax.all_to_all(value, "dp", 0, 0), 0)
+        return jnp.sum(lax.all_to_all(value, DP, 0, 0), 0)
 
     def gather_sk(value):
         return lax.all_to_all(jnp.broadcast_to(value[None], (n_sk,) + value.shape), "sketch", 0, 0)
@@ -429,11 +415,12 @@
         return gather_sk(jnp.concatenate([value.astype(bf16), slots(dots)], 1))
 
     def forward(send):
-        whole = lax.all_to_all(send, "dp", 0, 0).reshape(width, count)
+        whole = lax.all_to_all(send, DP, 0, 0).reshape(width, count)
         sums = lax.dot_general(whole, feat, (((1,), (1,)), ((), ())), preferred_element_type=f32)
         return whole, sums.astype(bf16).reshape(n_sk, cols, n)
 
     resid = scatter_dp(part)
+    inv_high, inv_low = coarse_inverse(factor_high, factor_low, resid)
     got = everywhere(resid, row_sum(scale * resid * resid))
     direction, send, rho, dots = run_coarse(
         first_kernel, factor, n_dp, parity, got, inv_high, inv_low, resid, scale
@@ -464,18 +451,20 @@
     got = gather_sk(jnp.concatenate([u, slots(curve)], 1)).reshape(width, n + SLOTS)
     image = dot(got[:, :n], feat)
     sent = jnp.concatenate([image.astype(bf16), got[:, n:]], 1)
-    got = lax.all_to_all(sent.reshape(n_dp, mine, count + SLOTS), "dp", 0, 0).astype(f32)
+    got = lax.all_to_all(sent.reshape(n_dp, mine, count + SLOTS), DP, 0, 0).astype(f32)
     total = jnp.sum(got, 0)
     image = total[:, :count] + RIDGE * direction
     alpha = dots[:, 1:2] / row_sum(total[:, count:])
     out = jnp.stack([answer + alpha * direction, resid - alpha * image]).astype(bf16)
-    got = lax.all_to_all(jnp.broadcast_to(out[None], (n_dp,) + out.shape), "dp", 0, 0)
+    got = lax.all_to_all(jnp.broadcast_to(out[None], (n_dp,) + out.shape), DP, 0, 0)
     answer, resid = outputs(got)
     return answer.T, resid.T
 
 
 def solution(mesh):
-    placed = (P("dp", None), P(None, "dp", "sketch"), P("dp", None), P("sketch"), P())
+    chips = mesh.shape["dp"] // 2
+    mesh = jax.sharding.Mesh(mesh.devices.reshape(chips, 2, -1), ("z", "core", "sketch"))
+    placed = (P(DP, None), P(None, DP, "sketch"), P(DP, None), P("sketch"), P())
     return jax.shard_map(
         body,
         mesh=mesh,

time: 262 us -> 230 us (0.88)
  Pallas kernels: 69.2 us -> 35.4 us
    pallas_call x1, Pallas kernels: 32.9 us -> 1.04 us  [repeat(): pl.pallas_call(repeat_kernel, out_shape=jax.ShapeDtypeStruct((count,) + v...]
  transfers between devices with their start and end apart: 4 -> 4, of which waited for: 4 -> 4; matrix products, arithmetic and copies ran while one was open for 0% -> 0% of each run, Pallas kernels for 9% -> 10%
where the time goes in v5:
time: 230 us; the launch traced here: 229 us
  blocking collectives  131 us (57%)
  Pallas kernels  35.4 us (15%)
  waiting for transfers between devices  27.8 us (12%)
  starting transfers between devices  26.6 us (12%)
  local copies, waits for them, and re-layouts  3.91 us (2%)
    all_to_all x3, blocking collectives, gather_sk(): lax.all_to_all(jnp.broadcast_to(value[None], (n_sk,) + value.shape), 'ske...  40.1 us
    all_to_all x2, blocking collectives, forward(): whole = lax.all_to_all(send, DP, 0, 0).reshape(width, count)  23.9 us
    pallas_call x1, Pallas kernels, coarse_factor_inverse(): pl.pallas_call(inverse_kernel, out_shape=[jax.ShapeDtypeStruct((n, n), bf...  15.6 us
    all_to_all x1, blocking collectives, scatter_dp(): return jnp.sum(lax.all_to_all(value, DP, 0, 0), 0)  14.3 us
    all_to_all x1, blocking collectives, body(): u = rounded(jnp.sum(lax.all_to_all(sums, 'sketch', 0, 0).astype(f32), 0))  14.2 us
    all_to_all x1, waiting for transfers between devices, body(): lax.all_to_all(repeat(projections, lax.axis_size('z')), 'z', 0, 0)  13.6 us
    all_to_all x1, blocking collectives, body(): lax.all_to_all(sent.reshape(n_dp, mine, count + SLOTS), DP, 0, 0)  13.3 us
    all_to_all x1, blocking collectives, body(): lax.all_to_all(jnp.concatenate([sums, slots(squares)], 2), 'sketch', 0, 0)  13.1 us
  transfers between devices with their start and end apart: 4, of which 4 were waited for; matrix products, arithmetic and copies ran while one was open for 0% of the time, Pallas kernels for 10%

profile of v5, /device:TPU:1, one launch (start us, length us, event | category | flops | bytes accessed | tf_op | source)
XLA Modules:
  0.0 229.1 jit_solution(12246544161157263517)
XLA Ops:
  2.6 10.9 %all-to-all-start = ((bf16[8,4,32,512]{3,2,1,0:T(8,128)(2,1)}), bf16[8,4,32,512]{3,2,1,0:T(8,128)(2,1)S(1)}, u32[]{:S(2)}, u32[]{:S(2)}) async-start(bf16[8,4,32,512]{3,2,1,0:T(8,128)(2,1)} %shard_map.68), calls=%async_computation | async-start | bytes 2097152 | tf_op jit(solution)/shard_map/all_to_all | solution.py:402
  13.5 15.6 %shard_map.69 = (bf16[1024,1024]{1,0:T(8,128)(2,1)}, bf16[1024,1024]{1,0:T(8,128)(2,1)}, s32[1]{0:T(128)}) custom-call(s32[1]{0:T(128)} %bitcast.1.core_ref, bf16[1024,1024]{1,0:T(8,128)(2,1)} %lower_hbm.1), custom_call_target="tpu_custom_call" | custom-call | flops 10000000000 | bytes 6291456 | tf_op jit(solution)/shard_map/pallas_call | solution.py:99
  29.0 13.6 %all-to-all-done.mine_hbm = bf16[8,4,32,512]{3,2,1,0:T(8,128)(2,1)S(1)} async-done(((bf16[8,4,32,512]{3,2,1,0:T(8,128)(2,1)}), bf16[8,4,32,512]{3,2,1,0:T(8,128)(2,1)S(1)}, u32[]{:S(2)}, u32[]{:S(2)}) %all-to-all-start) | async-done | bytes 1048608 | tf_op jit(solution)/shard_map/all_to_all | solution.py:402
  42.6 2.4 %collective-permute-start = (bf16[8,4,32,512]{3,2,1,0:T(8,128)(2,1)S(1)}, bf16[8,4,32,512]{3,2,1,0:T(8,128)(2,1)S(1)}, u32[]{:S(2)}, u32[]{:S(2)}) collective-permute-start(bf16[8,4,32,512]{3,2,1,0:T(8,128)(2,1)S(1)} %all-to-all-done.mine_hbm), channel_id=1, source_target_pairs={{0,32},{32,0},{1,33},{33,1},{2,34},{34,2},{3,35},{35,3},{4,36},{36... | collective-permute-start | bytes 3145736 | tf_op jit(solution)/shard_map/ppermute | solution.py:405
  45.0 2.3 collective-permute-done.other_hbm
  48.3 5.5 %shard_map.70 = (bf16[1024,512]{1,0:T(8,128)(2,1)S(1)}, f32[16,4,512]{2,1,0:T(4,128)}) custom-call(s32[1]{0:T(128)} %get-tuple-element.23.core_ref, bf16[1024,512]{1,0:T(8,128)(2,1)S(1)} %copy-done.2, bf16[8,4,32,512]{3,2,1,0:T(8,128)(2,1)S(1)} %all-to-all-done.mine_hbm, bf16[8,4,32,512]{3,2,1,0:T(8,128)(2,1)} %copy-done.4, bf16[64,1024]{1,0:T(8,128)(2,1)S(1)} %bitcast.34), custom_call_target="tpu_custom_call" | custom-call | flops 2000000000 | bytes 5242880 | tf_op jit(solution)/shard_map/pallas_call | solution.py:222
  53.7 3.7 %all-to-all-start.1 = ((f32[16,4,512]{2,1,0:T(4,128)}), f32[16,4,512]{2,1,0:T(4,128)S(1)}, u32[]{:S(2)}, u32[]{:S(2)}) async-start(f32[16,4,512]{2,1,0:T(4,128)} %get-tuple-element.25), calls=%async_computation.1 | async-start | bytes 262144 | tf_op jit(solution)/shard_map/all_to_all | solution.py:409
  57.4 9.2 %all-to-all-done.1 = f32[16,4,512]{2,1,0:T(4,128)S(1)} async-done(((f32[16,4,512]{2,1,0:T(4,128)}), f32[16,4,512]{2,1,0:T(4,128)S(1)}, u32[]{:S(2)}, u32[]{:S(2)}) %all-to-all-start.1) | async-done | bytes 131104 | tf_op jit(solution)/shard_map/all_to_all | solution.py:409
  67.7 9.7 %all-to-all-start.2 = ((bf16[32,4,640]{2,1,0:T(4,128)(2,1)}), bf16[32,4,640]{2,1,0:T(4,128)(2,1)S(1)}, u32[]{:S(2)}, u32[]{:S(2)}) async-start(bf16[32,4,640]{2,1,0:T(4,128)(2,1)} %broadcast_in_dim.16), calls=%async_computation.2 | async-start | bytes 327680 | tf_op jit(solution)/shard_map/all_to_all | solution.py:412
  77.4 6.8 %shard_map.71 = (bf16[1024,1024]{1,0:T(8,128)(2,1)S(1)}, bf16[1024,1024]{1,0:T(8,128)(2,1)}) custom-call(bf16[1024,1024]{1,0:T(8,128)(2,1)} %get-tuple-element.26.xh_ref, bf16[1024,1024]{1,0:T(8,128)(2,1)} %get-tuple-element.27.xl_ref, f32[4,512]{1,0:T(4,128)S(1)} %reduce_sum.119.order_hbm.resid_ref), custom_call_target="tpu_custom_call" | custom-call | flops 4000000000 | bytes 8388608 | tf_op jit(solution)/shard_map/pallas_call | solution.py:132
  84.2 2.8 %all-to-all-done.2.got_ref = bf16[32,4,640]{2,1,0:T(4,128)(2,1)S(1)} async-done(((bf16[32,4,640]{2,1,0:T(4,128)(2,1)}), bf16[32,4,640]{2,1,0:T(4,128)(2,1)S(1)}, u32[]{:S(2)}, u32[]{:S(2)}) %all-to-all-start.2) | async-done | bytes 163872 | tf_op jit(solution)/shard_map/all_to_all | solution.py:412
  87.0 2.3 %shard_map.72 = (f32[4,512]{1,0:T(4,128)S(1)}, bf16[16,4,512]{2,1,0:T(4,128)(2,1)S(1)}, f32[4,1024]{1,0:T(4,128)S(1)}, f32[4,128]{1,0:T(4,128)S(1)}) custom-call(s32[1]{0:T(128)} %bitcast.parity_ref, bf16[32,4,640]{2,1,0:T(4,128)(2,1)S(1)} %all-to-all-done.2.got_ref, bf16[1024,1024]{1,0:T(8,128)(2,1)S(1)} %get-tuple-element.28.high_ref, ...), custom_call_target="tpu_custom_call" | custom-call | flops 100000000 | bytes 5242880 | tf_op jit(solution)/shard_map/pallas_call | solution.py:361
  89.3 12.0 %all_to_all.65 = bf16[16,4,512]{2,1,0:T(4,128)(2,1)S(1)} all-to-all(bf16[16,4,512]{2,1,0:T(4,128)(2,1)S(1)} %get-tuple-element.30), channel_id=1, replica_groups=mesh['z'=8,'core'=2,'sketch'=32] {'z','core'}, dimensions={0} | all-to-all | bytes 131072 | tf_op jit(solution)/shard_map/all_to_all | solution.py:418
  101.8 14.2 %all_to_all.66 = bf16[32,2,1024]{2,1,0:T(2,128)(2,1)S(1)} all-to-all(bf16[32,2,1024]{2,1,0:T(2,128)(2,1)S(1)} %reshape.423), channel_id=1, replica_groups=mesh['z'=8,'core'=2,'sketch'=32] {'sketch'}, dimensions={0} | all-to-all | bytes 262144 | tf_op jit(solution)/shard_map/all_to_all | solution.py:431
  116.3 13.6 %all_to_all.67 = bf16[32,2,1024]{2,1,0:T(2,128)(2,1)S(1)} all-to-all(bf16[32,2,1024]{2,1,0:T(2,128)(2,1)S(1)} %broadcast_in_dim.18), channel_id=1, replica_groups=mesh['z'=8,'core'=2,'sketch'=32] {'sketch'}, dimensions={0} | all-to-all | bytes 262144 | tf_op jit(solution)/shard_map/all_to_all | solution.py:412
  130.3 14.3 %all_to_all.68 = f32[16,4,512]{2,1,0:T(4,128)S(1)} all-to-all(f32[16,4,512]{2,1,0:T(4,128)S(1)} %copy.34), channel_id=1, replica_groups=mesh['z'=8,'core'=2,'sketch'=32] {'z','core'}, dimensions={0} | all-to-all | bytes 262144 | tf_op jit(solution)/shard_map/all_to_all | solution.py:409
  145.0 12.8 %all_to_all.69.got_ref = bf16[32,4,640]{2,1,0:T(4,128)(2,1)S(1)} all-to-all(bf16[32,4,640]{2,1,0:T(4,128)(2,1)S(1)} %broadcast_in_dim.19), channel_id=1, replica_groups=mesh['z'=8,'core'=2,'sketch'=32] {'sketch'}, dimensions={0} | all-to-all | bytes 327680 | tf_op jit(solution)/shard_map/all_to_all | solution.py:412
  157.8 2.6 %shard_map.73 = (f32[4,512]{1,0:T(4,128)S(1)}, bf16[16,4,512]{2,1,0:T(4,128)(2,1)S(1)}, f32[4,1024]{1,0:T(4,128)}, f32[4,128]{1,0:T(4,128)S(1)}, f32[4,512]{1,0:T(4,128)S(1)}, /*index=5*/f32[4,512]{1,0:T(4,128)S(1)}) custom-call(s32[1]{0:T(128)} %bitcast.parity_ref, bf16[32,4,640]{2,1,0:T(4,128)(2,1)S(1)} %all_to_all.69.got_ref, ...), custom_call_target="tpu_custom_call" | custom-call | flops 100000000 | bytes 5242880 | tf_op jit(solution)/shard_map/pallas_call | solution.py:361
  160.4 12.0 %all_to_all.70 = bf16[16,4,512]{2,1,0:T(4,128)(2,1)S(1)} all-to-all(bf16[16,4,512]{2,1,0:T(4,128)(2,1)S(1)} %get-tuple-element.37), channel_id=1, replica_groups=mesh['z'=8,'core'=2,'sketch'=32] {'z','core'}, dimensions={0} | all-to-all | bytes 131072 | tf_op jit(solution)/shard_map/all_to_all | solution.py:418
  173.4 13.1 %all_to_all.71 = bf16[32,2,1152]{2,1,0:T(2,128)(2,1)S(1)} all-to-all(bf16[32,2,1152]{2,1,0:T(2,128)(2,1)S(1)} %fusion.2), channel_id=1, replica_groups=mesh['z'=8,'core'=2,'sketch'=32] {'sketch'}, dimensions={0} | all-to-all | bytes 294912 | tf_op jit(solution)/shard_map/all_to_all | solution.py:447
  187.1 13.8 %all_to_all.72 = bf16[32,2,1152]{2,1,0:T(2,128)(2,1)S(1)} all-to-all(bf16[32,2,1152]{2,1,0:T(2,128)(2,1)S(1)} %broadcast_in_dim.21), channel_id=1, replica_groups=mesh['z'=8,'core'=2,'sketch'=32] {'sketch'}, dimensions={0} | all-to-all | bytes 294912 | tf_op jit(solution)/shard_map/all_to_all | solution.py:412
  201.3 13.3 %all_to_all.73 = bf16[16,4,640]{2,1,0:T(4,128)(2,1)S(1)} all-to-all(bf16[16,4,640]{2,1,0:T(4,128)(2,1)S(1)} %reshape.428), channel_id=1, replica_groups=mesh['z'=8,'core'=2,'sketch'=32] {'z','core'}, dimensions={0} | all-to-all | bytes 163840 | tf_op jit(solution)/shard_map/all_to_all | solution.py:454
  215.1 12.3 %all_to_all.74.got_ref = bf16[16,2,4,512]{3,2,1,0:T(4,128)(2,1)} all-to-all(bf16[16,2,4,512]{3,2,1,0:T(4,128)(2,1)S(1)} %broadcast_in_dim.23), channel_id=1, replica_groups=mesh['z'=8,'core'=2,'sketch'=32] {'z','core'}, dimensions={0} | all-to-all | bytes 262144 | tf_op jit(solution)/shard_map/all_to_all | solution.py:459
  227.5 1.6 shard_map.74
  (68 shorter events, 8.2 us)
Async XLA Ops:
  0.6 0.9 copy-start
  2.6 40.1 %all-to-all-start = ((bf16[8,4,32,512]{3,2,1,0:T(8,128)(2,1)}), bf16[8,4,32,512]{3,2,1,0:T(8,128)(2,1)S(1)}, u32[]{:S(2)}, u32[]{:S(2)}) async-start(bf16[8,4,32,512]{3,2,1,0:T(8,128)(2,1)} %shard_map.68), calls=%async_computation | async-start | bytes 2097152 | tf_op jit(solution)/shard_map/all_to_all | solution.py:402
  13.4 34.8 %copy-start.2 = (bf16[1024,512]{1,0:T(8,128)(2,1)S(1)}, bf16[1024,512]{1,0:T(8,128)(2,1)}, u32[]{:S(2)}) copy-start(bf16[1024,512]{1,0:T(8,128)(2,1)} %samples_hbm.1) | copy-start | bytes 3145732
  13.4 34.8 %copy-start.3 = (bf16[1024,64]{0,1:T(8,128)(2,1)S(1)}, bf16[1024,64]{0,1:T(8,128)(2,1)}, u32[]{:S(2)}) copy-start(bf16[1024,64]{0,1:T(8,128)(2,1)} %param.7) | copy-start | bytes 393220
  42.6 4.7 %collective-permute-start = (bf16[8,4,32,512]{3,2,1,0:T(8,128)(2,1)S(1)}, bf16[8,4,32,512]{3,2,1,0:T(8,128)(2,1)S(1)}, u32[]{:S(2)}, u32[]{:S(2)}) collective-permute-start(bf16[8,4,32,512]{3,2,1,0:T(8,128)(2,1)S(1)} %all-to-all-done.mine_hbm), channel_id=1, source_target_pairs={{0,32},{32,0},{1,33},{33,1},{2,34},{34,2},{3,35},{35,3},{4,36},{36... | collective-permute-start | bytes 3145736 | tf_op jit(solution)/shard_map/ppermute | solution.py:405
  47.3 1.0 copy-start.4
  48.3 18.4 %copy-start.1 = (f32[512]{0:T(512)S(1)}, f32[512]{0:T(512)}, u32[]{:S(2)}) copy-start(f32[512]{0:T(512)} %param.8) | copy-start | bytes 6148
  53.7 12.9 %all-to-all-start.1 = ((f32[16,4,512]{2,1,0:T(4,128)}), f32[16,4,512]{2,1,0:T(4,128)S(1)}, u32[]{:S(2)}, u32[]{:S(2)}) async-start(f32[16,4,512]{2,1,0:T(4,128)} %get-tuple-element.25), calls=%async_computation.1 | async-start | bytes 262144 | tf_op jit(solution)/shard_map/all_to_all | solution.py:409
  67.7 19.3 %all-to-all-start.2 = ((bf16[32,4,640]{2,1,0:T(4,128)(2,1)}), bf16[32,4,640]{2,1,0:T(4,128)(2,1)S(1)}, u32[]{:S(2)}, u32[]{:S(2)}) async-start(bf16[32,4,640]{2,1,0:T(4,128)(2,1)} %broadcast_in_dim.16), calls=%async_computation.2 | async-start | bytes 327680 | tf_op jit(solution)/shard_map/all_to_all | solution.py:412

commit v6 on v5

--- a/solution.py
+++ b/solution.py
@@ -24,6 +24,10 @@
 
 def dot(a, b):
     return lax.dot_general(a, b, (((1,), (0,)), ((), ())), preferred_element_type=f32)
+
+
+def dot_turned(a, b):
+    return lax.dot_general(a, b, (((1,), (1,)), ((), ())), preferred_element_type=f32)
 
 
 def dot3(a, b):
@@ -111,30 +115,35 @@
     )(core, lower)
 
 
+def place(a, b):
+    return pl.ds((a * (a + 1) // 2 + b) * BLOCK, BLOCK)
+
+
 def product_kernel(xh_ref, xl_ref, order_hbm, high_ref, low_ref):
     del order_hbm
     spans = [slice(b, b + BLOCK) for b in range(0, xh_ref.shape[0], BLOCK)]
     parts = [[(xh_ref[row, col], xl_ref[row, col]) for col in spans[: r + 1]] for r, row in enumerate(spans)]
     turned = [[tuple(half.astype(f32).T.astype(bf16) for half in part) for part in row] for row in parts]
-    for a, row in enumerate(spans):
-        for b, col in enumerate(spans):
+    for a in range(len(spans)):
+        for b in range(a + 1):
             total = None
-            for k in range(max(a, b), len(spans)):
+            for k in range(a, len(spans)):
                 (ah, al), (bh, bl) = turned[k][a], parts[k][b]
                 term = dot(ah, bh) + (dot(ah, bl) + dot(al, bh))
                 total = term if total is None else total + term
-            high_ref[row, col], low_ref[row, col] = split(total)
+            high_ref[place(a, b), :], low_ref[place(a, b), :] = split(total)
 
 
 def coarse_inverse(xh, xl, order):
     n = xh.shape[0]
+    blocks = n // BLOCK
     vmem = pl.BlockSpec(memory_space=pltpu.VMEM)
     return pl.pallas_call(
         product_kernel,
-        out_shape=[jax.ShapeDtypeStruct((n, n), bf16)] * 2,
+        out_shape=[jax.ShapeDtypeStruct((blocks * (blocks + 1) // 2 * BLOCK, BLOCK), bf16)] * 2,
         in_specs=[vmem, vmem, pl.BlockSpec(memory_space=pl.ANY)],
         out_specs=[vmem] * 2,
-        compiler_params=pltpu.CompilerParams(vmem_limit_bytes=50 * 1024 * 1024),
+        compiler_params=pltpu.CompilerParams(vmem_limit_bytes=52 * 1024 * 1024),
         cost_estimate=pl.CostEstimate(flops=4 * 10**9, bytes_accessed=8 * 2**20, transcendentals=0),
     )(xh, xl, order)
 
@@ -173,68 +182,50 @@
     )(got)
 
 
-ROWS = 1024
-
-
 def feature_kernel(
-    core_ref, samples_hbm, mine_hbm, other_hbm, targets_hbm, feat_ref, part_ref, samples, proj, targets, acc, sems
+    core_ref, samples_hbm, mine_ref, other_ref, targets_hbm, feat_ref, part_ref, proj, samples_ref, targets_ref, sems
 ):
-    n, parts, panels = samples.shape[0], part_ref.shape[0], proj.shape[0]
-    core, rows = core_ref[0], min(ROWS, n)
-    get_samples = pltpu.make_async_copy(samples_hbm, samples, sems.at[0])
-    get_targets = pltpu.make_async_copy(targets_hbm, targets, sems.at[1])
-    get_proj = [
-        [
-            pltpu.make_async_copy(half.at[:, j], proj.at[j, :, at], sems.at[2 + 2 * j + k])
-            for k, (half, at) in enumerate(((mine_hbm, core), (other_hbm, 1 - core)))
-        ]
-        for j in range(panels)
-    ]
-    for copy in [get_samples] + sum(get_proj, []) + [get_targets]:
-        copy.start()
+    core = core_ref[0]
+    get_samples = pltpu.make_async_copy(samples_hbm, samples_ref, sems.at[0])
+    get_targets = pltpu.make_async_copy(targets_hbm, targets_ref, sems.at[1])
+    get_samples.start()
+    get_targets.start()
+    for j in range(proj.shape[0]):
+        proj[j, :, core] = mine_ref[:, j]
+        proj[j, :, 1 - core] = other_ref[:, j]
     get_samples.wait()
-    total = None
-    for j in range(panels):
-        for copy in get_proj[j]:
-            copy.wait()
-        panel = proj[j].reshape(samples.shape[1], proj.shape[-1])
-        if j == panels - 1:
-            get_targets.wait()
-        for at in range(0, n, rows):
-            value = dot(samples[at : at + rows, :], panel)
-            if j:
-                value = acc[at : at + rows, :] * value
-            if j < panels - 1:
-                acc[at : at + rows, :] = value
-            else:
-                feat = (value * (1.0 / math.sqrt(F))).astype(bf16)
-                feat_ref[at : at + rows, :] = feat
-                term = dot(targets[:, at : at + rows], feat)
-                total = term if total is None else total + term
-    step = total.shape[0] // parts
-    for p in range(parts):
+    samples, value = samples_ref[...], None
+    for j in range(proj.shape[0]):
+        panel = dot(samples, proj[j].reshape(samples.shape[1], proj.shape[-1]))
+        value = panel if value is None else value * panel
+    feat = (value * (1.0 / math.sqrt(F))).astype(bf16)
+    feat_ref[...] = feat
+    get_targets.wait()
+    total = dot(targets_ref[...], feat)
+    step = part_ref.shape[1]
+    for p in range(part_ref.shape[0]):
         part_ref[p] = total[p * step : (p + 1) * step, :]
 
 
 def make_features(core, samples, mine, other, targets_t, parts):
     n = samples.shape[0]
     chips, panels, rows, width = mine.shape
+    vmem, anywhere = pl.BlockSpec(memory_space=pltpu.VMEM), pl.BlockSpec(memory_space=pl.ANY)
     return pl.pallas_call(
         feature_kernel,
         out_shape=[
             jax.ShapeDtypeStruct((n, width), bf16),
             jax.ShapeDtypeStruct((parts, targets_t.shape[0] // parts, width), f32),
         ],
-        in_specs=[pl.BlockSpec(memory_space=pltpu.SMEM)] + [pl.BlockSpec(memory_space=pl.ANY)] * 4,
-        out_specs=[pl.BlockSpec(memory_space=pltpu.VMEM)] * 2,
+        in_specs=[pl.BlockSpec(memory_space=pltpu.SMEM), anywhere, vmem, vmem, anywhere],
+        out_specs=[vmem] * 2,
         scratch_shapes=[
+            pltpu.VMEM((panels, chips, 2, rows, width), bf16),
             pltpu.VMEM(samples.shape, bf16),
-            pltpu.VMEM((panels, chips, 2, rows, width), bf16),
             pltpu.VMEM(targets_t.shape, bf16),
-            pltpu.VMEM((n, width), f32),
-            pltpu.SemaphoreType.DMA((2 + 2 * panels,)),
+            pltpu.SemaphoreType.DMA((2,)),
         ],
-        compiler_params=pltpu.CompilerParams(vmem_limit_bytes=50 * 1024 * 1024),
+        compiler_params=pltpu.CompilerParams(vmem_limit_bytes=49 * 1024 * 1024),
         cost_estimate=pl.CostEstimate(flops=2 * 10**9, bytes_accessed=5 * 2**20, transcendentals=0),
     )(core, samples, mine, other, targets_t)
 
@@ -267,20 +258,25 @@
 
 
 def coarse(parts, inverse):
-    high_ref, low_ref, copy = inverse
-    rows, total, left = parts[0].shape[0], None, []
-    for h, part in enumerate(parts):
-        span = slice(h * part.shape[1], (h + 1) * part.shape[1])
+    high_ref, low_ref, fetch = inverse
+    rows, sides = parts[0].shape[0], []
+    for part in parts:
         high = part.astype(bf16).astype(f32)
         both = jnp.concatenate([high, part - high], 0).astype(bf16)
-        one = dot(both, high_ref[span, :])
-        term = one[:rows] + one[rows:]
-        total = term if total is None else total + term
-        left.append((span, both))
-    copy.wait()
-    for span, both in left:
-        total = total + dot(both, low_ref[span, :])[:rows]
-    return total
+        sides += [both[:, at : at + BLOCK] for at in range(0, part.shape[1], BLOCK)]
+    blocks = range(len(sides))
+
+    def times(ref, both, a, b):
+        return dot(both, ref[place(a, b), :]) if a >= b else dot_turned(both, ref[place(b, a), :])
+
+    solved = []
+    for b in blocks:
+        one = sum(times(high_ref, sides[a], a, b) for a in blocks)
+        solved.append(one[:rows] + one[rows:])
+    fetch.wait()
+    for b in blocks:
+        solved[b] = solved[b] + sum(times(low_ref, sides[a], a, b) for a in blocks)[:rows]
+    return jnp.concatenate(solved, 1)
 
 
 def next_direction(parity_ref, parts, inverse, resid, scale, energy, factor):
@@ -349,13 +345,12 @@
 
 def run_coarse(kernel, factor, n_dp, parity, *operands, more=0):
     rows, count = operands[3].shape
-    n = operands[1].shape[0]
     vmem = pl.BlockSpec(memory_space=pltpu.VMEM)
     wide = jax.ShapeDtypeStruct((rows, count), f32)
     outs = [
         wide,
         jax.ShapeDtypeStruct((n_dp, rows, count), bf16),
-        jax.ShapeDtypeStruct((rows, n), f32),
+        jax.ShapeDtypeStruct((rows, K), f32),
         jax.ShapeDtypeStruct((rows, SLOTS), f32),
     ] + [wide] * more
     return pl.pallas_call(
@@ -364,8 +359,8 @@
         in_specs=[pl.BlockSpec(memory_space=pltpu.SMEM), vmem, vmem, pl.BlockSpec(memory_space=pl.ANY)]
         + [vmem] * (len(operands) - 3),
         out_specs=[vmem] * len(outs),
-        scratch_shapes=[pltpu.VMEM((n, n), bf16), pltpu.SemaphoreType.DMA],
-        compiler_params=pltpu.CompilerParams(vmem_limit_bytes=50 * 1024 * 1024),
+        scratch_shapes=[pltpu.VMEM(operands[2].shape, bf16), pltpu.SemaphoreType.DMA],
+        compiler_params=pltpu.CompilerParams(vmem_limit_bytes=52 * 1024 * 1024),
         cost_estimate=pl.CostEstimate(flops=10**8, bytes_accessed=5 * 2**20, transcendentals=0),
     )(parity, *operands)
 

time: 230 us -> 227 us (0.987)
  Pallas kernels: 35.4 us -> 32.1 us
  transfers between devices with their start and end apart: 4 -> 4, of which waited for: 4 -> 4; matrix products, arithmetic and copies ran while one was open for 0% -> 0% of each run, Pallas kernels for 10% -> 9%
where the time goes in v6:
time: 227 us; the launch traced here: 226 us
  blocking collectives  130 us (57%)
  Pallas kernels  32.1 us (14%)
  waiting for transfers between devices  29.2 us (13%)
  starting transfers between devices  26.6 us (12%)
  local copies, waits for them, and re-layouts  4.18 us (2%)
    all_to_all x3, blocking collectives, gather_sk(): lax.all_to_all(jnp.broadcast_to(value[None], (n_sk,) + value.shape), 'ske...  39.9 us
    all_to_all x2, blocking collectives, forward(): whole = lax.all_to_all(send, DP, 0, 0).reshape(width, count)  23.9 us
    pallas_call x1, Pallas kernels, coarse_factor_inverse(): pl.pallas_call(inverse_kernel, out_shape=[jax.ShapeDtypeStruct((n, n), bf...  15.5 us
    all_to_all x1, blocking collectives, scatter_dp(): return jnp.sum(lax.all_to_all(value, DP, 0, 0), 0)  14.4 us
    all_to_all x1, waiting for transfers between devices, body(): lax.all_to_all(repeat(projections, lax.axis_size('z')), 'z', 0, 0)  13.7 us
    all_to_all x1, blocking collectives, body(): lax.all_to_all(sent.reshape(n_dp, mine, count + SLOTS), DP, 0, 0)  13.3 us
    all_to_all x1, blocking collectives, body(): lax.all_to_all(jnp.concatenate([sums, slots(squares)], 2), 'sketch', 0, 0)  13.1 us
    all_to_all x1, blocking collectives, body(): u = rounded(jnp.sum(lax.all_to_all(sums, 'sketch', 0, 0).astype(f32), 0))  13 us
  transfers between devices with their start and end apart: 4, of which 4 were waited for; matrix products, arithmetic and copies ran while one was open for 0% of the time, Pallas kernels for 9%

profile of v6, /device:TPU:1, one launch (start us, length us, event | category | flops | bytes accessed | tf_op | source)
XLA Modules:
  0.0 226.2 jit_solution(9911415200023481911)
XLA Ops:
  2.6 10.9 %all-to-all-start = ((bf16[8,4,32,512]{3,2,1,0:T(8,128)(2,1)}), bf16[8,4,32,512]{3,2,1,0:T(8,128)(2,1)S(1)}, u32[]{:S(2)}, u32[]{:S(2)}) async-start(bf16[8,4,32,512]{3,2,1,0:T(8,128)(2,1)} %shard_map.68), calls=%async_computation | async-start | bytes 2097152 | tf_op jit(solution)/shard_map/all_to_all | solution.py:397
  13.4 15.5 %shard_map.69 = (bf16[1024,1024]{1,0:T(8,128)(2,1)}, bf16[1024,1024]{1,0:T(8,128)(2,1)}, s32[1]{0:T(128)}) custom-call(s32[1]{0:T(128)} %bitcast.1.core_ref, bf16[1024,1024]{1,0:T(8,128)(2,1)} %lower_hbm.1), custom_call_target="tpu_custom_call" | custom-call | flops 10000000000 | bytes 6291456 | tf_op jit(solution)/shard_map/pallas_call | solution.py:103
  28.9 13.7 %all-to-all-done.mine_ref = bf16[8,4,32,512]{3,2,1,0:T(8,128)(2,1)S(1)} async-done(((bf16[8,4,32,512]{3,2,1,0:T(8,128)(2,1)}), bf16[8,4,32,512]{3,2,1,0:T(8,128)(2,1)S(1)}, u32[]{:S(2)}, u32[]{:S(2)}) %all-to-all-start) | async-done | bytes 1048608 | tf_op jit(solution)/shard_map/all_to_all | solution.py:397
  42.6 2.4 %collective-permute-start = (bf16[8,4,32,512]{3,2,1,0:T(8,128)(2,1)S(1)}, bf16[8,4,32,512]{3,2,1,0:T(8,128)(2,1)S(1)}, u32[]{:S(2)}, u32[]{:S(2)}) collective-permute-start(bf16[8,4,32,512]{3,2,1,0:T(8,128)(2,1)S(1)} %all-to-all-done.mine_ref), channel_id=1, source_target_pairs={{0,32},{32,0},{1,33},{33,1},{2,34},{34,2},{3,35},{35,3},{4,36},{36... | collective-permute-start | bytes 3145736 | tf_op jit(solution)/shard_map/ppermute | solution.py:400
  45.0 2.3 %collective-permute-done.other_ref = bf16[8,4,32,512]{3,2,1,0:T(8,128)(2,1)S(1)} collective-permute-done((bf16[8,4,32,512]{3,2,1,0:T(8,128)(2,1)S(1)}, bf16[8,4,32,512]{3,2,1,0:T(8,128)(2,1)S(1)}, u32[]{:S(2)}, u32[]{:S(2)}) %collective-permute-start) | collective-permute-done | bytes 1048608 | tf_op jit(solution)/shard_map/ppermute | solution.py:400
  48.5 4.3 %shard_map.70 = (bf16[1024,512]{1,0:T(8,128)(2,1)S(1)}, f32[16,4,512]{2,1,0:T(4,128)}) custom-call(s32[1]{0:T(128)} %get-tuple-element.23.core_ref, bf16[1024,512]{1,0:T(8,128)(2,1)S(1)} %copy-done.2, bf16[8,4,32,512]{3,2,1,0:T(8,128)(2,1)S(1)} %all-to-all-done.mine_ref, bf16[8,4,32,512]{3,2,1,0:T(8,128)(2,1)S(1)} %collective-permute-done.other_ref, ...), custom_call_target="tpu_custom_call" | custom-call | flops 2000000000 | bytes 5242880 | tf_op jit(solution)/shard_map/pallas_call | solution.py:214
  52.9 3.7 %all-to-all-start.1 = ((f32[16,4,512]{2,1,0:T(4,128)}), f32[16,4,512]{2,1,0:T(4,128)S(1)}, u32[]{:S(2)}, u32[]{:S(2)}) async-start(f32[16,4,512]{2,1,0:T(4,128)} %get-tuple-element.25), calls=%async_computation.1 | async-start | bytes 262144 | tf_op jit(solution)/shard_map/all_to_all | solution.py:404
  56.6 9.2 %all-to-all-done.1 = f32[16,4,512]{2,1,0:T(4,128)S(1)} async-done(((f32[16,4,512]{2,1,0:T(4,128)}), f32[16,4,512]{2,1,0:T(4,128)S(1)}, u32[]{:S(2)}, u32[]{:S(2)}) %all-to-all-start.1) | async-done | bytes 131104 | tf_op jit(solution)/shard_map/all_to_all | solution.py:404
  66.9 9.7 %all-to-all-start.2 = ((bf16[32,4,640]{2,1,0:T(4,128)(2,1)}), bf16[32,4,640]{2,1,0:T(4,128)(2,1)S(1)}, u32[]{:S(2)}, u32[]{:S(2)}) async-start(bf16[32,4,640]{2,1,0:T(4,128)(2,1)} %broadcast_in_dim.16), calls=%async_computation.2 | async-start | bytes 327680 | tf_op jit(solution)/shard_map/all_to_all | solution.py:407
  76.6 5.5 %shard_map.71 = (bf16[2560,256]{1,0:T(8,128)(2,1)S(1)}, bf16[2560,256]{1,0:T(8,128)(2,1)}) custom-call(bf16[1024,1024]{1,0:T(8,128)(2,1)} %get-tuple-element.26.xh_ref, bf16[1024,1024]{1,0:T(8,128)(2,1)} %get-tuple-element.27.xl_ref, f32[4,512]{1,0:T(4,128)S(1)} %reduce_sum.119.order_hbm.resid_ref), custom_call_target="tpu_custom_call" | custom-call | flops 4000000000 | bytes 8388608 | tf_op jit(solution)/shard_map/pallas_call | solution.py:141
  82.1 4.1 %all-to-all-done.2.got_ref = bf16[32,4,640]{2,1,0:T(4,128)(2,1)S(1)} async-done(((bf16[32,4,640]{2,1,0:T(4,128)(2,1)}), bf16[32,4,640]{2,1,0:T(4,128)(2,1)S(1)}, u32[]{:S(2)}, u32[]{:S(2)}) %all-to-all-start.2) | async-done | bytes 163872 | tf_op jit(solution)/shard_map/all_to_all | solution.py:407
  86.2 1.9 shard_map.72
  88.1 12.0 %all_to_all.65 = bf16[16,4,512]{2,1,0:T(4,128)(2,1)S(1)} all-to-all(bf16[16,4,512]{2,1,0:T(4,128)(2,1)S(1)} %get-tuple-element.30), channel_id=1, replica_groups=mesh['z'=8,'core'=2,'sketch'=32] {'z','core'}, dimensions={0} | all-to-all | bytes 131072 | tf_op jit(solution)/shard_map/all_to_all | solution.py:413
  100.6 13.0 %all_to_all.66 = bf16[32,2,1024]{2,1,0:T(2,128)(2,1)S(1)} all-to-all(bf16[32,2,1024]{2,1,0:T(2,128)(2,1)S(1)} %reshape.423), channel_id=1, replica_groups=mesh['z'=8,'core'=2,'sketch'=32] {'sketch'}, dimensions={0} | all-to-all | bytes 262144 | tf_op jit(solution)/shard_map/all_to_all | solution.py:426
  113.9 13.4 %all_to_all.67 = bf16[32,2,1024]{2,1,0:T(2,128)(2,1)S(1)} all-to-all(bf16[32,2,1024]{2,1,0:T(2,128)(2,1)S(1)} %broadcast_in_dim.18), channel_id=1, replica_groups=mesh['z'=8,'core'=2,'sketch'=32] {'sketch'}, dimensions={0} | all-to-all | bytes 262144 | tf_op jit(solution)/shard_map/all_to_all | solution.py:407
  127.7 14.4 %all_to_all.68 = f32[16,4,512]{2,1,0:T(4,128)S(1)} all-to-all(f32[16,4,512]{2,1,0:T(4,128)S(1)} %copy.34), channel_id=1, replica_groups=mesh['z'=8,'core'=2,'sketch'=32] {'z','core'}, dimensions={0} | all-to-all | bytes 262144 | tf_op jit(solution)/shard_map/all_to_all | solution.py:404
  142.5 12.8 %all_to_all.69.got_ref = bf16[32,4,640]{2,1,0:T(4,128)(2,1)S(1)} all-to-all(bf16[32,4,640]{2,1,0:T(4,128)(2,1)S(1)} %broadcast_in_dim.19), channel_id=1, replica_groups=mesh['z'=8,'core'=2,'sketch'=32] {'sketch'}, dimensions={0} | all-to-all | bytes 327680 | tf_op jit(solution)/shard_map/all_to_all | solution.py:407
  155.4 2.1 shard_map.73
  157.4 12.0 %all_to_all.70 = bf16[16,4,512]{2,1,0:T(4,128)(2,1)S(1)} all-to-all(bf16[16,4,512]{2,1,0:T(4,128)(2,1)S(1)} %get-tuple-element.37), channel_id=1, replica_groups=mesh['z'=8,'core'=2,'sketch'=32] {'z','core'}, dimensions={0} | all-to-all | bytes 131072 | tf_op jit(solution)/shard_map/all_to_all | solution.py:413
  170.5 13.1 %all_to_all.71 = bf16[32,2,1152]{2,1,0:T(2,128)(2,1)S(1)} all-to-all(bf16[32,2,1152]{2,1,0:T(2,128)(2,1)S(1)} %fusion.2), channel_id=1, replica_groups=mesh['z'=8,'core'=2,'sketch'=32] {'sketch'}, dimensions={0} | all-to-all | bytes 294912 | tf_op jit(solution)/shard_map/all_to_all | solution.py:442
  184.2 13.8 %all_to_all.72 = bf16[32,2,1152]{2,1,0:T(2,128)(2,1)S(1)} all-to-all(bf16[32,2,1152]{2,1,0:T(2,128)(2,1)S(1)} %broadcast_in_dim.21), channel_id=1, replica_groups=mesh['z'=8,'core'=2,'sketch'=32] {'sketch'}, dimensions={0} | all-to-all | bytes 294912 | tf_op jit(solution)/shard_map/all_to_all | solution.py:407
  198.4 13.3 %all_to_all.73 = bf16[16,4,640]{2,1,0:T(4,128)(2,1)S(1)} all-to-all(bf16[16,4,640]{2,1,0:T(4,128)(2,1)S(1)} %reshape.428), channel_id=1, replica_groups=mesh['z'=8,'core'=2,'sketch'=32] {'z','core'}, dimensions={0} | all-to-all | bytes 163840 | tf_op jit(solution)/shard_map/all_to_all | solution.py:449
  212.2 12.3 %all_to_all.74.got_ref = bf16[16,2,4,512]{3,2,1,0:T(4,128)(2,1)} all-to-all(bf16[16,2,4,512]{3,2,1,0:T(4,128)(2,1)S(1)} %broadcast_in_dim.23), channel_id=1, replica_groups=mesh['z'=8,'core'=2,'sketch'=32] {'z','core'}, dimensions={0} | all-to-all | bytes 262144 | tf_op jit(solution)/shard_map/all_to_all | solution.py:454
  224.5 1.6 shard_map.74
  (66 shorter events, 8.4 us)
Async XLA Ops:
  0.6 0.9 copy-start
  2.6 40.1 %all-to-all-start = ((bf16[8,4,32,512]{3,2,1,0:T(8,128)(2,1)}), bf16[8,4,32,512]{3,2,1,0:T(8,128)(2,1)S(1)}, u32[]{:S(2)}, u32[]{:S(2)}) async-start(bf16[8,4,32,512]{3,2,1,0:T(8,128)(2,1)} %shard_map.68), calls=%async_computation | async-start | bytes 2097152 | tf_op jit(solution)/shard_map/all_to_all | solution.py:397
  13.4 33.9 %copy-start.3 = (bf16[1024,64]{0,1:T(8,128)(2,1)S(1)}, bf16[1024,64]{0,1:T(8,128)(2,1)}, u32[]{:S(2)}) copy-start(bf16[1024,64]{0,1:T(8,128)(2,1)} %param.7) | copy-start | bytes 393220
  42.6 4.7 %collective-permute-start = (bf16[8,4,32,512]{3,2,1,0:T(8,128)(2,1)S(1)}, bf16[8,4,32,512]{3,2,1,0:T(8,128)(2,1)S(1)}, u32[]{:S(2)}, u32[]{:S(2)}) collective-permute-start(bf16[8,4,32,512]{3,2,1,0:T(8,128)(2,1)S(1)} %all-to-all-done.mine_ref), channel_id=1, source_target_pairs={{0,32},{32,0},{1,33},{33,1},{2,34},{34,2},{3,35},{35,3},{4,36},{36... | collective-permute-start | bytes 3145736 | tf_op jit(solution)/shard_map/ppermute | solution.py:400
  47.3 1.2 copy-start.2
  48.5 17.3 %copy-start.1 = (f32[512]{0:T(512)S(1)}, f32[512]{0:T(512)}, u32[]{:S(2)}) copy-start(f32[512]{0:T(512)} %param.8) | copy-start | bytes 6148
  52.9 12.9 %all-to-all-start.1 = ((f32[16,4,512]{2,1,0:T(4,128)}), f32[16,4,512]{2,1,0:T(4,128)S(1)}, u32[]{:S(2)}, u32[]{:S(2)}) async-start(f32[16,4,512]{2,1,0:T(4,128)} %get-tuple-element.25), calls=%async_computation.1 | async-start | bytes 262144 | tf_op jit(solution)/shard_map/all_to_all | solution.py:404
  66.9 19.3 %all-to-all-start.2 = ((bf16[32,4,640]{2,1,0:T(4,128)(2,1)}), bf16[32,4,640]{2,1,0:T(4,128)(2,1)S(1)}, u32[]{:S(2)}, u32[]{:S(2)}) async-start(bf16[32,4,640]{2,1,0:T(4,128)(2,1)} %broadcast_in_dim.16), calls=%async_computation.2 | async-start | bytes 327680 | tf_op jit(solution)/shard_map/all_to_all | solution.py:407

commit v7 on v6

--- a/solution.py
+++ b/solution.py
@@ -148,37 +148,49 @@
     )(xh, xl, order)
 
 
-def repeat_kernel(value_ref, out_ref):
-    for p in range(out_ref.shape[0]):
-        out_ref[p] = value_ref[...]
+def repeat_kernel(value_hbm, out_hbm, value, sems):
+    get = pltpu.make_async_copy(value_hbm, value, sems.at[0])
+    get.start()
+    get.wait()
+    puts = [pltpu.make_async_copy(value, out_hbm.at[p], sems.at[p + 1]) for p in range(out_hbm.shape[0])]
+    for put in puts:
+        put.start()
+    for put in puts:
+        put.wait()
 
 
 def repeat(value, count):
-    vmem = pl.BlockSpec(memory_space=pltpu.VMEM)
+    anywhere = pl.BlockSpec(memory_space=pl.ANY)
     return pl.pallas_call(
         repeat_kernel,
         out_shape=jax.ShapeDtypeStruct((count,) + value.shape, value.dtype),
-        in_specs=[vmem],
-        out_specs=vmem,
-        compiler_params=pltpu.CompilerParams(vmem_limit_bytes=8 * 1024 * 1024),
+        in_specs=[anywhere],
+        out_specs=anywhere,
+        scratch_shapes=[pltpu.VMEM(value.shape, value.dtype), pltpu.SemaphoreType.DMA((count + 1,))],
+        compiler_params=pltpu.CompilerParams(vmem_limit_bytes=56 * 1024 * 1024),
     )(value)
 
 
-def output_kernel(got_ref, answer_ref, resid_ref):
-    rows = got_ref.shape[2]
-    for p in range(got_ref.shape[0]):
-        answer_ref[p * rows : (p + 1) * rows, :] = got_ref[p, 0].astype(f32)
-        resid_ref[p * rows : (p + 1) * rows, :] = got_ref[p, 1].astype(f32)
+def output_kernel(got_ref, answer_hbm, resid_hbm, value, sems):
+    rows, puts = got_ref.shape[2], []
+    for k, out in enumerate((answer_hbm, resid_hbm)):
+        for p in range(got_ref.shape[0]):
+            value[k, p * rows : (p + 1) * rows, :] = got_ref[p, k].astype(f32)
+        puts.append(pltpu.make_async_copy(value.at[k], out, sems.at[k]))
+        puts[k].start()
+    for put in puts:
+        put.wait()
 
 
 def outputs(got):
     parts, _, rows, count = got.shape
-    vmem = pl.BlockSpec(memory_space=pltpu.VMEM)
     return pl.pallas_call(
         output_kernel,
         out_shape=[jax.ShapeDtypeStruct((parts * rows, count), f32)] * 2,
-        in_specs=[vmem],
-        out_specs=[vmem] * 2,
+        in_specs=[pl.BlockSpec(memory_space=pltpu.VMEM)],
+        out_specs=[pl.BlockSpec(memory_space=pl.ANY)] * 2,
+        scratch_shapes=[pltpu.VMEM((2, parts * rows, count), f32), pltpu.SemaphoreType.DMA((2,))],
+        compiler_params=pltpu.CompilerParams(vmem_limit_bytes=8 * 1024 * 1024),
     )(got)
 
 
@@ -242,6 +254,79 @@
     return row_sum(jnp.where(at == k, value, 0.0))
 
 
+def lanes_of(values):
+    at = lax.broadcasted_iota(jnp.int32, (values[0].shape[0], SLOTS), 1)
+    total = jnp.zeros(at.shape, f32)
+    for k, value in enumerate(values):
+        for piece in range(3):
+            part = value.astype(bf16).astype(f32)
+            total = jnp.where(at == 3 * k + piece, part, total)
+            value = value - part
+    return total
+
+
+def summed(ref):
+    total = ref[0].astype(f32)
+    for p in range(1, ref.shape[0]):
+        total = total + ref[p].astype(f32)
+    return total
+
+
+def spread(send_ref, value, dots):
+    sent = jnp.concatenate([value, lanes_of(dots)], 1).astype(bf16)
+    for p in range(send_ref.shape[0]):
+        send_ref[p] = sent
+
+
+def first_send_kernel(got_ref, scale_ref, value_ref, send_ref):
+    value = summed(got_ref)
+    value_ref[...] = value
+    spread(send_ref, value, [row_sum(scale_ref[...] * value * value)])
+
+
+def step_send_kernel(got_ref, scale_ref, direction_ref, resid_ref, value_ref, send_ref):
+    direction = direction_ref[...]
+    value = summed(got_ref) + RIDGE * direction
+    value_ref[...] = value
+    weighted = scale_ref[...] * value
+    spread(
+        send_ref, value, [row_sum(direction * value), row_sum(weighted * resid_ref[...]), row_sum(weighted * value)]
+    )
+
+
+def run_send(kernel, n_sk, got, *operands):
+    _, rows, count = got.shape
+    vmem = pl.BlockSpec(memory_space=pltpu.VMEM)
+    return pl.pallas_call(
+        kernel,
+        out_shape=[
+            jax.ShapeDtypeStruct((rows, count), f32),
+            jax.ShapeDtypeStruct((n_sk, rows, count + SLOTS), bf16),
+        ],
+        in_specs=[vmem] * (1 + len(operands)),
+        out_specs=[vmem] * 2,
+        compiler_params=pltpu.CompilerParams(vmem_limit_bytes=8 * 1024 * 1024),
+    )(got, *operands)
+
+
+def last_u_kernel(share, got_ref, send_ref):
+    total = summed(got_ref)
+    n = total.shape[1] - SLOTS
+    u = total[:, :n].astype(bf16).astype(f32)
+    spread(send_ref, u, [row_sum(total[:, :n] * u) + share * row_sum(total[:, n:])])
+
+
+def run_last_u(share, got):
+    vmem = pl.BlockSpec(memory_space=pltpu.VMEM)
+    return pl.pallas_call(
+        functools.partial(last_u_kernel, share),
+        out_shape=jax.ShapeDtypeStruct(got.shape, bf16),
+        in_specs=[vmem],
+        out_specs=vmem,
+        compiler_params=pltpu.CompilerParams(vmem_limit_bytes=8 * 1024 * 1024),
+    )(got)
+
+
 def gathered(got_ref, halves, count):
     parts = []
     for h in range(halves):
@@ -257,6 +342,14 @@
     return parts, sums
 
 
+def fetch_blocks(low_hbm, low, sems):
+    spans = [pl.ds(at, BLOCK) for at in range(0, low.shape[0], BLOCK)]
+    copies = [pltpu.make_async_copy(low_hbm.at[span], low.at[span], sems.at[k]) for k, span in enumerate(spans)]
+    for copy in copies:
+        copy.start()
+    return copies
+
+
 def coarse(parts, inverse):
     high_ref, low_ref, fetch = inverse
     rows, sides = parts[0].shape[0], []
@@ -273,7 +366,8 @@
     for b in blocks:
         one = sum(times(high_ref, sides[a], a, b) for a in blocks)
         solved.append(one[:rows] + one[rows:])
-    fetch.wait()
+    for copy in fetch:
+        copy.wait()
     for b in blocks:
         solved[b] = solved[b] + sum(times(low_ref, sides[a], a, b) for a in blocks)[:rows]
     return jnp.concatenate(solved, 1)
@@ -293,12 +387,10 @@
 
 
 def first_kernel(
-    factor, parity_ref, got_ref, high_ref, low_hbm, resid_ref, scale_ref, dir_ref, send_ref, rho_ref, dots_ref, low, sem
+    factor, parity_ref, got_ref, high_ref, low_hbm, resid_ref, scale_ref, dir_ref, send_ref, rho_ref, dots_ref, low, sems
 ):
     count = resid_ref.shape[1]
-    fetch = pltpu.make_async_copy(low_hbm, low, sem)
-    fetch.start()
-    inverse = high_ref, low, fetch
+    inverse = high_ref, low, fetch_blocks(low_hbm, low, sems)
     parts, sums = gathered(got_ref, rho_ref.shape[1] // count, count)
     parts = [part * factor for part in parts]
     product, direction = next_direction(
@@ -315,12 +407,10 @@
 
 def step_kernel(
     factor, parity_ref, got_ref, high_ref, low_hbm, resid_ref, scale_ref, image_ref, old_ref, rho_ref, dots_ref, answer_ref,
-    dir_ref, send_ref, new_rho_ref, new_dots_ref, new_resid_ref, new_answer_ref, low, sem,
+    dir_ref, send_ref, new_rho_ref, new_dots_ref, new_resid_ref, new_answer_ref, low, sems,
 ):
     count = resid_ref.shape[1]
-    fetch = pltpu.make_async_copy(low_hbm, low, sem)
-    fetch.start()
-    inverse = high_ref, low, fetch
+    inverse = high_ref, low, fetch_blocks(low_hbm, low, sems)
     parts, sums = gathered(got_ref, rho_ref.shape[1] // count, count)
     energy, product = lane(dots_ref[...], 0), lane(dots_ref[...], 1)
     alpha = product / sums[0]
@@ -359,20 +449,23 @@
         in_specs=[pl.BlockSpec(memory_space=pltpu.SMEM), vmem, vmem, pl.BlockSpec(memory_space=pl.ANY)]
         + [vmem] * (len(operands) - 3),
         out_specs=[vmem] * len(outs),
-        scratch_shapes=[pltpu.VMEM(operands[2].shape, bf16), pltpu.SemaphoreType.DMA],
+        scratch_shapes=[
+            pltpu.VMEM(operands[2].shape, bf16),
+            pltpu.SemaphoreType.DMA((operands[2].shape[0] // BLOCK,)),
+        ],
         compiler_params=pltpu.CompilerParams(vmem_limit_bytes=52 * 1024 * 1024),
         cost_estimate=pl.CostEstimate(flops=10**8, bytes_accessed=5 * 2**20, transcendentals=0),
     )(parity, *operands)
+
+
+def rounded(value):
+    return lax.reduce_precision(value, 8, 7).astype(bf16)
 
 
 def triple(value):
     high = lax.reduce_precision(value, 8, 7)
     mid = lax.reduce_precision(value - high, 8, 7)
     return jnp.stack([high, mid, value - high - mid], -1).astype(bf16)
-
-
-def rounded(value):
-    return lax.reduce_precision(value, 8, 7).astype(bf16)
 
 
 def slots(values):
@@ -401,22 +494,19 @@
     feat, part = make_features(core, samples, mine_proj, other_proj, targets.T, n_dp)
 
     def scatter_dp(value):
-        return jnp.sum(lax.all_to_all(value, DP, 0, 0), 0)
+        return lax.all_to_all(value, DP, 0, 0)
 
     def gather_sk(value):
         return lax.all_to_all(jnp.broadcast_to(value[None], (n_sk,) + value.shape), "sketch", 0, 0)
-
-    def everywhere(value, dots):
-        return gather_sk(jnp.concatenate([value.astype(bf16), slots(dots)], 1))
 
     def forward(send):
         whole = lax.all_to_all(send, DP, 0, 0).reshape(width, count)
         sums = lax.dot_general(whole, feat, (((1,), (1,)), ((), ())), preferred_element_type=f32)
         return whole, sums.astype(bf16).reshape(n_sk, cols, n)
 
-    resid = scatter_dp(part)
+    resid, sent = run_send(first_send_kernel, n_sk, scatter_dp(part), scale)
     inv_high, inv_low = coarse_inverse(factor_high, factor_low, resid)
-    got = everywhere(resid, row_sum(scale * resid * resid))
+    got = lax.all_to_all(sent, "sketch", 0, 0)
     direction, send, rho, dots = run_coarse(
         first_kernel, factor, n_dp, parity, got, inv_high, inv_low, resid, scale
     )
@@ -425,25 +515,18 @@
         _, sums = forward(send)
         u = rounded(jnp.sum(lax.all_to_all(sums, "sketch", 0, 0).astype(f32), 0))
         whole = gather_sk(u).reshape(width, n)
-        image = scatter_dp(dot(whole, feat).reshape(n_dp, mine, count)) + RIDGE * direction
-        weighted = scale * image
-        got = everywhere(
-            image,
-            jnp.concatenate(
-                [row_sum(direction * image), row_sum(weighted * resid), row_sum(weighted * image)], 1
-            ),
-        )
+        parts = scatter_dp(dot(whole, feat).reshape(n_dp, mine, count))
+        image, sent = run_send(step_send_kernel, n_sk, parts, scale, direction, resid)
+        got = lax.all_to_all(sent, "sketch", 0, 0)
         direction, send, rho, dots, resid, answer = run_coarse(
             step_kernel, factor, n_dp, parity, got, inv_high, inv_low, resid, scale, image, direction, rho, dots, answer,
             more=2,
         )
     whole, sums = forward(send)
     squares = jnp.sum(jnp.square(whole.astype(f32)), 1).reshape(n_sk, cols, 1)
-    got = lax.all_to_all(jnp.concatenate([sums, slots(squares)], 2), "sketch", 0, 0).astype(f32)
-    total = jnp.sum(got, 0)
-    u = rounded(total[:, :n])
-    curve = row_sum(total[:, :n] * u.astype(f32)) + (RIDGE / n_dp) * row_sum(total[:, n:])
-    got = gather_sk(jnp.concatenate([u, slots(curve)], 1)).reshape(width, n + SLOTS)
+    got = lax.all_to_all(jnp.concatenate([sums, slots(squares)], 2), "sketch", 0, 0)
+    sent = run_last_u(RIDGE / n_dp, got)
+    got = lax.all_to_all(sent, "sketch", 0, 0).reshape(width, n + SLOTS)
     image = dot(got[:, :n], feat)
     sent = jnp.concatenate([image.astype(bf16), got[:, n:]], 1)
     got = lax.all_to_all(sent.reshape(n_dp, mine, count + SLOTS), DP, 0, 0).astype(f32)

time: 227 us -> 225 us (level)
    all_to_all x3 -> x1, blocking collectives: 39.9 us -> 13.4 us  [gather_sk(): lax.all_to_all(jnp.broadcast_to(value[None], (n_sk,) + value.shape), 'ske...]
    all_to_all x1 -> x3, blocking collectives: 14.4 us -> 40.8 us  [the longest x1 14.2 us: scatter_dp(): return lax.all_to_all(value, DP, 0, 0)]
where the time goes in v7:
time: 225 us
  blocking collectives  129 us (57%)
  Pallas kernels  33.6 us (15%)
  waiting for transfers between devices  29.2 us (13%)
  starting transfers between devices  26.6 us (12%)
  local copies, waits for them, and re-layouts  2.5 us (1%)
    all_to_all x2, blocking collectives, forward(): whole = lax.all_to_all(send, DP, 0, 0).reshape(width, count)  23.9 us
    pallas_call x1, Pallas kernels, coarse_factor_inverse(): pl.pallas_call(inverse_kernel, out_shape=[jax.ShapeDtypeStruct((n, n), bf...  15.5 us
    all_to_all x1, blocking collectives, scatter_dp(): return lax.all_to_all(value, DP, 0, 0)  14.2 us
    all_to_all x1, blocking collectives, body(): got = lax.all_to_all(sent, 'sketch', 0, 0).reshape(width, n + SLOTS)  13.8 us
    all_to_all x1, waiting for transfers between devices, body(): lax.all_to_all(repeat(projections, lax.axis_size('z')), 'z', 0, 0)  13.7 us
    all_to_all x1, blocking collectives, gather_sk(): lax.all_to_all(jnp.broadcast_to(value[None], (n_sk,) + value.shape), 'ske...  13.4 us
    all_to_all x1, blocking collectives, body(): lax.all_to_all(sent.reshape(n_dp, mine, count + SLOTS), DP, 0, 0)  13.3 us
    all_to_all x1, blocking collectives, body(): lax.all_to_all(jnp.concatenate([sums, slots(squares)], 2), 'sketch', 0, 0)  13.1 us
  transfers between devices with their start and end apart: 4, of which 4 were waited for; matrix products, arithmetic and copies ran while one was open for 0% of the time, Pallas kernels for 9%

profile of v7, /device:TPU:1, one launch (start us, length us, event | category | flops | bytes accessed | tf_op | source)
XLA Modules:
  0.0 224.6 jit_solution(2985319514348247328)
XLA Ops:
  0.6 2.0 shard_map.68
  2.6 10.9 %all-to-all-start = ((bf16[8,4,32,512]{3,2,1,0:T(8,128)(2,1)}), bf16[8,4,32,512]{3,2,1,0:T(8,128)(2,1)S(1)}, u32[]{:S(2)}, u32[]{:S(2)}) async-start(bf16[8,4,32,512]{3,2,1,0:T(8,128)(2,1)} %shard_map.68), calls=%async_computation | async-start | bytes 2097152 | tf_op jit(solution)/shard_map/all_to_all | solution.py:490
  13.5 15.5 %shard_map.69 = (bf16[1024,1024]{1,0:T(8,128)(2,1)}, bf16[1024,1024]{1,0:T(8,128)(2,1)}, s32[1]{0:T(128)}) custom-call(s32[1]{0:T(128)} %bitcast.1.core_ref, bf16[1024,1024]{1,0:T(8,128)(2,1)} %lower_hbm.1), custom_call_target="tpu_custom_call" | custom-call | flops 10000000000 | bytes 6291456 | tf_op jit(solution)/shard_map/pallas_call | solution.py:103
  29.0 13.7 %all-to-all-done.mine_ref = bf16[8,4,32,512]{3,2,1,0:T(8,128)(2,1)S(1)} async-done(((bf16[8,4,32,512]{3,2,1,0:T(8,128)(2,1)}), bf16[8,4,32,512]{3,2,1,0:T(8,128)(2,1)S(1)}, u32[]{:S(2)}, u32[]{:S(2)}) %all-to-all-start) | async-done | bytes 1048608 | tf_op jit(solution)/shard_map/all_to_all | solution.py:490
  42.7 2.4 %collective-permute-start = (bf16[8,4,32,512]{3,2,1,0:T(8,128)(2,1)S(1)}, bf16[8,4,32,512]{3,2,1,0:T(8,128)(2,1)S(1)}, u32[]{:S(2)}, u32[]{:S(2)}) collective-permute-start(bf16[8,4,32,512]{3,2,1,0:T(8,128)(2,1)S(1)} %all-to-all-done.mine_ref), channel_id=1, source_target_pairs={{0,32},{32,0},{1,33},{33,1},{2,34},{34,2},{3,35},{35,3},{4,36},{36... | collective-permute-start | bytes 3145736 | tf_op jit(solution)/shard_map/ppermute | solution.py:493
  45.1 2.3 %collective-permute-done.other_ref = bf16[8,4,32,512]{3,2,1,0:T(8,128)(2,1)S(1)} collective-permute-done((bf16[8,4,32,512]{3,2,1,0:T(8,128)(2,1)S(1)}, bf16[8,4,32,512]{3,2,1,0:T(8,128)(2,1)S(1)}, u32[]{:S(2)}, u32[]{:S(2)}) %collective-permute-start) | collective-permute-done | bytes 1048608 | tf_op jit(solution)/shard_map/ppermute | solution.py:493
  48.6 4.3 %shard_map.70 = (bf16[1024,512]{1,0:T(8,128)(2,1)S(1)}, f32[16,4,512]{2,1,0:T(4,128)}) custom-call(s32[1]{0:T(128)} %get-tuple-element.27.core_ref, bf16[1024,512]{1,0:T(8,128)(2,1)S(1)} %copy-done.1, bf16[8,4,32,512]{3,2,1,0:T(8,128)(2,1)S(1)} %all-to-all-done.mine_ref, bf16[8,4,32,512]{3,2,1,0:T(8,128)(2,1)S(1)} %collective-permute-done.other_ref, ...), custom_call_target="tpu_custom_call" | custom-call | flops 2000000000 | bytes 5242880 | tf_op jit(solution)/shard_map/pallas_call | solution.py:226
  52.9 3.7 %all-to-all-start.1 = ((f32[16,4,512]{2,1,0:T(4,128)}), f32[16,4,512]{2,1,0:T(4,128)S(1)}, u32[]{:S(2)}, u32[]{:S(2)}) async-start(f32[16,4,512]{2,1,0:T(4,128)} %get-tuple-element.29), calls=%async_computation.1 | async-start | bytes 262144 | tf_op jit(solution)/shard_map/all_to_all | solution.py:497
  56.6 9.2 %all-to-all-done.1.got_ref = f32[16,4,512]{2,1,0:T(4,128)S(1)} async-done(((f32[16,4,512]{2,1,0:T(4,128)}), f32[16,4,512]{2,1,0:T(4,128)S(1)}, u32[]{:S(2)}, u32[]{:S(2)}) %all-to-all-start.1) | async-done | bytes 131104 | tf_op jit(solution)/shard_map/all_to_all | solution.py:497
  66.6 9.7 %all-to-all-start.2 = ((bf16[32,4,640]{2,1,0:T(4,128)(2,1)}), bf16[32,4,640]{2,1,0:T(4,128)(2,1)S(1)}, u32[]{:S(2)}, u32[]{:S(2)}) async-start(bf16[32,4,640]{2,1,0:T(4,128)(2,1)} %get-tuple-element.30), calls=%async_computation.2 | async-start | bytes 327680 | tf_op jit(solution)/shard_map/all_to_all | solution.py:509
  76.3 5.6 %shard_map.72 = (bf16[2560,256]{1,0:T(8,128)(2,1)S(1)}, bf16[2560,256]{1,0:T(8,128)(2,1)}) custom-call(bf16[1024,1024]{1,0:T(8,128)(2,1)} %get-tuple-element.31.xh_ref, bf16[1024,1024]{1,0:T(8,128)(2,1)} %get-tuple-element.32.xl_ref, f32[4,512]{1,0:T(4,128)S(1)} %get-tuple-element.33.order_hbm.resid_ref), custom_call_target="tpu_custom_call" | custom-call | flops 4000000000 | bytes 8388608 | tf_op jit(solution)/shard_map/pallas_call | solution.py:141
  81.8 4.1 %all-to-all-done.2.got_ref = bf16[32,4,640]{2,1,0:T(4,128)(2,1)S(1)} async-done(((bf16[32,4,640]{2,1,0:T(4,128)(2,1)}), bf16[32,4,640]{2,1,0:T(4,128)(2,1)S(1)}, u32[]{:S(2)}, u32[]{:S(2)}) %all-to-all-start.2) | async-done | bytes 163872 | tf_op jit(solution)/shard_map/all_to_all | solution.py:509
  85.9 2.2 shard_map.73
  88.1 12.0 %all_to_all.65 = bf16[16,4,512]{2,1,0:T(4,128)(2,1)S(1)} all-to-all(bf16[16,4,512]{2,1,0:T(4,128)(2,1)S(1)} %get-tuple-element.36), channel_id=1, replica_groups=mesh['z'=8,'core'=2,'sketch'=32] {'z','core'}, dimensions={0} | all-to-all | bytes 131072 | tf_op jit(solution)/shard_map/all_to_all | solution.py:503
  100.6 13.0 %all_to_all.66 = bf16[32,2,1024]{2,1,0:T(2,128)(2,1)S(1)} all-to-all(bf16[32,2,1024]{2,1,0:T(2,128)(2,1)S(1)} %reshape.135), channel_id=1, replica_groups=mesh['z'=8,'core'=2,'sketch'=32] {'sketch'}, dimensions={0} | all-to-all | bytes 262144 | tf_op jit(solution)/shard_map/all_to_all | solution.py:516
  113.9 13.4 %all_to_all.67 = bf16[32,2,1024]{2,1,0:T(2,128)(2,1)S(1)} all-to-all(bf16[32,2,1024]{2,1,0:T(2,128)(2,1)S(1)} %broadcast_in_dim.22), channel_id=1, replica_groups=mesh['z'=8,'core'=2,'sketch'=32] {'sketch'}, dimensions={0} | all-to-all | bytes 262144 | tf_op jit(solution)/shard_map/all_to_all | solution.py:500
  127.7 14.2 %all_to_all.68.got_ref = f32[16,4,512]{2,1,0:T(4,128)S(1)} all-to-all(f32[16,4,512]{2,1,0:T(4,128)S(1)} %copy.29), channel_id=1, replica_groups=mesh['z'=8,'core'=2,'sketch'=32] {'z','core'}, dimensions={0} | all-to-all | bytes 262144 | tf_op jit(solution)/shard_map/all_to_all | solution.py:497
  142.1 12.8 %all_to_all.69.got_ref = bf16[32,4,640]{2,1,0:T(4,128)(2,1)S(1)} all-to-all(bf16[32,4,640]{2,1,0:T(4,128)(2,1)S(1)} %get-tuple-element.39), channel_id=1, replica_groups=mesh['z'=8,'core'=2,'sketch'=32] {'sketch'}, dimensions={0} | all-to-all | bytes 327680 | tf_op jit(solution)/shard_map/all_to_all | solution.py:520
  154.9 2.2 shard_map.75
  157.1 12.0 %all_to_all.70 = bf16[16,4,512]{2,1,0:T(4,128)(2,1)S(1)} all-to-all(bf16[16,4,512]{2,1,0:T(4,128)(2,1)S(1)} %get-tuple-element.45), channel_id=1, replica_groups=mesh['z'=8,'core'=2,'sketch'=32] {'z','core'}, dimensions={0} | all-to-all | bytes 131072 | tf_op jit(solution)/shard_map/all_to_all | solution.py:503
  170.7 13.1 %all_to_all.71.got_ref = bf16[32,2,1152]{2,1,0:T(2,128)(2,1)S(1)} all-to-all(bf16[32,2,1152]{2,1,0:T(2,128)(2,1)S(1)} %pad_maximum_fusion), channel_id=1, replica_groups=mesh['z'=8,'core'=2,'sketch'=32] {'sketch'}, dimensions={0} | all-to-all | bytes 294912 | tf_op jit(solution)/shard_map/all_to_all | solution.py:527
  184.0 13.8 %all_to_all.72 = bf16[32,2,1152]{2,1,0:T(2,128)(2,1)S(1)} all-to-all(bf16[32,2,1152]{2,1,0:T(2,128)(2,1)S(1)} %shard_map.76), channel_id=1, replica_groups=mesh['z'=8,'core'=2,'sketch'=32] {'sketch'}, dimensions={0} | all-to-all | bytes 294912 | tf_op jit(solution)/shard_map/all_to_all | solution.py:529
  198.1 13.3 %all_to_all.73 = bf16[16,4,640]{2,1,0:T(4,128)(2,1)S(1)} all-to-all(bf16[16,4,640]{2,1,0:T(4,128)(2,1)S(1)} %reshape.140), channel_id=1, replica_groups=mesh['z'=8,'core'=2,'sketch'=32] {'z','core'}, dimensions={0} | all-to-all | bytes 163840 | tf_op jit(solution)/shard_map/all_to_all | solution.py:532
  212.0 11.7 %all_to_all.74.got_ref = bf16[16,2,4,512]{3,2,1,0:T(4,128)(2,1)S(1)} all-to-all(bf16[16,2,4,512]{3,2,1,0:T(4,128)(2,1)S(1)} %broadcast_in_dim.25), channel_id=1, replica_groups=mesh['z'=8,'core'=2,'sketch'=32] {'z','core'}, dimensions={0} | all-to-all | bytes 262144 | tf_op jit(solution)/shard_map/all_to_all | solution.py:537
  (45 shorter events, 6.8 us)
Async XLA Ops:
  2.6 40.1 %all-to-all-start = ((bf16[8,4,32,512]{3,2,1,0:T(8,128)(2,1)}), bf16[8,4,32,512]{3,2,1,0:T(8,128)(2,1)S(1)}, u32[]{:S(2)}, u32[]{:S(2)}) async-start(bf16[8,4,32,512]{3,2,1,0:T(8,128)(2,1)} %shard_map.68), calls=%async_computation | async-start | bytes 2097152 | tf_op jit(solution)/shard_map/all_to_all | solution.py:490
  13.5 33.9 %copy-start.2 = (bf16[1024,64]{0,1:T(8,128)(2,1)S(1)}, bf16[1024,64]{0,1:T(8,128)(2,1)}, u32[]{:S(2)}) copy-start(bf16[1024,64]{0,1:T(8,128)(2,1)} %param.7) | copy-start | bytes 393220
  42.7 4.7 %collective-permute-start = (bf16[8,4,32,512]{3,2,1,0:T(8,128)(2,1)S(1)}, bf16[8,4,32,512]{3,2,1,0:T(8,128)(2,1)S(1)}, u32[]{:S(2)}, u32[]{:S(2)}) collective-permute-start(bf16[8,4,32,512]{3,2,1,0:T(8,128)(2,1)S(1)} %all-to-all-done.mine_ref), channel_id=1, source_target_pairs={{0,32},{32,0},{1,33},{33,1},{2,34},{34,2},{3,35},{35,3},{4,36},{36... | collective-permute-start | bytes 3145736 | tf_op jit(solution)/shard_map/ppermute | solution.py:493
  47.3 1.2 copy-start.1
  48.6 17.3 %copy-start = (f32[512]{0:T(512)S(1)}, f32[512]{0:T(512)}, u32[]{:S(2)}) copy-start(f32[512]{0:T(512)} %param.8) | copy-start | bytes 6148
  52.9 12.9 %all-to-all-start.1 = ((f32[16,4,512]{2,1,0:T(4,128)}), f32[16,4,512]{2,1,0:T(4,128)S(1)}, u32[]{:S(2)}, u32[]{:S(2)}) async-start(f32[16,4,512]{2,1,0:T(4,128)} %get-tuple-element.29), calls=%async_computation.1 | async-start | bytes 262144 | tf_op jit(solution)/shard_map/all_to_all | solution.py:497
  66.6 19.3 %all-to-all-start.2 = ((bf16[32,4,640]{2,1,0:T(4,128)(2,1)}), bf16[32,4,640]{2,1,0:T(4,128)(2,1)S(1)}, u32[]{:S(2)}, u32[]{:S(2)}) async-start(bf16[32,4,640]{2,1,0:T(4,128)(2,1)} %get-tuple-element.30), calls=%async_computation.2 | async-start | bytes 327680 | tf_op jit(solution)/shard_map/all_to_all | solution.py:509

commit v8 on v7

--- a/solution.py
+++ b/solution.py
@@ -194,25 +194,17 @@
     )(got)
 
 
-def feature_kernel(
-    core_ref, samples_hbm, mine_ref, other_ref, targets_hbm, feat_ref, part_ref, proj, samples_ref, targets_ref, sems
-):
+def feature_kernel(core_ref, samples_ref, mine_ref, other_ref, targets_ref, feat_ref, part_ref, proj):
     core = core_ref[0]
-    get_samples = pltpu.make_async_copy(samples_hbm, samples_ref, sems.at[0])
-    get_targets = pltpu.make_async_copy(targets_hbm, targets_ref, sems.at[1])
-    get_samples.start()
-    get_targets.start()
     for j in range(proj.shape[0]):
         proj[j, :, core] = mine_ref[:, j]
         proj[j, :, 1 - core] = other_ref[:, j]
-    get_samples.wait()
     samples, value = samples_ref[...], None
     for j in range(proj.shape[0]):
         panel = dot(samples, proj[j].reshape(samples.shape[1], proj.shape[-1]))
         value = panel if value is None else value * panel
     feat = (value * (1.0 / math.sqrt(F))).astype(bf16)
     feat_ref[...] = feat
-    get_targets.wait()
     total = dot(targets_ref[...], feat)
     step = part_ref.shape[1]
     for p in range(part_ref.shape[0]):
@@ -222,21 +214,16 @@
 def make_features(core, samples, mine, other, targets_t, parts):
     n = samples.shape[0]
     chips, panels, rows, width = mine.shape
-    vmem, anywhere = pl.BlockSpec(memory_space=pltpu.VMEM), pl.BlockSpec(memory_space=pl.ANY)
+    vmem = pl.BlockSpec(memory_space=pltpu.VMEM)
     return pl.pallas_call(
         feature_kernel,
         out_shape=[
             jax.ShapeDtypeStruct((n, width), bf16),
             jax.ShapeDtypeStruct((parts, targets_t.shape[0] // parts, width), f32),
         ],
-        in_specs=[pl.BlockSpec(memory_space=pltpu.SMEM), anywhere, vmem, vmem, anywhere],
+        in_specs=[pl.BlockSpec(memory_space=pltpu.SMEM)] + [vmem] * 4,
         out_specs=[vmem] * 2,
-        scratch_shapes=[
-            pltpu.VMEM((panels, chips, 2, rows, width), bf16),
-            pltpu.VMEM(samples.shape, bf16),
-            pltpu.VMEM(targets_t.shape, bf16),
-            pltpu.SemaphoreType.DMA((2,)),
-        ],
+        scratch_shapes=[pltpu.VMEM((panels, chips, 2, rows, width), bf16)],
         compiler_params=pltpu.CompilerParams(vmem_limit_bytes=49 * 1024 * 1024),
         cost_estimate=pl.CostEstimate(flops=2 * 10**9, bytes_accessed=5 * 2**20, transcendentals=0),
     )(core, samples, mine, other, targets_t)
@@ -307,6 +294,27 @@
         out_specs=[vmem] * 2,
         compiler_params=pltpu.CompilerParams(vmem_limit_bytes=8 * 1024 * 1024),
     )(got, *operands)
+
+
+def last_sums_kernel(whole_ref, sums_ref, send_ref):
+    parts, rows, cols = whole_ref.shape[0], whole_ref.shape[1], send_ref.shape[1]
+    for p in range(parts):
+        value = whole_ref[p].astype(f32)
+        sent = jnp.concatenate([sums_ref[p * rows : (p + 1) * rows, :], lanes_of([row_sum(value * value)])], 1)
+        for k in range(rows // cols):
+            send_ref[p * (rows // cols) + k] = sent[k * cols : (k + 1) * cols, :].astype(bf16)
+
+
+def run_last_sums(n_sk, whole, sums):
+    width, n = sums.shape
+    vmem = pl.BlockSpec(memory_space=pltpu.VMEM)
+    return pl.pallas_call(
+        last_sums_kernel,
+        out_shape=jax.ShapeDtypeStruct((n_sk, width // n_sk, n + SLOTS), bf16),
+        in_specs=[vmem] * 2,
+        out_specs=vmem,
+        compiler_params=pltpu.CompilerParams(vmem_limit_bytes=8 * 1024 * 1024),
+    )(whole, sums)
 
 
 def last_u_kernel(share, got_ref, send_ref):
@@ -342,16 +350,8 @@
     return parts, sums
 
 
-def fetch_blocks(low_hbm, low, sems):
-    spans = [pl.ds(at, BLOCK) for at in range(0, low.shape[0], BLOCK)]
-    copies = [pltpu.make_async_copy(low_hbm.at[span], low.at[span], sems.at[k]) for k, span in enumerate(spans)]
-    for copy in copies:
-        copy.start()
-    return copies
-
-
 def coarse(parts, inverse):
-    high_ref, low_ref, fetch = inverse
+    high_ref, low_ref = inverse
     rows, sides = parts[0].shape[0], []
     for part in parts:
         high = part.astype(bf16).astype(f32)
@@ -366,8 +366,6 @@
     for b in blocks:
         one = sum(times(high_ref, sides[a], a, b) for a in blocks)
         solved.append(one[:rows] + one[rows:])
-    for copy in fetch:
-        copy.wait()
     for b in blocks:
         solved[b] = solved[b] + sum(times(low_ref, sides[a], a, b) for a in blocks)[:rows]
     return jnp.concatenate(solved, 1)
@@ -387,10 +385,10 @@
 
 
 def first_kernel(
-    factor, parity_ref, got_ref, high_ref, low_hbm, resid_ref, scale_ref, dir_ref, send_ref, rho_ref, dots_ref, low, sems
+    factor, parity_ref, got_ref, high_ref, low_ref, resid_ref, scale_ref, dir_ref, send_ref, rho_ref, dots_ref
 ):
     count = resid_ref.shape[1]
-    inverse = high_ref, low, fetch_blocks(low_hbm, low, sems)
+    inverse = high_ref, low_ref
     parts, sums = gathered(got_ref, rho_ref.shape[1] // count, count)
     parts = [part * factor for part in parts]
     product, direction = next_direction(
@@ -406,11 +404,11 @@
 
 
 def step_kernel(
-    factor, parity_ref, got_ref, high_ref, low_hbm, resid_ref, scale_ref, image_ref, old_ref, rho_ref, dots_ref, answer_ref,
-    dir_ref, send_ref, new_rho_ref, new_dots_ref, new_resid_ref, new_answer_ref, low, sems,
+    factor, parity_ref, got_ref, high_ref, low_ref, resid_ref, scale_ref, image_ref, old_ref, rho_ref, dots_ref, answer_ref,
+    dir_ref, send_ref, new_rho_ref, new_dots_ref, new_resid_ref, new_answer_ref,
 ):
     count = resid_ref.shape[1]
-    inverse = high_ref, low, fetch_blocks(low_hbm, low, sems)
+    inverse = high_ref, low_ref
     parts, sums = gathered(got_ref, rho_ref.shape[1] // count, count)
     energy, product = lane(dots_ref[...], 0), lane(dots_ref[...], 1)
     alpha = product / sums[0]
@@ -446,16 +444,15 @@
     return pl.pallas_call(
         functools.partial(kernel, factor),
         out_shape=outs,
-        in_specs=[pl.BlockSpec(memory_space=pltpu.SMEM), vmem, vmem, pl.BlockSpec(memory_space=pl.ANY)]
-        + [vmem] * (len(operands) - 3),
+        in_specs=[pl.BlockSpec(memory_space=pltpu.SMEM)] + [vmem] * len(operands),
         out_specs=[vmem] * len(outs),
-        scratch_shapes=[
-            pltpu.VMEM(operands[2].shape, bf16),
-            pltpu.SemaphoreType.DMA((operands[2].shape[0] // BLOCK,)),
-        ],
-        compiler_params=pltpu.CompilerParams(vmem_limit_bytes=52 * 1024 * 1024),
+        compiler_params=pltpu.CompilerParams(vmem_limit_bytes=50 * 1024 * 1024),
         cost_estimate=pl.CostEstimate(flops=10**8, bytes_accessed=5 * 2**20, transcendentals=0),
     )(parity, *operands)
+
+
+def rounded(value):
+    return lax.reduce_precision(value, 8, 7).astype(bf16)
 
 
 def rounded(value):
@@ -466,12 +463,6 @@
     high = lax.reduce_precision(value, 8, 7)
     mid = lax.reduce_precision(value - high, 8, 7)
     return jnp.stack([high, mid, value - high - mid], -1).astype(bf16)
-
-
-def slots(values):
-    parts = triple(values)
-    flat = parts.reshape(parts.shape[:-2] + (-1,))
-    return jnp.pad(flat, ((0, 0),) * (flat.ndim - 1) + ((0, SLOTS - flat.shape[-1]),))
 
 
 def body(samples, projections, targets, feature_scale, coarse_factor):
@@ -500,9 +491,8 @@
         return lax.all_to_all(jnp.broadcast_to(value[None], (n_sk,) + value.shape), "sketch", 0, 0)
 
     def forward(send):
-        whole = lax.all_to_all(send, DP, 0, 0).reshape(width, count)
-        sums = lax.dot_general(whole, feat, (((1,), (1,)), ((), ())), preferred_element_type=f32)
-        return whole, sums.astype(bf16).reshape(n_sk, cols, n)
+        whole = lax.all_to_all(send, DP, 0, 0)
+        return whole, dot_turned(whole.reshape(width, count), feat)
 
     resid, sent = run_send(first_send_kernel, n_sk, scatter_dp(part), scale)
     inv_high, inv_low = coarse_inverse(factor_high, factor_low, resid)
@@ -513,7 +503,8 @@
     answer = jnp.zeros_like(resid)
     for step in range(ITERS - 1):
         _, sums = forward(send)
-        u = rounded(jnp.sum(lax.all_to_all(sums, "sketch", 0, 0).astype(f32), 0))
+        sums = lax.all_to_all(sums.astype(bf16).reshape(n_sk, cols, n), "sketch", 0, 0)
+        u = rounded(jnp.sum(sums.astype(f32), 0))
         whole = gather_sk(u).reshape(width, n)
         parts = scatter_dp(dot(whole, feat).reshape(n_dp, mine, count))
         image, sent = run_send(step_send_kernel, n_sk, parts, scale, direction, resid)
@@ -523,8 +514,7 @@
             more=2,
         )
     whole, sums = forward(send)
-    squares = jnp.sum(jnp.square(whole.astype(f32)), 1).reshape(n_sk, cols, 1)
-    got = lax.all_to_all(jnp.concatenate([sums, slots(squares)], 2), "sketch", 0, 0)
+    got = lax.all_to_all(run_last_sums(n_sk, whole, sums), "sketch", 0, 0)
     sent = run_last_u(RIDGE / n_dp, got)
     got = lax.all_to_all(sent, "sketch", 0, 0).reshape(width, n + SLOTS)
     image = dot(got[:, :n], feat)

time: 225 us -> 223 us (level)
  no operation moved by 1% of the time
where the time goes in v8:
time: 223 us; the launch traced here: 222 us
  blocking collectives  129 us (58%)
  Pallas kernels  31.4 us (14%)
  waiting for transfers between devices  29.2 us (13%)
  starting transfers between devices  26.6 us (12%)
  local copies, waits for them, and re-layouts  3.09 us (1%)
    all_to_all x2, blocking collectives, forward(): whole = lax.all_to_all(send, DP, 0, 0)  23.9 us
    pallas_call x1, Pallas kernels, coarse_factor_inverse(): pl.pallas_call(inverse_kernel, out_shape=[jax.ShapeDtypeStruct((n, n), bf...  15.5 us
    all_to_all x1, blocking collectives, scatter_dp(): return lax.all_to_all(value, DP, 0, 0)  14.2 us
    all_to_all x1, blocking collectives, body(): got = lax.all_to_all(sent, 'sketch', 0, 0).reshape(width, n + SLOTS)  13.8 us
    all_to_all x1, waiting for transfers between devices, body(): lax.all_to_all(repeat(projections, lax.axis_size('z')), 'z', 0, 0)  13.7 us
    all_to_all x1, blocking collectives, gather_sk(): lax.all_to_all(jnp.broadcast_to(value[None], (n_sk,) + value.shape), 'ske...  13.4 us
    all_to_all x1, blocking collectives, body(): lax.all_to_all(sent.reshape(n_dp, mine, count + SLOTS), DP, 0, 0)  13.3 us
    all_to_all x1, blocking collectives, body(): got = lax.all_to_all(run_last_sums(n_sk, whole, sums), 'sketch', 0, 0)  13.1 us
  transfers between devices with their start and end apart: 4, of which 4 were waited for; matrix products, arithmetic and copies ran while one was open for 0% of the time, Pallas kernels for 9%

profile of v8, /device:TPU:1, one launch (start us, length us, event | category | flops | bytes accessed | tf_op | source)
XLA Modules:
  0.0 222.4 jit_solution(10248096600054914836)
XLA Ops:
  0.6 1.9 shard_map.68
  2.6 10.9 %all-to-all-start = ((bf16[8,4,32,512]{3,2,1,0:T(8,128)(2,1)}), bf16[8,4,32,512]{3,2,1,0:T(8,128)(2,1)S(1)}, u32[]{:S(2)}, u32[]{:S(2)}) async-start(bf16[8,4,32,512]{3,2,1,0:T(8,128)(2,1)} %shard_map.68), calls=%async_computation | async-start | bytes 2097152 | tf_op jit(solution)/shard_map/all_to_all | solution.py:481
  13.5 15.5 %shard_map.69 = (bf16[1024,1024]{1,0:T(8,128)(2,1)}, bf16[1024,1024]{1,0:T(8,128)(2,1)}, s32[1]{0:T(128)}) custom-call(s32[1]{0:T(128)} %bitcast.1.core_ref, bf16[1024,1024]{1,0:T(8,128)(2,1)} %lower_hbm.1), custom_call_target="tpu_custom_call" | custom-call | flops 10000000000 | bytes 6291456 | tf_op jit(solution)/shard_map/pallas_call | solution.py:103
  29.0 13.7 %all-to-all-done.mine_ref = bf16[8,4,32,512]{3,2,1,0:T(8,128)(2,1)S(1)} async-done(((bf16[8,4,32,512]{3,2,1,0:T(8,128)(2,1)}), bf16[8,4,32,512]{3,2,1,0:T(8,128)(2,1)S(1)}, u32[]{:S(2)}, u32[]{:S(2)}) %all-to-all-start) | async-done | bytes 1048608 | tf_op jit(solution)/shard_map/all_to_all | solution.py:481
  42.7 2.4 %collective-permute-start = (bf16[8,4,32,512]{3,2,1,0:T(8,128)(2,1)S(1)}, bf16[8,4,32,512]{3,2,1,0:T(8,128)(2,1)S(1)}, u32[]{:S(2)}, u32[]{:S(2)}) collective-permute-start(bf16[8,4,32,512]{3,2,1,0:T(8,128)(2,1)S(1)} %all-to-all-done.mine_ref), channel_id=1, source_target_pairs={{0,32},{32,0},{1,33},{33,1},{2,34},{34,2},{3,35},{35,3},{4,36},{36... | collective-permute-start | bytes 3145736 | tf_op jit(solution)/shard_map/ppermute | solution.py:484
  45.0 2.3 %collective-permute-done.other_ref = bf16[8,4,32,512]{3,2,1,0:T(8,128)(2,1)S(1)} collective-permute-done((bf16[8,4,32,512]{3,2,1,0:T(8,128)(2,1)S(1)}, bf16[8,4,32,512]{3,2,1,0:T(8,128)(2,1)S(1)}, u32[]{:S(2)}, u32[]{:S(2)}) %collective-permute-start) | collective-permute-done | bytes 1048608 | tf_op jit(solution)/shard_map/ppermute | solution.py:484
  48.5 4.0 %shard_map.70 = (bf16[1024,512]{1,0:T(8,128)(2,1)S(1)}, f32[16,4,512]{2,1,0:T(4,128)}) custom-call(s32[1]{0:T(128)} %get-tuple-element.27.core_ref, bf16[1024,512]{1,0:T(8,128)(2,1)S(1)} %copy-done.3, bf16[8,4,32,512]{3,2,1,0:T(8,128)(2,1)S(1)} %all-to-all-done.mine_ref, bf16[8,4,32,512]{3,2,1,0:T(8,128)(2,1)S(1)} %collective-permute-done.other_ref, ...), custom_call_target="tpu_custom_call" | custom-call | flops 2000000000 | bytes 5242880 | tf_op jit(solution)/shard_map/pallas_call | solution.py:218
  52.5 3.7 %all-to-all-start.1 = ((f32[16,4,512]{2,1,0:T(4,128)}), f32[16,4,512]{2,1,0:T(4,128)S(1)}, u32[]{:S(2)}, u32[]{:S(2)}) async-start(f32[16,4,512]{2,1,0:T(4,128)} %get-tuple-element.29), calls=%async_computation.1 | async-start | bytes 262144 | tf_op jit(solution)/shard_map/all_to_all | solution.py:488
  56.2 9.2 %all-to-all-done.1.got_ref = f32[16,4,512]{2,1,0:T(4,128)S(1)} async-done(((f32[16,4,512]{2,1,0:T(4,128)}), f32[16,4,512]{2,1,0:T(4,128)S(1)}, u32[]{:S(2)}, u32[]{:S(2)}) %all-to-all-start.1) | async-done | bytes 131104 | tf_op jit(solution)/shard_map/all_to_all | solution.py:488
  66.2 9.7 %all-to-all-start.2 = ((bf16[32,4,640]{2,1,0:T(4,128)(2,1)}), bf16[32,4,640]{2,1,0:T(4,128)(2,1)S(1)}, u32[]{:S(2)}, u32[]{:S(2)}) async-start(bf16[32,4,640]{2,1,0:T(4,128)(2,1)} %get-tuple-element.30), calls=%async_computation.2 | async-start | bytes 327680 | tf_op jit(solution)/shard_map/all_to_all | solution.py:499
  75.9 5.6 %shard_map.72 = (bf16[2560,256]{1,0:T(8,128)(2,1)S(1)}, bf16[2560,256]{1,0:T(8,128)(2,1)}) custom-call(bf16[1024,1024]{1,0:T(8,128)(2,1)} %get-tuple-element.31.xh_ref, bf16[1024,1024]{1,0:T(8,128)(2,1)} %get-tuple-element.32.xl_ref, f32[4,512]{1,0:T(4,128)S(1)} %get-tuple-element.33.order_hbm.resid_ref), custom_call_target="tpu_custom_call" | custom-call | flops 4000000000 | bytes 8388608 | tf_op jit(solution)/shard_map/pallas_call | solution.py:141
  81.5 4.0 %all-to-all-done.2.got_ref = bf16[32,4,640]{2,1,0:T(4,128)(2,1)S(1)} async-done(((bf16[32,4,640]{2,1,0:T(4,128)(2,1)}), bf16[32,4,640]{2,1,0:T(4,128)(2,1)S(1)}, u32[]{:S(2)}, u32[]{:S(2)}) %all-to-all-start.2) | async-done | bytes 163872 | tf_op jit(solution)/shard_map/all_to_all | solution.py:499
  85.5 1.3 copy-done
  87.8 12.0 %all_to_all.65 = bf16[16,4,512]{2,1,0:T(4,128)(2,1)S(1)} all-to-all(bf16[16,4,512]{2,1,0:T(4,128)(2,1)S(1)} %get-tuple-element.36), channel_id=1, replica_groups=mesh['z'=8,'core'=2,'sketch'=32] {'z','core'}, dimensions={0} | all-to-all | bytes 131072 | tf_op jit(solution)/shard_map/all_to_all | solution.py:494
  100.3 13.0 %all_to_all.66 = bf16[32,2,1024]{2,1,0:T(2,128)(2,1)S(1)} all-to-all(bf16[32,2,1024]{2,1,0:T(2,128)(2,1)S(1)} %reshape.55), channel_id=1, replica_groups=mesh['z'=8,'core'=2,'sketch'=32] {'sketch'}, dimensions={0} | all-to-all | bytes 262144 | tf_op jit(solution)/shard_map/all_to_all | solution.py:506
  113.5 13.4 %all_to_all.67 = bf16[32,2,1024]{2,1,0:T(2,128)(2,1)S(1)} all-to-all(bf16[32,2,1024]{2,1,0:T(2,128)(2,1)S(1)} %broadcast_in_dim.22), channel_id=1, replica_groups=mesh['z'=8,'core'=2,'sketch'=32] {'sketch'}, dimensions={0} | all-to-all | bytes 262144 | tf_op jit(solution)/shard_map/all_to_all | solution.py:491
  127.3 14.2 %all_to_all.68.got_ref = f32[16,4,512]{2,1,0:T(4,128)S(1)} all-to-all(f32[16,4,512]{2,1,0:T(4,128)S(1)} %copy.10), channel_id=1, replica_groups=mesh['z'=8,'core'=2,'sketch'=32] {'z','core'}, dimensions={0} | all-to-all | bytes 262144 | tf_op jit(solution)/shard_map/all_to_all | solution.py:488
  141.7 12.8 %all_to_all.69.got_ref = bf16[32,4,640]{2,1,0:T(4,128)(2,1)S(1)} all-to-all(bf16[32,4,640]{2,1,0:T(4,128)(2,1)S(1)} %get-tuple-element.39), channel_id=1, replica_groups=mesh['z'=8,'core'=2,'sketch'=32] {'sketch'}, dimensions={0} | all-to-all | bytes 327680 | tf_op jit(solution)/shard_map/all_to_all | solution.py:511
  154.5 1.5 shard_map.75
  156.0 12.0 %all_to_all.70.whole_ref = bf16[16,4,512]{2,1,0:T(4,128)(2,1)S(1)} all-to-all(bf16[16,4,512]{2,1,0:T(4,128)(2,1)S(1)} %get-tuple-element.45), channel_id=1, replica_groups=mesh['z'=8,'core'=2,'sketch'=32] {'z','core'}, dimensions={0} | all-to-all | bytes 131072 | tf_op jit(solution)/shard_map/all_to_all | solution.py:494
  168.6 13.1 %all_to_all.71.got_ref = bf16[32,2,1152]{2,1,0:T(2,128)(2,1)S(1)} all-to-all(bf16[32,2,1152]{2,1,0:T(2,128)(2,1)S(1)} %shard_map.76), channel_id=1, replica_groups=mesh['z'=8,'core'=2,'sketch'=32] {'sketch'}, dimensions={0} | all-to-all | bytes 294912 | tf_op jit(solution)/shard_map/all_to_all | solution.py:517
  181.8 13.8 %all_to_all.72 = bf16[32,2,1152]{2,1,0:T(2,128)(2,1)S(1)} all-to-all(bf16[32,2,1152]{2,1,0:T(2,128)(2,1)S(1)} %shard_map.77), channel_id=1, replica_groups=mesh['z'=8,'core'=2,'sketch'=32] {'sketch'}, dimensions={0} | all-to-all | bytes 294912 | tf_op jit(solution)/shard_map/all_to_all | solution.py:519
  196.0 13.3 %all_to_all.73 = bf16[16,4,640]{2,1,0:T(4,128)(2,1)S(1)} all-to-all(bf16[16,4,640]{2,1,0:T(4,128)(2,1)S(1)} %reshape.58), channel_id=1, replica_groups=mesh['z'=8,'core'=2,'sketch'=32] {'z','core'}, dimensions={0} | all-to-all | bytes 163840 | tf_op jit(solution)/shard_map/all_to_all | solution.py:522
  209.8 11.7 %all_to_all.74.got_ref = bf16[16,2,4,512]{3,2,1,0:T(4,128)(2,1)S(1)} all-to-all(bf16[16,2,4,512]{3,2,1,0:T(4,128)(2,1)S(1)} %broadcast_in_dim.25), channel_id=1, replica_groups=mesh['z'=8,'core'=2,'sketch'=32] {'z','core'}, dimensions={0} | all-to-all | bytes 262144 | tf_op jit(solution)/shard_map/all_to_all | solution.py:527
  (39 shorter events, 6.7 us)
Async XLA Ops:
  2.6 40.1 %all-to-all-start = ((bf16[8,4,32,512]{3,2,1,0:T(8,128)(2,1)}), bf16[8,4,32,512]{3,2,1,0:T(8,128)(2,1)S(1)}, u32[]{:S(2)}, u32[]{:S(2)}) async-start(bf16[8,4,32,512]{3,2,1,0:T(8,128)(2,1)} %shard_map.68), calls=%async_computation | async-start | bytes 2097152 | tf_op jit(solution)/shard_map/all_to_all | solution.py:481
  13.5 33.9 %copy-start.4 = (bf16[1024,64]{0,1:T(8,128)(2,1)S(1)}, bf16[1024,64]{0,1:T(8,128)(2,1)}, u32[]{:S(2)}) copy-start(bf16[1024,64]{0,1:T(8,128)(2,1)} %param.7) | copy-start | bytes 393220
  42.7 4.7 %collective-permute-start = (bf16[8,4,32,512]{3,2,1,0:T(8,128)(2,1)S(1)}, bf16[8,4,32,512]{3,2,1,0:T(8,128)(2,1)S(1)}, u32[]{:S(2)}, u32[]{:S(2)}) collective-permute-start(bf16[8,4,32,512]{3,2,1,0:T(8,128)(2,1)S(1)} %all-to-all-done.mine_ref), channel_id=1, source_target_pairs={{0,32},{32,0},{1,33},{33,1},{2,34},{34,2},{3,35},{35,3},{4,36},{36... | collective-permute-start | bytes 3145736 | tf_op jit(solution)/shard_map/ppermute | solution.py:484
  47.3 1.2 copy-start.3
  48.5 16.9 %copy-start.2 = (f32[512]{0:T(512)S(1)}, f32[512]{0:T(512)}, u32[]{:S(2)}) copy-start(f32[512]{0:T(512)} %param.8) | copy-start | bytes 6148
  52.5 12.9 %all-to-all-start.1 = ((f32[16,4,512]{2,1,0:T(4,128)}), f32[16,4,512]{2,1,0:T(4,128)S(1)}, u32[]{:S(2)}, u32[]{:S(2)}) async-start(f32[16,4,512]{2,1,0:T(4,128)} %get-tuple-element.29), calls=%async_computation.1 | async-start | bytes 262144 | tf_op jit(solution)/shard_map/all_to_all | solution.py:488
  66.2 19.3 %all-to-all-start.2 = ((bf16[32,4,640]{2,1,0:T(4,128)(2,1)}), bf16[32,4,640]{2,1,0:T(4,128)(2,1)S(1)}, u32[]{:S(2)}, u32[]{:S(2)}) async-start(bf16[32,4,640]{2,1,0:T(4,128)(2,1)} %get-tuple-element.30), calls=%async_computation.2 | async-start | bytes 327680 | tf_op jit(solution)/shard_map/all_to_all | solution.py:499
  85.5 1.3 copy-start
  126.9 27.6 %copy-start.1 = (bf16[2560,256]{1,0:T(8,128)(2,1)S(1)}, bf16[2560,256]{1,0:T(8,128)(2,1)}, u32[]{:S(2)}) copy-start(bf16[2560,256]{1,0:T(8,128)(2,1)} %get-tuple-element.35.low_ref) | copy-start | bytes 3932164

commit v9 on v8

--- a/solution.py
+++ b/solution.py
@@ -50,7 +50,7 @@
 DP = ("z", "core")
 
 
-def inverse_kernel(core_ref, lower_hbm, high_ref, low_ref, made_ref, lower, inv, sems):
+def inverse_kernel(core_ref, parity_ref, lower_hbm, high_ref, low_ref, made_core_ref, made_parity_ref, lower, inv, sems):
     n = lower.shape[0]
     blocks = n // BLOCK
     spans = [pl.ds(b * BLOCK, BLOCK) for b in range(blocks)]
@@ -64,7 +64,7 @@
     ]
     for copy in copies:
         copy.start()
-    made_ref[0] = core_ref[0]
+    made_core_ref[0], made_parity_ref[0] = core_ref[0], parity_ref[0]
     inv[...] = jnp.zeros_like(inv)
     rows = lax.broadcasted_iota(jnp.int32, (BLOCK, BLOCK), 0)
     cols = lax.broadcasted_iota(jnp.int32, (BLOCK, BLOCK), 1)
@@ -97,14 +97,14 @@
         high_ref[span, :], low_ref[span, :] = split(inv[span, :])
 
 
-def coarse_factor_inverse(core, lower):
+def coarse_factor_inverse(core, parity, lower):
     n = lower.shape[0]
     vmem = pl.BlockSpec(memory_space=pltpu.VMEM)
     return pl.pallas_call(
         inverse_kernel,
-        out_shape=[jax.ShapeDtypeStruct((n, n), bf16)] * 2 + [jax.ShapeDtypeStruct((1,), jnp.int32)],
-        in_specs=[pl.BlockSpec(memory_space=pltpu.SMEM), pl.BlockSpec(memory_space=pl.ANY)],
-        out_specs=[vmem] * 2 + [pl.BlockSpec(memory_space=pltpu.SMEM)],
+        out_shape=[jax.ShapeDtypeStruct((n, n), bf16)] * 2 + [jax.ShapeDtypeStruct((1,), jnp.int32)] * 2,
+        in_specs=[pl.BlockSpec(memory_space=pltpu.SMEM)] * 2 + [pl.BlockSpec(memory_space=pl.ANY)],
+        out_specs=[vmem] * 2 + [pl.BlockSpec(memory_space=pltpu.SMEM)] * 2,
         scratch_shapes=[
             pltpu.VMEM((n, n), bf16),
             pltpu.VMEM((n, n), f32),
@@ -112,7 +112,7 @@
         ],
         compiler_params=pltpu.CompilerParams(vmem_limit_bytes=56 * 1024 * 1024),
         cost_estimate=pl.CostEstimate(flops=10**10, bytes_accessed=6 * 2**20, transcendentals=0),
-    )(core, lower)
+    )(core, parity, lower)
 
 
 def place(a, b):
@@ -473,13 +473,13 @@
     cols = width // n_sk
     factor = 1.0 / math.sqrt(F // K)
     halves = K // count
-    parity = (lax.axis_index("sketch") % halves).astype(jnp.int32).reshape(1)
     n = samples.shape[0]
     scale = feature_scale[None, :]
 
     core = lax.axis_index("core").astype(jnp.int32).reshape(1)
+    parity = (lax.axis_index("sketch") % halves).astype(jnp.int32).reshape(1)
     mine_proj = lax.all_to_all(repeat(projections, lax.axis_size("z")), "z", 0, 0)
-    factor_high, factor_low, core = coarse_factor_inverse(core, coarse_factor)
+    factor_high, factor_low, core, parity = coarse_factor_inverse(core, parity, coarse_factor)
     mine_proj, core = lax.optimization_barrier((mine_proj, core))
     other_proj = lax.ppermute(mine_proj, "core", [(0, 1), (1, 0)])
     feat, part = make_features(core, samples, mine_proj, other_proj, targets.T, n_dp)

time: 223 us -> 223 us (level)
  blocking collectives: 129 us -> 141 us
  waiting for transfers between devices: 29.2 us -> 20 us
  starting transfers between devices: 26.6 us -> 22.9 us
    all_to_all x1 -> x2, blocking collectives: 14.2 us -> 26.2 us  [scatter_dp(): return lax.all_to_all(value, DP, 0, 0)]
    all_to_all x1 -> x0, waiting for transfers between devices: 9.21 us -> none  [scatter_dp(): return lax.all_to_all(value, DP, 0, 0)]
    all_to_all x1 -> x0, starting transfers between devices: 3.68 us -> none  [scatter_dp(): return lax.all_to_all(value, DP, 0, 0)]
  transfers between devices with their start and end apart: 4 -> 3, of which waited for: 4 -> 3; matrix products, arithmetic and copies ran while one was open for 0% -> 0% of each run, Pallas kernels for 9% -> 9%
where the time goes in v9:
time: 223 us; the launch traced here: 222 us
  blocking collectives  141 us (63%)
  Pallas kernels  31.8 us (14%)
  starting transfers between devices  22.9 us (10%)
  waiting for transfers between devices  20 us (9%)
  local copies, waits for them, and re-layouts  3.09 us (1%)
    all_to_all x2, blocking collectives, scatter_dp(): return lax.all_to_all(value, DP, 0, 0)  26.2 us
    all_to_all x2, blocking collectives, forward(): whole = lax.all_to_all(send, DP, 0, 0)  23.9 us
    pallas_call x1, Pallas kernels, coarse_factor_inverse(): pl.pallas_call(inverse_kernel, out_shape=[jax.ShapeDtypeStruct((n, n), bf...  15.5 us
    all_to_all x1, blocking collectives, body(): got = lax.all_to_all(sent, 'sketch', 0, 0).reshape(width, n + SLOTS)  13.8 us
    all_to_all x1, waiting for transfers between devices, body(): lax.all_to_all(repeat(projections, lax.axis_size('z')), 'z', 0, 0)  13.7 us
    all_to_all x1, blocking collectives, gather_sk(): lax.all_to_all(jnp.broadcast_to(value[None], (n_sk,) + value.shape), 'ske...  13.4 us
    all_to_all x1, blocking collectives, body(): lax.all_to_all(sent.reshape(n_dp, mine, count + SLOTS), DP, 0, 0)  13.3 us
    all_to_all x1, blocking collectives, body(): got = lax.all_to_all(run_last_sums(n_sk, whole, sums), 'sketch', 0, 0)  13.1 us
  transfers between devices with their start and end apart: 3, of which 3 were waited for; matrix products, arithmetic and copies ran while one was open for 0% of the time, Pallas kernels for 9%

profile of v9, /device:TPU:1, one launch (start us, length us, event | category | flops | bytes accessed | tf_op | source)
XLA Modules:
  0.0 222.0 jit_solution(6749503699931311389)
XLA Ops:
  0.6 2.0 shard_map.69
  2.6 10.9 %all-to-all-start = ((bf16[8,4,32,512]{3,2,1,0:T(8,128)(2,1)}), bf16[8,4,32,512]{3,2,1,0:T(8,128)(2,1)S(1)}, u32[]{:S(2)}, u32[]{:S(2)}) async-start(bf16[8,4,32,512]{3,2,1,0:T(8,128)(2,1)} %shard_map.69), calls=%async_computation | async-start | bytes 2097152 | tf_op jit(solution)/shard_map/all_to_all | solution.py:481
  13.5 15.5 %shard_map.68 = (bf16[1024,1024]{1,0:T(8,128)(2,1)}, bf16[1024,1024]{1,0:T(8,128)(2,1)}, s32[1]{0:T(128)}, s32[1]{0:T(128)}) custom-call(s32[1]{0:T(128)} %bitcast.core_ref, s32[1]{0:T(128)} %bitcast.1.parity_ref, bf16[1024,1024]{1,0:T(8,128)(2,1)} %lower_hbm.1), custom_call_target="tpu_custom_call" | custom-call | flops 10000000000 | bytes 6291456 | tf_op jit(solution)/shard_map/pallas_call | solution.py:103
  29.0 13.7 %all-to-all-done.mine_ref = bf16[8,4,32,512]{3,2,1,0:T(8,128)(2,1)S(1)} async-done(((bf16[8,4,32,512]{3,2,1,0:T(8,128)(2,1)}), bf16[8,4,32,512]{3,2,1,0:T(8,128)(2,1)S(1)}, u32[]{:S(2)}, u32[]{:S(2)}) %all-to-all-start) | async-done | bytes 1048608 | tf_op jit(solution)/shard_map/all_to_all | solution.py:481
  42.7 2.4 %collective-permute-start = (bf16[8,4,32,512]{3,2,1,0:T(8,128)(2,1)S(1)}, bf16[8,4,32,512]{3,2,1,0:T(8,128)(2,1)S(1)}, u32[]{:S(2)}, u32[]{:S(2)}) collective-permute-start(bf16[8,4,32,512]{3,2,1,0:T(8,128)(2,1)S(1)} %all-to-all-done.mine_ref), channel_id=1, source_target_pairs={{0,32},{32,0},{1,33},{33,1},{2,34},{34,2},{3,35},{35,3},{4,36},{36... | collective-permute-start | bytes 3145736 | tf_op jit(solution)/shard_map/ppermute | solution.py:484
  45.1 2.3 %collective-permute-done.other_ref = bf16[8,4,32,512]{3,2,1,0:T(8,128)(2,1)S(1)} collective-permute-done((bf16[8,4,32,512]{3,2,1,0:T(8,128)(2,1)S(1)}, bf16[8,4,32,512]{3,2,1,0:T(8,128)(2,1)S(1)}, u32[]{:S(2)}, u32[]{:S(2)}) %collective-permute-start) | collective-permute-done | bytes 1048608 | tf_op jit(solution)/shard_map/ppermute | solution.py:484
  48.6 3.2 %shard_map.70 = (bf16[1024,512]{1,0:T(8,128)(2,1)S(1)}, f32[16,4,512]{2,1,0:T(4,128)S(1)}) custom-call(s32[1]{0:T(128)} %get-tuple-element.29.core_ref, bf16[1024,512]{1,0:T(8,128)(2,1)S(1)} %copy-done.3, bf16[8,4,32,512]{3,2,1,0:T(8,128)(2,1)S(1)} %all-to-all-done.mine_ref, bf16[8,4,32,512]{3,2,1,0:T(8,128)(2,1)S(1)} %collective-permute-done.other_ref, ...), custom_call_target="tpu_custom_call" | custom-call | flops 2000000000 | bytes 5242880 | tf_op jit(solution)/shard_map/pallas_call | solution.py:218
  51.8 12.0 %all_to_all.65.got_ref = f32[16,4,512]{2,1,0:T(4,128)S(1)} all-to-all(f32[16,4,512]{2,1,0:T(4,128)S(1)} %get-tuple-element.31), channel_id=1, replica_groups=mesh['z'=8,'core'=2,'sketch'=32] {'z','core'}, dimensions={0} | all-to-all | bytes 262144 | tf_op jit(solution)/shard_map/all_to_all | solution.py:488
  64.6 9.7 %all-to-all-start.2 = ((bf16[32,4,640]{2,1,0:T(4,128)(2,1)}), bf16[32,4,640]{2,1,0:T(4,128)(2,1)S(1)}, u32[]{:S(2)}, u32[]{:S(2)}) async-start(bf16[32,4,640]{2,1,0:T(4,128)(2,1)} %get-tuple-element.32), calls=%async_computation.2 | async-start | bytes 327680 | tf_op jit(solution)/shard_map/all_to_all | solution.py:499
  74.2 5.6 %shard_map.72 = (bf16[2560,256]{1,0:T(8,128)(2,1)S(1)}, bf16[2560,256]{1,0:T(8,128)(2,1)}) custom-call(bf16[1024,1024]{1,0:T(8,128)(2,1)} %get-tuple-element.33.xh_ref, bf16[1024,1024]{1,0:T(8,128)(2,1)} %get-tuple-element.34.xl_ref, f32[4,512]{1,0:T(4,128)S(1)} %get-tuple-element.35.order_hbm.resid_ref), custom_call_target="tpu_custom_call" | custom-call | flops 4000000000 | bytes 8388608 | tf_op jit(solution)/shard_map/pallas_call | solution.py:141
  79.8 4.1 %all-to-all-done.2.got_ref = bf16[32,4,640]{2,1,0:T(4,128)(2,1)S(1)} async-done(((bf16[32,4,640]{2,1,0:T(4,128)(2,1)}), bf16[32,4,640]{2,1,0:T(4,128)(2,1)S(1)}, u32[]{:S(2)}, u32[]{:S(2)}) %all-to-all-start.2) | async-done | bytes 163872 | tf_op jit(solution)/shard_map/all_to_all | solution.py:499
  83.8 1.3 copy-done
  85.2 1.6 shard_map.73
  86.7 12.0 %all_to_all.66 = bf16[16,4,512]{2,1,0:T(4,128)(2,1)S(1)} all-to-all(bf16[16,4,512]{2,1,0:T(4,128)(2,1)S(1)} %get-tuple-element.38), channel_id=1, replica_groups=mesh['z'=8,'core'=2,'sketch'=32] {'z','core'}, dimensions={0} | all-to-all | bytes 131072 | tf_op jit(solution)/shard_map/all_to_all | solution.py:494
  99.2 13.0 %all_to_all.67 = bf16[32,2,1024]{2,1,0:T(2,128)(2,1)S(1)} all-to-all(bf16[32,2,1024]{2,1,0:T(2,128)(2,1)S(1)} %reshape.55), channel_id=1, replica_groups=mesh['z'=8,'core'=2,'sketch'=32] {'sketch'}, dimensions={0} | all-to-all | bytes 262144 | tf_op jit(solution)/shard_map/all_to_all | solution.py:506
  112.5 13.4 %all_to_all.68 = bf16[32,2,1024]{2,1,0:T(2,128)(2,1)S(1)} all-to-all(bf16[32,2,1024]{2,1,0:T(2,128)(2,1)S(1)} %broadcast_in_dim.22), channel_id=1, replica_groups=mesh['z'=8,'core'=2,'sketch'=32] {'sketch'}, dimensions={0} | all-to-all | bytes 262144 | tf_op jit(solution)/shard_map/all_to_all | solution.py:491
  126.3 14.3 %all_to_all.69.got_ref = f32[16,4,512]{2,1,0:T(4,128)S(1)} all-to-all(f32[16,4,512]{2,1,0:T(4,128)S(1)} %copy.10), channel_id=1, replica_groups=mesh['z'=8,'core'=2,'sketch'=32] {'z','core'}, dimensions={0} | all-to-all | bytes 262144 | tf_op jit(solution)/shard_map/all_to_all | solution.py:488
  140.7 12.8 %all_to_all.70.got_ref = bf16[32,4,640]{2,1,0:T(4,128)(2,1)S(1)} all-to-all(bf16[32,4,640]{2,1,0:T(4,128)(2,1)S(1)} %get-tuple-element.41), channel_id=1, replica_groups=mesh['z'=8,'core'=2,'sketch'=32] {'sketch'}, dimensions={0} | all-to-all | bytes 327680 | tf_op jit(solution)/shard_map/all_to_all | solution.py:511
  153.5 2.1 shard_map.75
  155.6 12.0 %all_to_all.71.whole_ref = bf16[16,4,512]{2,1,0:T(4,128)(2,1)S(1)} all-to-all(bf16[16,4,512]{2,1,0:T(4,128)(2,1)S(1)} %get-tuple-element.47), channel_id=1, replica_groups=mesh['z'=8,'core'=2,'sketch'=32] {'z','core'}, dimensions={0} | all-to-all | bytes 131072 | tf_op jit(solution)/shard_map/all_to_all | solution.py:494
  168.1 13.1 %all_to_all.72.got_ref = bf16[32,2,1152]{2,1,0:T(2,128)(2,1)S(1)} all-to-all(bf16[32,2,1152]{2,1,0:T(2,128)(2,1)S(1)} %shard_map.76), channel_id=1, replica_groups=mesh['z'=8,'core'=2,'sketch'=32] {'sketch'}, dimensions={0} | all-to-all | bytes 294912 | tf_op jit(solution)/shard_map/all_to_all | solution.py:517
  181.4 13.8 %all_to_all.73 = bf16[32,2,1152]{2,1,0:T(2,128)(2,1)S(1)} all-to-all(bf16[32,2,1152]{2,1,0:T(2,128)(2,1)S(1)} %shard_map.77), channel_id=1, replica_groups=mesh['z'=8,'core'=2,'sketch'=32] {'sketch'}, dimensions={0} | all-to-all | bytes 294912 | tf_op jit(solution)/shard_map/all_to_all | solution.py:519
  195.6 13.3 %all_to_all.74 = bf16[16,4,640]{2,1,0:T(4,128)(2,1)S(1)} all-to-all(bf16[16,4,640]{2,1,0:T(4,128)(2,1)S(1)} %reshape.58), channel_id=1, replica_groups=mesh['z'=8,'core'=2,'sketch'=32] {'z','core'}, dimensions={0} | all-to-all | bytes 163840 | tf_op jit(solution)/shard_map/all_to_all | solution.py:522
  209.4 11.7 %all_to_all.75.got_ref = bf16[16,2,4,512]{3,2,1,0:T(4,128)(2,1)S(1)} all-to-all(bf16[16,2,4,512]{3,2,1,0:T(4,128)(2,1)S(1)} %broadcast_in_dim.25), channel_id=1, replica_groups=mesh['z'=8,'core'=2,'sketch'=32] {'z','core'}, dimensions={0} | all-to-all | bytes 262144 | tf_op jit(solution)/shard_map/all_to_all | solution.py:527
  (38 shorter events, 5.7 us)
Async XLA Ops:
  2.6 40.1 %all-to-all-start = ((bf16[8,4,32,512]{3,2,1,0:T(8,128)(2,1)}), bf16[8,4,32,512]{3,2,1,0:T(8,128)(2,1)S(1)}, u32[]{:S(2)}, u32[]{:S(2)}) async-start(bf16[8,4,32,512]{3,2,1,0:T(8,128)(2,1)} %shard_map.69), calls=%async_computation | async-start | bytes 2097152 | tf_op jit(solution)/shard_map/all_to_all | solution.py:481
  13.5 33.9 %copy-start.4 = (bf16[1024,64]{0,1:T(8,128)(2,1)S(1)}, bf16[1024,64]{0,1:T(8,128)(2,1)}, u32[]{:S(2)}) copy-start(bf16[1024,64]{0,1:T(8,128)(2,1)} %param.7) | copy-start | bytes 393220
  42.7 4.7 %collective-permute-start = (bf16[8,4,32,512]{3,2,1,0:T(8,128)(2,1)S(1)}, bf16[8,4,32,512]{3,2,1,0:T(8,128)(2,1)S(1)}, u32[]{:S(2)}, u32[]{:S(2)}) collective-permute-start(bf16[8,4,32,512]{3,2,1,0:T(8,128)(2,1)S(1)} %all-to-all-done.mine_ref), channel_id=1, source_target_pairs={{0,32},{32,0},{1,33},{33,1},{2,34},{34,2},{3,35},{35,3},{4,36},{36... | collective-permute-start | bytes 3145736 | tf_op jit(solution)/shard_map/ppermute | solution.py:484
  47.3 1.2 copy-start.3
  48.5 15.2 %copy-start.2 = (f32[512]{0:T(512)S(1)}, f32[512]{0:T(512)}, u32[]{:S(2)}) copy-start(f32[512]{0:T(512)} %param.8) | copy-start | bytes 6148
  64.6 19.3 %all-to-all-start.2 = ((bf16[32,4,640]{2,1,0:T(4,128)(2,1)}), bf16[32,4,640]{2,1,0:T(4,128)(2,1)S(1)}, u32[]{:S(2)}, u32[]{:S(2)}) async-start(bf16[32,4,640]{2,1,0:T(4,128)(2,1)} %get-tuple-element.32), calls=%async_computation.2 | async-start | bytes 327680 | tf_op jit(solution)/shard_map/all_to_all | solution.py:499
  83.8 1.3 copy-start
  125.9 27.6 %copy-start.1 = (bf16[2560,256]{1,0:T(8,128)(2,1)S(1)}, bf16[2560,256]{1,0:T(8,128)(2,1)}, u32[]{:S(2)}) copy-start(bf16[2560,256]{1,0:T(8,128)(2,1)} %get-tuple-element.37.low_ref) | copy-start | bytes 3932164

commit v10 on v9

--- a/solution.py
+++ b/solution.py
@@ -292,6 +292,29 @@
         ],
         in_specs=[vmem] * (1 + len(operands)),
         out_specs=[vmem] * 2,
+        compiler_params=pltpu.CompilerParams(vmem_limit_bytes=8 * 1024 * 1024),
+    )(got, *operands)
+
+
+def last_step_kernel(got_ref, direction_ref, dots_ref, answer_ref, resid_ref, send_ref):
+    count = direction_ref.shape[1]
+    total, direction = summed(got_ref), direction_ref[...]
+    image = total[:, :count] + RIDGE * direction
+    alpha = lane(dots_ref[...], 1) / row_sum(total[:, count:])
+    answer = (answer_ref[...] + alpha * direction).astype(bf16)
+    resid = (resid_ref[...] - alpha * image).astype(bf16)
+    for p in range(send_ref.shape[0]):
+        send_ref[p, 0] = answer
+        send_ref[p, 1] = resid
+
+
+def run_last_step(got, *operands):
+    vmem = pl.BlockSpec(memory_space=pltpu.VMEM)
+    return pl.pallas_call(
+        last_step_kernel,
+        out_shape=jax.ShapeDtypeStruct((got.shape[0], 2) + operands[0].shape, bf16),
+        in_specs=[vmem] * (1 + len(operands)),
+        out_specs=vmem,
         compiler_params=pltpu.CompilerParams(vmem_limit_bytes=8 * 1024 * 1024),
     )(got, *operands)
 
@@ -519,12 +542,8 @@
     got = lax.all_to_all(sent, "sketch", 0, 0).reshape(width, n + SLOTS)
     image = dot(got[:, :n], feat)
     sent = jnp.concatenate([image.astype(bf16), got[:, n:]], 1)
-    got = lax.all_to_all(sent.reshape(n_dp, mine, count + SLOTS), DP, 0, 0).astype(f32)
-    total = jnp.sum(got, 0)
-    image = total[:, :count] + RIDGE * direction
-    alpha = dots[:, 1:2] / row_sum(total[:, count:])
-    out = jnp.stack([answer + alpha * direction, resid - alpha * image]).astype(bf16)
-    got = lax.all_to_all(jnp.broadcast_to(out[None], (n_dp,) + out.shape), DP, 0, 0)
+    got = lax.all_to_all(sent.reshape(n_dp, mine, count + SLOTS), DP, 0, 0)
+    got = lax.all_to_all(run_last_step(got, direction, dots, answer, resid), DP, 0, 0)
     answer, resid = outputs(got)
     return answer.T, resid.T
 

time: 223 us -> 222 us (level)
  transfers between devices with their start and end apart: 3 -> 3, of which waited for: 3 -> 3; matrix products, arithmetic and copies ran while one was open for 0% -> 0% of each run, Pallas kernels for 9% -> 10%
where the time goes in v10:
time: 222 us; the launch traced here: 221 us
  blocking collectives  141 us (64%)
  Pallas kernels  31.9 us (14%)
  starting transfers between devices  22.9 us (10%)
  waiting for transfers between devices  19.9 us (9%)
  local copies, waits for them, and re-layouts  2.95 us (1%)
    all_to_all x2, blocking collectives, scatter_dp(): return lax.all_to_all(value, DP, 0, 0)  26.2 us
    all_to_all x2, blocking collectives, forward(): whole = lax.all_to_all(send, DP, 0, 0)  23.9 us
    pallas_call x1, Pallas kernels, coarse_factor_inverse(): pl.pallas_call(inverse_kernel, out_shape=[jax.ShapeDtypeStruct((n, n), bf...  15.5 us
    all_to_all x1, blocking collectives, body(): got = lax.all_to_all(sent, 'sketch', 0, 0).reshape(width, n + SLOTS)  13.8 us
    all_to_all x1, waiting for transfers between devices, body(): lax.all_to_all(repeat(projections, lax.axis_size('z')), 'z', 0, 0)  13.7 us
    all_to_all x1, blocking collectives, gather_sk(): lax.all_to_all(jnp.broadcast_to(value[None], (n_sk,) + value.shape), 'ske...  13.4 us
    all_to_all x1, blocking collectives, body(): got = lax.all_to_all(sent.reshape(n_dp, mine, count + SLOTS), DP, 0, 0)  13.3 us
    all_to_all x1, blocking collectives, body(): got = lax.all_to_all(run_last_sums(n_sk, whole, sums), 'sketch', 0, 0)  13.1 us
  transfers between devices with their start and end apart: 3, of which 3 were waited for; matrix products, arithmetic and copies ran while one was open for 0% of the time, Pallas kernels for 10%

profile of v10, /device:TPU:1, one launch (start us, length us, event | category | flops | bytes accessed | tf_op | source)
XLA Modules:
  0.0 221.4 jit_solution(10378986146965917777)
XLA Ops:
  0.6 2.0 shard_map.69
  2.6 10.9 %all-to-all-start = ((bf16[8,4,32,512]{3,2,1,0:T(8,128)(2,1)}), bf16[8,4,32,512]{3,2,1,0:T(8,128)(2,1)S(1)}, u32[]{:S(2)}, u32[]{:S(2)}) async-start(bf16[8,4,32,512]{3,2,1,0:T(8,128)(2,1)} %shard_map.69), calls=%async_computation | async-start | bytes 2097152 | tf_op jit(solution)/shard_map/all_to_all | solution.py:504
  13.5 15.5 %shard_map.68 = (bf16[1024,1024]{1,0:T(8,128)(2,1)}, bf16[1024,1024]{1,0:T(8,128)(2,1)}, s32[1]{0:T(128)}, s32[1]{0:T(128)}) custom-call(s32[1]{0:T(128)} %bitcast.core_ref, s32[1]{0:T(128)} %bitcast.1.parity_ref, bf16[1024,1024]{1,0:T(8,128)(2,1)} %lower_hbm.1), custom_call_target="tpu_custom_call" | custom-call | flops 10000000000 | bytes 6291456 | tf_op jit(solution)/shard_map/pallas_call | solution.py:103
  29.0 13.7 %all-to-all-done.mine_ref = bf16[8,4,32,512]{3,2,1,0:T(8,128)(2,1)S(1)} async-done(((bf16[8,4,32,512]{3,2,1,0:T(8,128)(2,1)}), bf16[8,4,32,512]{3,2,1,0:T(8,128)(2,1)S(1)}, u32[]{:S(2)}, u32[]{:S(2)}) %all-to-all-start) | async-done | bytes 1048608 | tf_op jit(solution)/shard_map/all_to_all | solution.py:504
  42.7 2.4 %collective-permute-start = (bf16[8,4,32,512]{3,2,1,0:T(8,128)(2,1)S(1)}, bf16[8,4,32,512]{3,2,1,0:T(8,128)(2,1)S(1)}, u32[]{:S(2)}, u32[]{:S(2)}) collective-permute-start(bf16[8,4,32,512]{3,2,1,0:T(8,128)(2,1)S(1)} %all-to-all-done.mine_ref), channel_id=1, source_target_pairs={{0,32},{32,0},{1,33},{33,1},{2,34},{34,2},{3,35},{35,3},{4,36},{36... | collective-permute-start | bytes 3145736 | tf_op jit(solution)/shard_map/ppermute | solution.py:507
  45.1 2.3 %collective-permute-done.other_ref = bf16[8,4,32,512]{3,2,1,0:T(8,128)(2,1)S(1)} collective-permute-done((bf16[8,4,32,512]{3,2,1,0:T(8,128)(2,1)S(1)}, bf16[8,4,32,512]{3,2,1,0:T(8,128)(2,1)S(1)}, u32[]{:S(2)}, u32[]{:S(2)}) %collective-permute-start) | collective-permute-done | bytes 1048608 | tf_op jit(solution)/shard_map/ppermute | solution.py:507
  48.6 3.2 %shard_map.70 = (bf16[1024,512]{1,0:T(8,128)(2,1)S(1)}, f32[16,4,512]{2,1,0:T(4,128)S(1)}) custom-call(s32[1]{0:T(128)} %get-tuple-element.29.core_ref, bf16[1024,512]{1,0:T(8,128)(2,1)S(1)} %copy-done.3, bf16[8,4,32,512]{3,2,1,0:T(8,128)(2,1)S(1)} %all-to-all-done.mine_ref, bf16[8,4,32,512]{3,2,1,0:T(8,128)(2,1)S(1)} %collective-permute-done.other_ref, ...), custom_call_target="tpu_custom_call" | custom-call | flops 2000000000 | bytes 5242880 | tf_op jit(solution)/shard_map/pallas_call | solution.py:218
  51.7 12.0 %all_to_all.65.got_ref = f32[16,4,512]{2,1,0:T(4,128)S(1)} all-to-all(f32[16,4,512]{2,1,0:T(4,128)S(1)} %get-tuple-element.31), channel_id=1, replica_groups=mesh['z'=8,'core'=2,'sketch'=32] {'z','core'}, dimensions={0} | all-to-all | bytes 262144 | tf_op jit(solution)/shard_map/all_to_all | solution.py:511
  64.5 9.7 %all-to-all-start.2 = ((bf16[32,4,640]{2,1,0:T(4,128)(2,1)}), bf16[32,4,640]{2,1,0:T(4,128)(2,1)S(1)}, u32[]{:S(2)}, u32[]{:S(2)}) async-start(bf16[32,4,640]{2,1,0:T(4,128)(2,1)} %get-tuple-element.32), calls=%async_computation.2 | async-start | bytes 327680 | tf_op jit(solution)/shard_map/all_to_all | solution.py:522
  74.2 5.6 %shard_map.72 = (bf16[2560,256]{1,0:T(8,128)(2,1)S(1)}, bf16[2560,256]{1,0:T(8,128)(2,1)}) custom-call(bf16[1024,1024]{1,0:T(8,128)(2,1)} %get-tuple-element.33.xh_ref, bf16[1024,1024]{1,0:T(8,128)(2,1)} %get-tuple-element.34.xl_ref, f32[4,512]{1,0:T(4,128)S(1)} %get-tuple-element.35.order_hbm.resid_ref), custom_call_target="tpu_custom_call" | custom-call | flops 4000000000 | bytes 8388608 | tf_op jit(solution)/shard_map/pallas_call | solution.py:141
  79.8 4.0 %all-to-all-done.2.got_ref = bf16[32,4,640]{2,1,0:T(4,128)(2,1)S(1)} async-done(((bf16[32,4,640]{2,1,0:T(4,128)(2,1)}), bf16[32,4,640]{2,1,0:T(4,128)(2,1)S(1)}, u32[]{:S(2)}, u32[]{:S(2)}) %all-to-all-start.2) | async-done | bytes 163872 | tf_op jit(solution)/shard_map/all_to_all | solution.py:522
  83.8 1.3 copy-done
  85.1 1.5 shard_map.73
  86.7 12.0 %all_to_all.66 = bf16[16,4,512]{2,1,0:T(4,128)(2,1)S(1)} all-to-all(bf16[16,4,512]{2,1,0:T(4,128)(2,1)S(1)} %get-tuple-element.38), channel_id=1, replica_groups=mesh['z'=8,'core'=2,'sketch'=32] {'z','core'}, dimensions={0} | all-to-all | bytes 131072 | tf_op jit(solution)/shard_map/all_to_all | solution.py:517
  99.2 13.0 %all_to_all.67 = bf16[32,2,1024]{2,1,0:T(2,128)(2,1)S(1)} all-to-all(bf16[32,2,1024]{2,1,0:T(2,128)(2,1)S(1)} %reshape.36), channel_id=1, replica_groups=mesh['z'=8,'core'=2,'sketch'=32] {'sketch'}, dimensions={0} | all-to-all | bytes 262144 | tf_op jit(solution)/shard_map/all_to_all | solution.py:529
  112.4 13.4 %all_to_all.68 = bf16[32,2,1024]{2,1,0:T(2,128)(2,1)S(1)} all-to-all(bf16[32,2,1024]{2,1,0:T(2,128)(2,1)S(1)} %broadcast_in_dim.13), channel_id=1, replica_groups=mesh['z'=8,'core'=2,'sketch'=32] {'sketch'}, dimensions={0} | all-to-all | bytes 262144 | tf_op jit(solution)/shard_map/all_to_all | solution.py:514
  126.2 14.2 %all_to_all.69.got_ref = f32[16,4,512]{2,1,0:T(4,128)S(1)} all-to-all(f32[16,4,512]{2,1,0:T(4,128)S(1)} %copy.9), channel_id=1, replica_groups=mesh['z'=8,'core'=2,'sketch'=32] {'z','core'}, dimensions={0} | all-to-all | bytes 262144 | tf_op jit(solution)/shard_map/all_to_all | solution.py:511
  140.6 12.8 %all_to_all.70.got_ref = bf16[32,4,640]{2,1,0:T(4,128)(2,1)S(1)} all-to-all(bf16[32,4,640]{2,1,0:T(4,128)(2,1)S(1)} %get-tuple-element.41), channel_id=1, replica_groups=mesh['z'=8,'core'=2,'sketch'=32] {'sketch'}, dimensions={0} | all-to-all | bytes 327680 | tf_op jit(solution)/shard_map/all_to_all | solution.py:534
  153.4 2.0 shard_map.75
  155.5 12.0 %all_to_all.71.whole_ref = bf16[16,4,512]{2,1,0:T(4,128)(2,1)S(1)} all-to-all(bf16[16,4,512]{2,1,0:T(4,128)(2,1)S(1)} %get-tuple-element.45), channel_id=1, replica_groups=mesh['z'=8,'core'=2,'sketch'=32] {'z','core'}, dimensions={0} | all-to-all | bytes 131072 | tf_op jit(solution)/shard_map/all_to_all | solution.py:517
  168.0 13.1 %all_to_all.72.got_ref = bf16[32,2,1152]{2,1,0:T(2,128)(2,1)S(1)} all-to-all(bf16[32,2,1152]{2,1,0:T(2,128)(2,1)S(1)} %shard_map.76), channel_id=1, replica_groups=mesh['z'=8,'core'=2,'sketch'=32] {'sketch'}, dimensions={0} | all-to-all | bytes 294912 | tf_op jit(solution)/shard_map/all_to_all | solution.py:540
  181.3 13.8 %all_to_all.73 = bf16[32,2,1152]{2,1,0:T(2,128)(2,1)S(1)} all-to-all(bf16[32,2,1152]{2,1,0:T(2,128)(2,1)S(1)} %shard_map.77), channel_id=1, replica_groups=mesh['z'=8,'core'=2,'sketch'=32] {'sketch'}, dimensions={0} | all-to-all | bytes 294912 | tf_op jit(solution)/shard_map/all_to_all | solution.py:542
  195.4 13.3 %all_to_all.74.got_ref = bf16[16,4,640]{2,1,0:T(4,128)(2,1)S(1)} all-to-all(bf16[16,4,640]{2,1,0:T(4,128)(2,1)S(1)} %reshape.39), channel_id=1, replica_groups=mesh['z'=8,'core'=2,'sketch'=32] {'z','core'}, dimensions={0} | all-to-all | bytes 163840 | tf_op jit(solution)/shard_map/all_to_all | solution.py:545
  208.8 11.7 %all_to_all.75.got_ref = bf16[16,2,4,512]{3,2,1,0:T(4,128)(2,1)S(1)} all-to-all(bf16[16,2,4,512]{3,2,1,0:T(4,128)(2,1)S(1)} %shard_map.78), channel_id=1, replica_groups=mesh['z'=8,'core'=2,'sketch'=32] {'z','core'}, dimensions={0} | all-to-all | bytes 262144 | tf_op jit(solution)/shard_map/all_to_all | solution.py:546
  (32 shorter events, 5.3 us)
Async XLA Ops:
  2.6 40.1 %all-to-all-start = ((bf16[8,4,32,512]{3,2,1,0:T(8,128)(2,1)}), bf16[8,4,32,512]{3,2,1,0:T(8,128)(2,1)S(1)}, u32[]{:S(2)}, u32[]{:S(2)}) async-start(bf16[8,4,32,512]{3,2,1,0:T(8,128)(2,1)} %shard_map.69), calls=%async_computation | async-start | bytes 2097152 | tf_op jit(solution)/shard_map/all_to_all | solution.py:504
  13.5 33.9 %copy-start.4 = (bf16[1024,64]{0,1:T(8,128)(2,1)S(1)}, bf16[1024,64]{0,1:T(8,128)(2,1)}, u32[]{:S(2)}) copy-start(bf16[1024,64]{0,1:T(8,128)(2,1)} %param.7) | copy-start | bytes 393220
  42.7 4.7 %collective-permute-start = (bf16[8,4,32,512]{3,2,1,0:T(8,128)(2,1)S(1)}, bf16[8,4,32,512]{3,2,1,0:T(8,128)(2,1)S(1)}, u32[]{:S(2)}, u32[]{:S(2)}) collective-permute-start(bf16[8,4,32,512]{3,2,1,0:T(8,128)(2,1)S(1)} %all-to-all-done.mine_ref), channel_id=1, source_target_pairs={{0,32},{32,0},{1,33},{33,1},{2,34},{34,2},{3,35},{35,3},{4,36},{36... | collective-permute-start | bytes 3145736 | tf_op jit(solution)/shard_map/ppermute | solution.py:507
  47.3 1.2 copy-start.3
  48.6 15.2 %copy-start.2 = (f32[512]{0:T(512)S(1)}, f32[512]{0:T(512)}, u32[]{:S(2)}) copy-start(f32[512]{0:T(512)} %param.8) | copy-start | bytes 6148
  64.5 19.3 %all-to-all-start.2 = ((bf16[32,4,640]{2,1,0:T(4,128)(2,1)}), bf16[32,4,640]{2,1,0:T(4,128)(2,1)S(1)}, u32[]{:S(2)}, u32[]{:S(2)}) async-start(bf16[32,4,640]{2,1,0:T(4,128)(2,1)} %get-tuple-element.32), calls=%async_computation.2 | async-start | bytes 327680 | tf_op jit(solution)/shard_map/all_to_all | solution.py:522
  83.8 1.3 copy-start
  125.8 27.6 %copy-start.1 = (bf16[2560,256]{1,0:T(8,128)(2,1)S(1)}, bf16[2560,256]{1,0:T(8,128)(2,1)}, u32[]{:S(2)}) copy-start(bf16[2560,256]{1,0:T(8,128)(2,1)} %get-tuple-element.37.low_ref) | copy-start | bytes 3932164
